TPU v7x, 32 devices: a whole 2x2x4 slice. The times are simulated.
32 devices in a mesh: rows: 8 (over y, x, core), cols: 4 (over z).
Axes of the slice: x: 2, y: 2, z: 4, core: 2. Of those that a mesh axis runs over, the one named last changes fastest.
Arguments:
- tokens: bfloat16 [104, 2048], P(None, 'rows'), may hold values from -24 to 24
- arrival: int32 [104], replicated, may hold values from 0 to 103, each once
- cache_lengths: int32 [104], replicated, may hold values from 1 to 1023, as said below
- move_slot: int32 [8, 4], replicated, may hold values from 0 to 12, as said below
- move_target: int32 [8, 4], replicated, may hold values from 0 to 7, as said below
- page_table: int32 [8, 4, 13, 8], P('rows', 'cols'), may hold values from 0 to 103, as said below
- kv_pool: bfloat16 [832, 4, 32, 512], P('rows', 'cols'), may hold values from -400 to 400
- ssm_state: bfloat16 [104, 32, 64, 256], P('rows', 'cols'), may hold values from -1.5 to 1.5
- conv_x: bfloat16 [104, 3, 2048], P('rows', None, 'cols'), may hold values from -6 to 6
- conv_bc: bfloat16 [104, 3, 512], P('rows'), may hold values from -6 to 6
- norm_gain: bfloat16 [2048], P('rows'), may hold values from 0.099609375 to 1.8984375
- weight_z: bfloat16 [2048, 2048], P('rows', 'cols'), may hold values from -0.125 to 0.125
- weight_x: bfloat16 [2048, 2048], P('rows', 'cols'), may hold values from -0.125 to 0.125
- weight_dt: bfloat16 [2048, 32], P('rows', 'cols'), may hold values from -0.125 to 0.125
- weight_bc: bfloat16 [2048, 512], P('rows'), may hold values from -0.125 to 0.125
- weight_qkv: bfloat16 [2048, 1536], P('rows'), may hold values from -0.125 to 0.125
- conv_weight_x: bfloat16 [4, 2048], P(None, 'cols'), may hold values from -3 to 3
- conv_weight_bc: bfloat16 [4, 512], replicated, may hold values from -3 to 3
- dt_bias: float32 [32], P('cols'), may hold values from -4 to -1
- a_log: float32 [32], P('cols'), may hold values from 0 to 2.5
- d_skip: float32 [32], P('cols'), may hold values from 0.5 to 1.5
- weight_ssm_out: bfloat16 [2048, 2048], P('cols'), may hold values from -0.125 to 0.125
- weight_attn_out: bfloat16 [1024, 2048], P('cols'), may hold values from -0.1875 to 0.1875
Outputs:
- mixed: bfloat16 [104, 2048], P('rows', 'cols')
- ssm_next: bfloat16 [104, 32, 64, 256], P('rows', 'cols')
- conv_x_next: bfloat16 [104, 3, 2048], P('rows', None, 'cols')
- conv_bc_next: bfloat16 [104, 3, 512], P('rows')
- kv_next: bfloat16 [832, 4, 32, 512], P('rows', 'cols')
Inputs may be any that keep to these rules, and one draw needn't show every extreme that they name: `cache_lengths`: some request has 1023 cached tokens. `move_slot`: each row lists 4 distinct slots. `move_target`: each row lists 4 distinct row indices other than its own; every row index is named exactly 4 times, by distinct sources. `page_table`: the 13 x 8 entries of one device are each of 0 to 103 once.
All inputs are finite; a program needn't handle non-finite values.
Results may differ from a plain program's by a relative error of at most 0.011.
Values may be sent and summed in bfloat16 or wider, within the bound.
No kernel may reach another device: no remote copies, remote signals or barrier semaphores. Data moves between devices by JAX's collectives and lax.ppermute only.
A program may use at most 64 MiB of HBM per device.

v0:
```python
import jax
import jax.numpy as jnp
from jax import lax
from jax.sharding import PartitionSpec as P

D = 2048
HP = 64
NS = 256
QH = 8
KVH = 2
HD = 128
PAGE = 32


EPSILON = 1e-05
FLOOR_SCORE = -1e30
PRECISE = lax.Precision.HIGHEST


def merged(value, axis, combine):
    everything = jax.tree.map(lambda part: lax.all_gather(part, axis), value)
    initial = jax.tree.map(lambda part: part[0], everything)

    def step(k, so_far):
        return combine(so_far, jax.tree.map(lambda part: part[k], everything))

    return lax.fori_loop(1, lax.axis_size(axis), step, initial)


def residents(move_slot, move_target, row_count, slot_count):
    move_count = move_slot.shape[1]
    devices = jnp.arange(row_count, dtype=jnp.int32)
    matches = move_target[:, None, :] == devices[None, :, None]
    sending = jnp.any(matches, axis=2)
    slot_from = jnp.sum(jnp.where(matches, move_slot[:, None, :], 0), axis=2)
    ranking = jnp.cumsum(sending.astype(jnp.int32), axis=0) - 1
    leaving = devices[:, None] * slot_count + slot_from
    turn_order = jnp.arange(move_count, dtype=jnp.int32)
    chosen = sending[:, :, None] & (ranking[:, :, None] == turn_order[None, None, :])
    incoming = jnp.sum(jnp.where(chosen, leaving[:, :, None], 0), axis=0)
    places = jnp.arange(slot_count, dtype=jnp.int32)
    vacant = move_slot[:, :, None] == places[None, None, :]
    filled = jnp.sum(jnp.where(vacant, incoming[:, :, None], 0), axis=1)
    staying = devices[:, None] * slot_count + places[None, :]
    return jnp.where(jnp.any(vacant, axis=1), filled, staying)


def outgoing_slots(move_slot, move_target, row_index, row_count):
    targets_here = lax.dynamic_index_in_dim(move_target, row_index, 0, keepdims=False)
    slots_here = lax.dynamic_index_in_dim(move_slot, row_index, 0, keepdims=False)
    peer_index = jnp.arange(row_count, dtype=jnp.int32)
    matches = targets_here[None, :] == peer_index[:, None]
    return jnp.sum(jnp.where(matches, slots_here[None, :], 0), axis=1)


def arrival_index(layout, row_index, slot_count):
    resident = lax.dynamic_index_in_dim(layout, row_index, 0, keepdims=False)
    anchor = resident // slot_count
    return jnp.where(
        anchor == row_index, jnp.arange(slot_count, dtype=jnp.int32), slot_count + anchor
    )


def migrate(members, sending, placing):
    state_part, conv_x_part, conv_bc_part, pages_part = members
    arrived = (
        lax.all_to_all(
            jnp.take(state_part, sending, axis=0), "rows", split_axis=0, concat_axis=0, tiled=True
        ),
        lax.all_to_all(
            jnp.take(conv_x_part, sending, axis=0), "rows", split_axis=0, concat_axis=0, tiled=True
        ),
        lax.all_to_all(
            jnp.take(conv_bc_part, sending, axis=0), "rows", split_axis=0, concat_axis=0, tiled=True
        ),
        lax.all_to_all(
            jnp.take(pages_part, sending, axis=0), "rows", split_axis=0, concat_axis=0, tiled=True
        ),
    )
    return tuple(
        (
            jnp.take(jnp.concatenate([resident_part, arrived_part], axis=0), placing, axis=0)
            for resident_part, arrived_part in zip(members, arrived)
        )
    )


def combine(first_part, second_part):
    joint_peak = jnp.maximum(first_part[0], second_part[0])
    first_scale = jnp.exp(first_part[0] - joint_peak)
    second_scale = jnp.exp(second_part[0] - joint_peak)
    joint_total = first_part[1] * first_scale + second_part[1] * second_scale
    joint_sum = first_part[2] * first_scale[..., None] + second_part[2] * second_scale[..., None]
    return (joint_peak, joint_total, joint_sum)


def serve_rows(
    projected,
    state_part,
    conv_x_part,
    conv_bc_part,
    pages_part,
    lengths_here,
    conv_weight_x,
    conv_weight_bc,
    dt_bias,
    a_log,
    d_skip,
    col_index,
    col_count,
):
    slot_count = projected.shape[0]
    head_count = dt_bias.shape[0]
    inner_width = head_count * HP
    bc_start = 2 * inner_width + head_count
    gate_in = projected[:, :inner_width]
    value_in = projected[:, inner_width : 2 * inner_width]
    step_in = projected[:, 2 * inner_width : bc_start]
    bc_in = projected[:, bc_start : bc_start + 2 * NS]
    qkv_in = projected[:, bc_start + 2 * NS :]
    window_x = jnp.concatenate([conv_x_part, value_in[:, None, :]], axis=1)
    window_bc = jnp.concatenate([conv_bc_part, bc_in[:, None, :]], axis=1)
    value_act = jax.nn.silu(
        jnp.sum(window_x.astype(jnp.float32) * conv_weight_x.astype(jnp.float32)[None], axis=1)
    )
    bc_act = jax.nn.silu(
        jnp.sum(window_bc.astype(jnp.float32) * conv_weight_bc.astype(jnp.float32)[None], axis=1)
    ).astype(jnp.bfloat16)
    b_in = bc_act[:, :NS].astype(jnp.float32)
    c_out = bc_act[:, NS:].astype(jnp.float32)
    step_size = jax.nn.softplus(step_in.astype(jnp.float32) + dt_bias[None, :])
    decay_rate = jnp.exp(-jnp.exp(a_log)[None, :] * step_size)
    value_heads = value_act.reshape(slot_count, head_count, HP)
    state_new = (
        decay_rate[:, :, None, None] * state_part.astype(jnp.float32)
        + (step_size[:, :, None] * value_heads)[:, :, :, None] * b_in[:, None, None, :]
    )
    readout = (
        jnp.einsum("shpn,sn->shp", state_new, c_out, precision=PRECISE)
        + d_skip[None, :, None] * value_heads
    )
    gated = (
        readout.reshape(slot_count, inner_width) * jax.nn.silu(gate_in.astype(jnp.float32))
    ).astype(jnp.bfloat16)
    group_size = QH // KVH
    queries = qkv_in[:, : QH * HD].reshape(slot_count, KVH, group_size, HD)
    key_new = qkv_in[:, QH * HD : (QH + KVH) * HD]
    value_new = qkv_in[:, (QH + KVH) * HD :]
    pages_here = pages_part.shape[1]
    width = pages_part.shape[3]
    cached = pages_part.reshape(slot_count, pages_here * PAGE, width)
    cached_keys = cached[:, :, : KVH * HD].reshape(slot_count, pages_here * PAGE, KVH, HD)
    cached_values = cached[:, :, KVH * HD :].reshape(slot_count, pages_here * PAGE, KVH, HD)
    local_page = jnp.arange(pages_here, dtype=jnp.int32)[:, None]
    offsets = jnp.arange(PAGE, dtype=jnp.int32)[None, :]
    positions = ((local_page * col_count + col_index) * PAGE + offsets).reshape(-1)
    live_mask = (positions[None, :] < lengths_here[:, None])[:, None, None, :]
    score_scale = HD ** (-0.5)
    scores = (
        jnp.einsum("skgd,stkd->skgt", queries, cached_keys, preferred_element_type=jnp.float32)
        * score_scale
    )
    local_peak = jnp.max(jnp.where(live_mask, scores, FLOOR_SCORE), axis=3)
    weights = jnp.where(live_mask, jnp.exp(scores - local_peak[..., None]), 0.0)
    local_total = jnp.sum(weights, axis=3)
    summed = jnp.einsum(
        "skgt,stkd->skgd", weights, cached_values.astype(jnp.float32), precision=PRECISE
    )
    logical = lengths_here // PAGE
    owner_col = logical % col_count
    write_page = logical // col_count
    write_off = lengths_here % PAGE
    fresh_rows = jnp.concatenate([key_new, value_new], axis=1)
    write_mask = (
        (owner_col == col_index)[:, None, None]
        & (jnp.arange(pages_here, dtype=jnp.int32)[None, :, None] == write_page[:, None, None])
        & (jnp.arange(PAGE, dtype=jnp.int32)[None, None, :] == write_off[:, None, None])
    )
    pages_next = jnp.where(write_mask[..., None], fresh_rows[:, None, None, :], pages_part)
    results = (state_new.astype(jnp.bfloat16), window_x[:, 1:], window_bc[:, 1:], pages_next)
    partials = (local_peak, local_total, summed)
    fresh_parts = (
        queries,
        key_new.reshape(slot_count, KVH, HD),
        value_new.reshape(slot_count, KVH, HD),
    )
    return (results, partials, fresh_parts, gated)


def local(
    tokens,
    arrival,
    cache_lengths,
    move_slot,
    move_target,
    page_table,
    kv_pool,
    ssm_state,
    conv_x,
    conv_bc,
    norm_gain,
    weight_z,
    weight_x,
    weight_dt,
    weight_bc,
    weight_qkv,
    conv_weight_x,
    conv_weight_bc,
    dt_bias,
    a_log,
    d_skip,
    weight_ssm_out,
    weight_attn_out,
):
    row_count = lax.axis_size("rows")
    col_count = lax.axis_size("cols")
    row_index = lax.axis_index("rows")
    col_index = lax.axis_index("cols")
    slot_count = ssm_state.shape[0]
    total_rows = tokens.shape[0]
    pages_here = page_table.shape[3]
    width = kv_pool.shape[3]
    layout = residents(move_slot, move_target, row_count, slot_count)
    sending = outgoing_slots(move_slot, move_target, row_index, row_count)
    placing = arrival_index(layout, row_index, slot_count)
    inverse = (
        jnp.zeros((total_rows,), jnp.int32).at[arrival].set(jnp.arange(total_rows, dtype=jnp.int32))
    )
    picked = jnp.take(tokens, inverse[layout.reshape(-1)], axis=0)
    widened = picked.astype(jnp.float32)
    squares = jnp.sum(jnp.square(widened), axis=1)
    scaled = (widened * norm_gain.astype(jnp.float32)[None, :]).astype(jnp.bfloat16)
    weights_in = jnp.concatenate([weight_z, weight_x, weight_dt, weight_bc, weight_qkv], axis=1)
    partial_terms = jnp.dot(scaled, weights_in, preferred_element_type=jnp.float32)
    summed, square_sum = (
        lax.psum_scatter(partial_terms, "rows", scatter_dimension=0, tiled=True),
        lax.psum_scatter(squares, "rows", scatter_dimension=0, tiled=True),
    )
    projected = (summed / jnp.sqrt(square_sum / D + EPSILON)[:, None]).astype(jnp.bfloat16)
    flat_table = page_table[0, 0].reshape(-1)
    own_pages = jnp.take(kv_pool[:, 0], flat_table, axis=0).reshape(
        slot_count, pages_here, PAGE, width
    )
    members = (ssm_state, conv_x, conv_bc, own_pages)
    members = migrate(members, sending, placing)
    served = lax.dynamic_index_in_dim(layout, row_index, 0, keepdims=False)
    lengths_here = jnp.take(cache_lengths, served)
    results, partials, fresh_parts, gated = serve_rows(
        projected,
        members[0],
        members[1],
        members[2],
        members[3],
        lengths_here,
        conv_weight_x,
        conv_weight_bc,
        dt_bias,
        a_log,
        d_skip,
        col_index,
        col_count,
    )
    merged_peak, merged_total, merged_sum = merged(partials, "cols", combine)
    queries, key_new, value_new = fresh_parts
    score_scale = HD ** (-0.5)
    own_score = (
        jnp.einsum("skgd,skd->skg", queries, key_new, preferred_element_type=jnp.float32)
        * score_scale
    )
    joint_peak = jnp.maximum(merged_peak, own_score)
    cache_scale = jnp.exp(merged_peak - joint_peak)
    own_weight = jnp.exp(own_score - joint_peak)
    weighted = (
        merged_sum * cache_scale[..., None]
        + own_weight[..., None] * value_new.astype(jnp.float32)[:, :, None, :]
    )
    attended = (
        (weighted / (merged_total * cache_scale + own_weight)[..., None])
        .reshape(slot_count, QH * HD)
        .astype(jnp.bfloat16)
    )
    share = QH * HD // col_count
    attn_here = lax.dynamic_slice_in_dim(attended, col_index * share, share, 1)
    out_terms = jnp.dot(gated, weight_ssm_out, preferred_element_type=jnp.float32) + jnp.dot(
        attn_here, weight_attn_out, preferred_element_type=jnp.float32
    )
    mixed = lax.psum_scatter(out_terms, "cols", scatter_dimension=1, tiled=True).astype(
        jnp.bfloat16
    )
    state_next, conv_x_next, conv_bc_next, pages_next = results
    owner = (
        jnp.zeros(flat_table.shape, jnp.int32)
        .at[flat_table]
        .set(jnp.arange(flat_table.shape[0], dtype=jnp.int32))
    )
    pool_next = jnp.take(pages_next.reshape(-1, PAGE, width), owner, axis=0)[:, None]
    return (mixed, state_next, conv_x_next, conv_bc_next, pool_next)


def solution(mesh):
    in_specs = (
        P(None, "rows"),
        P(),
        P(),
        P(),
        P(),
        P("rows", "cols", None, None),
        P("rows", "cols", None, None),
        P("rows", "cols", None, None),
        P("rows", None, "cols"),
        P("rows", None, None),
        P("rows"),
        P("rows", "cols"),
        P("rows", "cols"),
        P("rows", "cols"),
        P("rows", None),
        P("rows", None),
        P(None, "cols"),
        P(),
        P("cols"),
        P("cols"),
        P("cols"),
        P("cols", None),
        P("cols", None),
    )
    out_specs = (
        P("rows", "cols"),
        P("rows", "cols", None, None),
        P("rows", None, "cols"),
        P("rows", None, None),
        P("rows", "cols", None, None),
    )
    return jax.shard_map(local, mesh=mesh, in_specs=in_specs, out_specs=out_specs, check_vma=False)
```

profile of v0, /device:TPU:0, one launch (start us, length us, event | category | flops | bytes accessed | tf_op | source)
XLA Modules:
  0.0 297.9 jit_solution(8288255331838023146)
XLA Ops:
  19.9 4.2 %concatenate.24 = bf16[256,3080]{1,0:T(8,128)(2,1)} concatenate(bf16[256,512]{1,0:T(8,128)(2,1)} %param.42, bf16[256,512]{1,0:T(8,128)(2,1)} %param.43, bf16[256,8]{1,0:T(8,128)(2,1)} %copy.181, bf16[256,512]{1,0:T(8,128)(2,1)} %param.45, bf16[256,1536]{1,0:T(8,128)(2,1)} %param.46), dimensions={1} | concatenate | bytes 3153920 | tf_op jit(solution)/shard_map/concatenate | solution.py:233
  27.0 25.8 %fusion = f32[16,3080]{1,0:T(8,128)} fusion(f32[104,3080]{1,0:T(8,128)} %fusion.17), kind=kCustom, calls=%all-reduce-scatter | all-reduce-scatter fusion | flops 394241 | bytes 1478912
  63.2 4.0 %all-to-all-start.1 = ((bf16[8,3,512]{2,1,0:T(4,128)(2,1)}), bf16[8,3,512]{2,1,0:T(4,128)(2,1)}, u32[]{:S(2)}, u32[]{:S(2)}) async-start(bf16[8,3,512]{2,1,0:T(4,128)(2,1)} %copy.182), calls=%async_computation.1 | async-start | bytes 65536 | tf_op jit(solution)/shard_map/all_to_all | solution.py:70
  81.3 14.9 %all-reduce.1 = f32[104]{0:T(128)} all-reduce(f32[104]{0:T(128)S(1)} %fusion.12), channel_id=6, replica_groups=mesh['rows'=8,'cols'=4] {'rows'}, use_global_device_ids=true, to_apply=%region_9.10.clone | all-reduce | flops 104 | bytes 832
  99.0 4.0 %gather_fusion.2 = bf16[8,8,64,256]{3,2,1,0:T(8,128)(2,1)} fusion(bf16[13,8,64,256]{3,2,1,0:T(8,128)(2,1)} %param.38, s32[1024]{0:T(1024)S(1)} %pad_clamp_fusion.6), kind=kCustom, calls=%fused_computation.8 | custom fusion | bytes 4194336 | tf_op jit(solution)/shard_map/jit(_take)/gather | solution.py:68
  116.3 4.0 %all-to-all-start.2 = ((bf16[8,3,512]{2,1,0:T(4,128)(2,1)}), bf16[8,3,512]{2,1,0:T(4,128)(2,1)}, u32[]{:S(2)}, u32[]{:S(2)}) async-start(bf16[8,3,512]{2,1,0:T(4,128)(2,1)} %copy.185), calls=%async_computation.2 | async-start | bytes 65536 | tf_op jit(solution)/shard_map/all_to_all | solution.py:73
  125.1 4.3 %all-to-all-start.3 = ((bf16[8,8,32,512]{3,2,1,0:T(8,128)(2,1)}), bf16[8,8,32,512]{3,2,1,0:T(8,128)(2,1)}, u32[]{:S(2)}, u32[]{:S(2)}) async-start(bf16[8,8,32,512]{3,2,1,0:T(8,128)(2,1)} %broadcast_select_fusion.2), calls=%async_computation.3 | async-start | bytes 4194304 | tf_op jit(solution)/shard_map/all_to_all | solution.py:76
  132.6 6.9 %concatenate.33 = f32[37,3080]{1,0:T(8,128)} concatenate(f32[5,3080]{1,0:T(8,128)} %collective-permute-done.1, f32[16,3080]{1,0:T(8,128)} %collective-permute-done, f32[16,3080]{1,0:T(8,128)} %fusion), dimensions={0} | concatenate | bytes 911680
  158.3 4.4 %all-to-all-start = ((bf16[8,8,64,256]{3,2,1,0:T(8,128)(2,1)}), bf16[8,8,64,256]{3,2,1,0:T(8,128)(2,1)}, u32[]{:S(2)}, u32[]{:S(2)}) async-start(bf16[8,8,64,256]{3,2,1,0:T(8,128)(2,1)} %broadcast_select_fusion.3), calls=%async_computation | async-start | bytes 4194304 | tf_op jit(solution)/shard_map/all_to_all | solution.py:67
  162.7 4.5 %pad_maximum_fusion.1 = bf16[21,8,32,512]{3,2,1,0:T(8,128)(2,1)} fusion(bf16[8,8,32,512]{3,2,1,0:T(8,128)(2,1)} %all-to-all-done.3, bf16[13,8,32,512]{3,2,1,0:T(8,128)(2,1)S(1)} %bitcast.111), kind=kLoop, calls=%fused_computation.27 | loop fusion | flops 2752512 | bytes 11010048 | tf_op jit(solution)/shard_map/concatenate | solution.py:82
  167.2 3.4 %gather_fusion.6 = bf16[13,8,32,512]{3,2,1,0:T(8,128)(2,1)S(1)} fusion(bf16[21,8,32,512]{3,2,1,0:T(8,128)(2,1)} %pad_maximum_fusion.1, s32[1024]{0:T(1024)} %pad_clamp_fusion.5), kind=kCustom, calls=%fused_computation.12 | custom fusion | bytes 6815796 | tf_op jit(solution)/shard_map/jit(_take)/gather | solution.py:82
  173.3 3.6 %copy.189 = bf16[13,256,256]{1,2,0:T(8,128)(2,1)} copy(bf16[13,256,256]{2,1,0:T(8,128)(2,1)} %get-tuple-element.291) | data formatting | bytes 3407872 | tf_op jit(solution)/shard_map/slice | solution.py:152
  177.0 3.6 %copy.191 = bf16[13,256,256]{1,2,0:T(8,128)(2,1)} copy(bf16[13,256,256]{2,1,0:T(8,128)(2,1)} %get-tuple-element.290) | data formatting | bytes 3407872 | tf_op jit(solution)/shard_map/slice | solution.py:153
  185.6 14.0 %all-gather.2 = f32[52,2,4,128]{3,2,1,0:T(4,128)S(1)} all-gather(f32[13,2,4,128]{3,2,1,0:T(4,128)S(1)} %fusion.13), channel_id=4, replica_groups=mesh['rows'=8,'cols'=4] {'cols'}, dimensions={0}, use_global_device_ids=true | all-gather | bytes 266240 | tf_op jit(solution)/shard_map/all_gather | solution.py:21
  200.3 13.1 %all-gather.1 = f32[52,2,4]{2,1,0:T(2,128)S(1)} all-gather(f32[13,2,4]{2,1,0:T(2,128)S(1)} %fusion.14), channel_id=3, replica_groups=mesh['rows'=8,'cols'=4] {'cols'}, dimensions={0}, use_global_device_ids=true | all-gather | bytes 2080 | tf_op jit(solution)/shard_map/all_gather | solution.py:21
  215.6 13.3 %all-gather = f32[52,2,4]{2,1,0:T(2,128)S(1)} all-gather(f32[13,2,4]{2,1,0:T(2,128)S(1)} %get-tuple-element.307), channel_id=2, replica_groups=mesh['rows'=8,'cols'=4] {'cols'}, dimensions={0}, use_global_device_ids=true | all-gather | bytes 2080 | tf_op jit(solution)/shard_map/all_gather | solution.py:21
  231.7 7.5 %while.19 = (s32[]{:T(128)}, f32[13,2,4]{0,2,1:T(4,128)}, f32[13,2,4]{0,2,1:T(4,128)S(1)}, f32[13,2,4,128]{3,2,1,0:T(4,128)S(1)}, f32[4,13,2,4]{1,3,2,0:T(4,128)...) while((s32[]{:T(128)}, f32[13,2,4]{0,2,1:T(4,128)}, ...), condition=%wide.region_16.20_spmd, body=%wide.region_15.19_spmd.sunk | while | flops 40565 | bytes 165719 | solution.py:27
  243.6 5.5 %pad_maximum_fusion = bf16[21,8,64,256]{3,2,1,0:T(8,128)(2,1)} fusion(bf16[8,8,64,256]{3,2,1,0:T(8,128)(2,1)} %all-to-all-done, bf16[13,8,64,256]{3,2,1,0:T(8,128)(2,1)} %param.38), kind=kLoop, calls=%fused_computation.26 | loop fusion | flops 2752512 | bytes 11010048 | tf_op jit(solution)/shard_map/concatenate | solution.py:82
  249.1 5.3 %gather_fusion.3 = bf16[13,8,64,256]{3,2,1,0:T(8,128)(2,1)} fusion(bf16[21,8,64,256]{3,2,1,0:T(8,128)(2,1)} %pad_maximum_fusion, s32[1024]{0:T(1024)} %pad_clamp_fusion.5), kind=kCustom, calls=%fused_computation.9 | custom fusion | bytes 6815796 | tf_op jit(solution)/shard_map/jit(_take)/gather | solution.py:82
  254.4 4.5 %fusion.4 = bf16[13,8,64,256]{3,2,1,0:T(8,128)(2,1)} fusion(f32[13,256]{1,0:T(8,128)S(1)} %copy-done.15, f32[13,8,64]{2,1,0:T(8,128)S(1)} %copy-done.12, f32[13,8]{1,0:T(8,128)S(1)} %copy-done.16, bf16[13,8,64,256]{3,2,1,0:T(8,128)(2,1)} %gather_fusion.3, pred[13]{0:T(512)(128)(4,1)S(1)} %copy-done.20), kind=kLoop, calls=%fused_computation.24 | loop fusion | flops 10223616 | bytes 6856109 | tf_op jit(solution)/shard_map/convert_element_type | solution.py:180
  259.0 5.2 %fusion.5 = f32[13,1,8,64]{3,1,2,0:T(1,128)S(1)} fusion(f32[13,256]{1,0:T(8,128)S(1)} %copy-done.15, f32[13,8,64]{2,1,0:T(8,128)S(1)} %copy-done.12, f32[13,8]{1,0:T(8,128)S(1)} %copy-done.16, bf16[13,8,64,256]{3,2,1,0:T(8,128)(2,1)S(1)} %copy-done.3, pred[13]{0:T(512)(128)(4,1)S(1)} %copy-done.20, bf16[13,256,1,1]{1,0,2,3:T(8,128)(2,1)S(1)} %copy-done.21), kind=kOutput, calls=%fused_computation.25 | convolution fusion | flops 28966912 | bytes 3481517 | tf_op jit(solution)/shard_map/shpn,sn->shp/dot_general | solution.py:139
  271.6 4.9 %gather_fusion.12 = bf16[104,32,512]{2,1,0:T(8,128)(2,1)} fusion(bf16[104,32,512]{2,1,0:T(8,128)(2,1)} %fusion.6, s32[1024]{0:T(1024)} %pad_clamp_fusion), kind=kCustom, calls=%fused_computation.5.clone | custom fusion | bytes 6816160 | tf_op jit(solution)/shard_map/jit(_take)/gather | solution.py:296
  276.4 4.1 %select_bitcast_fusion = bf16[104,1,32,512]{3,2,1,0:T(8,128)(2,1)} fusion(bf16[104,32,512]{2,1,0:T(8,128)(2,1)} %gather_fusion.12, pred[104]{0:T(512)(128)(4,1)S(1)} %copy-done.25), kind=kLoop, calls=%fused_computation.31 | loop fusion | flops 1703936 | bytes 6815848
  280.5 9.2 %reduce-scatter.4.cloned.1.call-done = f32[13,512]{1,0:T(8,128)} async-done(((f32[13,2048]{1,0:T(8,128)}), f32[13,512]{1,0:T(8,128)}) %reduce-scatter.4.cloned.1.call-update) | async-done | bytes 26640 | tf_op jit(solution)/shard_map/reduce_scatter | solution.py:287
  (209 shorter events, 115.6 us)
Async XLA Ops:
  7.2 63.4 %copy-start = (bf16[104,1,32,512]{3,2,1,0:T(8,128)(2,1)S(1)}, bf16[104,1,32,512]{3,2,1,0:T(8,128)(2,1)}, u32[]{:S(2)}) copy-start(bf16[104,1,32,512]{3,2,1,0:T(8,128)(2,1)} %param.37) | copy-start | bytes 10223620
  19.9 39.1 %copy-start.17 = (s32[8,4]{0,1:T(4,128)S(1)}, s32[8,4]{0,1:T(4,128)}, u32[]{:S(2)}) copy-start(s32[8,4]{0,1:T(4,128)} %param.34) | copy-start | bytes 388
  19.9 39.1 %copy-start.18 = (s32[8,4]{0,1:T(4,128)S(1)}, s32[8,4]{0,1:T(4,128)}, u32[]{:S(2)}) copy-start(s32[8,4]{0,1:T(4,128)} %param.35) | copy-start | bytes 388
  19.9 39.4 %copy-start.4 = (bf16[13,3,512]{2,0,1:T(8,128)(2,1)S(1)}, bf16[13,3,512]{2,0,1:T(8,128)(2,1)}, u32[]{:S(2)}) copy-start(bf16[13,3,512]{2,0,1:T(8,128)(2,1)} %param.39) | copy-start | bytes 119812
  19.9 40.1 %copy-start.5 = (bf16[13,3,512]{2,0,1:T(8,128)(2,1)S(1)}, bf16[13,3,512]{2,0,1:T(8,128)(2,1)}, u32[]{:S(2)}) copy-start(bf16[13,3,512]{2,0,1:T(8,128)(2,1)} %param.40) | copy-start | bytes 119812
  52.8 79.8 %collective-permute-start = (f32[16,3080]{1,0:T(8,128)}, f32[16,3080]{1,0:T(8,128)}, u32[]{:S(2)}, u32[]{:S(2)}) collective-permute-start(f32[16,3080]{1,0:T(8,128)} %fusion), channel_id=1, source_target_pairs={{0,4},{4,8},{8,12},{12,16},{16,20},{20,24},{24,28},{1,5},{5,9},{9,... | collective-permute-start | bytes 591368
  56.3 76.3 %collective-permute-start.1 = (f32[5,3080]{1,0:T(8,128)}, f32[5,3080]{1,0:T(8,128)}, u32[]{:S(2)}, u32[]{:S(2)}) collective-permute-start(f32[5,3080]{1,0:T(8,128)} %slice.116), channel_id=1, source_target_pairs={{0,8},{4,12},{8,16},{12,20},{16,24},{20,28},{1,9},{5,13},{9,17},{1... | collective-permute-start | bytes 184808
  63.2 53.0 %all-to-all-start.1 = ((bf16[8,3,512]{2,1,0:T(4,128)(2,1)}), bf16[8,3,512]{2,1,0:T(4,128)(2,1)}, u32[]{:S(2)}, u32[]{:S(2)}) async-start(bf16[8,3,512]{2,1,0:T(4,128)(2,1)} %copy.182), calls=%async_computation.1 | async-start | bytes 65536 | tf_op jit(solution)/shard_map/all_to_all | solution.py:70
  67.3 103.4 %copy-start.19 = (pred[13]{0:T(512)(128)(4,1)}, pred[13]{0:T(512)(128)(4,1)S(1)}, u32[]{:S(2)}) copy-start(pred[13]{0:T(512)(128)(4,1)S(1)} %get-tuple-element.288) | copy-start | bytes 43
  75.5 20.6 %copy-start.2 = (s32[104]{0:T(128)S(1)}, s32[104]{0:T(128)}, u32[]{:S(2)}) copy-start(s32[104]{0:T(128)} %param.33) | copy-start | bytes 1252
  99.0 8.0 %copy-start.22 = (u32[32]{0:T(128)S(1)}, u32[32]{0:T(128)}, u32[]{:S(2)}) copy-start(u32[32]{0:T(128)} %constant.267) | copy-start | bytes 388
  99.0 10.0 %copy-start.26 = (f32[104]{0:T(128)S(1)}, f32[104]{0:T(128)}, u32[]{:S(2)}) copy-start(f32[104]{0:T(128)} %all-reduce.1) | copy-start | bytes 1252
  110.9 18.6 %copy-start.13 = (bf16[13,3,512]{2,1,0:T(4,128)(2,1)S(1)}, bf16[13,3,512]{2,1,0:T(4,128)(2,1)}, u32[]{:S(2)}) copy-start(bf16[13,3,512]{2,1,0:T(4,128)(2,1)} %copy.186) | copy-start | bytes 119812
  116.3 8.8 %all-to-all-start.2 = ((bf16[8,3,512]{2,1,0:T(4,128)(2,1)}), bf16[8,3,512]{2,1,0:T(4,128)(2,1)}, u32[]{:S(2)}, u32[]{:S(2)}) async-start(bf16[8,3,512]{2,1,0:T(4,128)(2,1)} %copy.185), calls=%async_computation.2 | async-start | bytes 65536 | tf_op jit(solution)/shard_map/all_to_all | solution.py:73
  125.1 33.2 %all-to-all-start.3 = ((bf16[8,8,32,512]{3,2,1,0:T(8,128)(2,1)}), bf16[8,8,32,512]{3,2,1,0:T(8,128)(2,1)}, u32[]{:S(2)}, u32[]{:S(2)}) async-start(bf16[8,8,32,512]{3,2,1,0:T(8,128)(2,1)} %broadcast_select_fusion.2), calls=%async_computation.3 | async-start | bytes 4194304 | tf_op jit(solution)/shard_map/all_to_all | solution.py:76
  132.6 15.0 %copy-start.7 = (bf16[13,3,512]{2,1,0:T(4,128)(2,1)}, bf16[13,3,512]{2,1,0:T(4,128)(2,1)S(1)}, u32[]{:S(2)}) copy-start(bf16[13,3,512]{2,1,0:T(4,128)(2,1)S(1)} %get-tuple-element.301) | copy-start | bytes 119812
  158.3 85.3 %all-to-all-start = ((bf16[8,8,64,256]{3,2,1,0:T(8,128)(2,1)}), bf16[8,8,64,256]{3,2,1,0:T(8,128)(2,1)}, u32[]{:S(2)}, u32[]{:S(2)}) async-start(bf16[8,8,64,256]{3,2,1,0:T(8,128)(2,1)} %broadcast_select_fusion.3), calls=%async_computation | async-start | bytes 4194304 | tf_op jit(solution)/shard_map/all_to_all | solution.py:67
  162.7 127.0 %reduce-scatter.4.cloned.1.call-start = ((), (), s32[]{:S(2)}) async-start(), calls=%async_computation.5 | async-start | bytes 163840 | tf_op jit(solution)/shard_map/reduce_scatter | solution.py:287
  173.3 7.3 %copy-start.14 = (bf16[13,2,4,128]{3,2,1,0:T(4,128)(2,1)S(1)}, bf16[13,2,4,128]{3,2,1,0:T(4,128)(2,1)}, u32[]{:S(2)}) copy-start(bf16[13,2,4,128]{3,2,1,0:T(4,128)(2,1)} %reshape.569) | copy-start | bytes 79876
  249.0 5.3 %copy-start.12 = (f32[13,8,64]{2,1,0:T(8,128)S(1)}, f32[13,8,64]{2,1,0:T(8,128)}, u32[]{:S(2)}) copy-start(f32[13,8,64]{2,1,0:T(8,128)} %broadcast_multiply_fusion) | copy-start | bytes 79876
  249.0 5.3 %copy-start.15 = (f32[13,256]{1,0:T(8,128)S(1)}, f32[13,256]{1,0:T(8,128)}, u32[]{:S(2)}) copy-start(f32[13,256]{1,0:T(8,128)} %get-tuple-element.300) | copy-start | bytes 39940
  249.0 5.3 %copy-start.16 = (f32[13,8]{1,0:T(8,128)S(1)}, f32[13,8]{1,0:T(8,128)}, u32[]{:S(2)}) copy-start(f32[13,8]{1,0:T(8,128)} %get-tuple-element.292) | copy-start | bytes 1252
  249.1 5.3 %copy-start.20 = (pred[13]{0:T(512)(128)(4,1)S(1)}, pred[13]{0:T(512)(128)(4,1)}, u32[]{:S(2)}) copy-start(pred[13]{0:T(512)(128)(4,1)} %copy-done.19) | copy-start | bytes 43
  271.6 19.5 %copy-start.1 = (bf16[104,1,32,512]{3,2,1,0:T(8,128)(2,1)S(1)}, bf16[104,1,32,512]{3,2,1,0:T(8,128)(2,1)}, u32[]{:S(2)}) copy-start(bf16[104,1,32,512]{3,2,1,0:T(8,128)(2,1)} %param.37) | copy-start | bytes 10223620
  (10 other events, 26.8 us)
Sparse Core Ops, SparseCore 0:
  268.6 21.0 reduce-scatter.3
where the time goes:
time: 301 us; the launch traced here: 298 us
  local copies, waits for them, and re-layouts  81.7 us (27%)
  blocking collectives  81 us (27%)
  other arithmetic  68.2 us (23%)
  starting transfers between devices  21.3 us (7%)
  matrix products  18 us (6%)
  between operations  15.8 us (5%)
  waiting for transfers between devices  11.8 us (4%)
    unnamed x2, blocking collectives  40.7 us
    all_gather x3, blocking collectives, merged(): everything = jax.tree.map(lambda part: lax.all_gather(part, axis), value)  40.3 us
    unnamed x63, local copies, waits for them, and re-layouts  17 us
    concatenate x4, other arithmetic, migrate(): jnp.concatenate([resident_part, arrived_part], axis=0)  11.6 us
    gather x4, local copies, waits for them, and re-layouts, migrate(): jnp.take(jnp.concatenate([resident_part, arrived_part], axis=0), placing,...  11.4 us
    reduce_scatter x1, waiting for transfers between devices, local(): lax.psum_scatter(out_terms, 'cols', scatter_dimension=1, tiled=True)  9.16 us
  transfers between devices with their start and end apart: 7, of which 2 were waited for; matrix products, arithmetic and copies ran while one was open for 40% of the time, Pallas kernels for 0%

commit v1 on v0

v1 whole, which is shorter than its diff:
```python
import functools

import jax
import jax.numpy as jnp
from jax import lax
from jax.experimental import pallas as pl
from jax.experimental.pallas import tpu as pltpu
from jax.sharding import PartitionSpec as P

HP = 64
NS = 256
KW = 4
QH = 8
KVH = 2
HD = 128
PAGE = 32
LANES = 128
BLOCK = 16

EPSILON = 1e-05
FLOOR_SCORE = -1e30
VMEM_LIMIT = 32 * 1024 * 1024

F32 = jnp.float32
BF16 = jnp.bfloat16
I32 = jnp.int32

SMEM_SPEC = pl.BlockSpec(memory_space=pltpu.SMEM)
VMEM_SPEC = pl.BlockSpec(memory_space=pltpu.VMEM)
ANY_SPEC = pl.BlockSpec(memory_space=pl.ANY)


def silu(v):
    return v / (1.0 + jnp.exp(-v))


def dot(a, b):
    return jnp.dot(a, b, preferred_element_type=F32)


def dot_t(a, b):
    return lax.dot_general(a, b, (((1,), (1,)), ((), ())), preferred_element_type=F32)


def row_iota(shape):
    return lax.broadcasted_iota(I32, shape, 0)


def lane_iota(shape):
    return lax.broadcasted_iota(I32, shape, 1)


class Columns:
    def __init__(self, inner):
        self.z = 0
        self.x = inner
        self.bc = 2 * inner
        self.q = self.bc + 2 * NS
        self.kv = self.q + QH * HD
        self.tail = self.kv + 2 * KVH * HD
        self.width = self.tail + 2 * LANES


class Plan:
    def __init__(self, slots, moves):
        self.source = 0
        self.moved = slots
        self.length = 2 * slots
        self.arrive_slot = 3 * slots
        self.arrive_source = self.arrive_slot + moves
        self.stay_slot = self.arrive_source + moves
        self.size = self.stay_slot + slots - moves


def project_kernel(
    row_ref, arrival, lengths, move_slot, move_target, page_table,
    tokens, gain, conv_x, conv_bc, w_z, w_x, w_dt, w_bc, w_qkv, pool, state,
    out, pages_send, state_send, plan,
    layout, inverse, count, wide, picked, acc_x, acc_bc, tail, sems,
):
    row_count, moves = move_slot.shape
    slots, inner = conv_x.shape[0], conv_x.shape[2]
    pages_here = page_table.shape[1]
    heads = w_dt.shape[1]
    cols, at = Columns(inner), Plan(slots, moves)
    me = row_ref[0]

    copies = []
    for m in range(moves):
        slot, target = move_slot[me, m], move_target[me, m]
        copies.append(pltpu.make_async_copy(state.at[slot], state_send.at[target], sems.at[m, pages_here]))
        for page in range(pages_here):
            copies.append(
                pltpu.make_async_copy(
                    pool.at[page_table[slot, page]], pages_send.at[target, page], sems.at[m, page]
                )
            )
    for copy in copies:
        copy.start()

    wide[...] = tokens[...].astype(F32)
    picked[...] = jnp.zeros_like(picked)

    def begin(t, carry):
        count[t] = 0
        for s in range(slots):
            q = t * slots + s
            layout[q] = q
            inverse[arrival[q]] = q
        return carry

    lax.fori_loop(0, row_count, begin, 0)

    def place(i, carry):
        for m in range(moves):
            target = move_target[i, m]
            turn = count[target]
            count[target] = turn + 1
            layout[target * slots + move_slot[target, turn]] = i * slots + move_slot[i, m]
        return carry

    lax.fori_loop(0, row_count, place, 0)

    def pick(t, carry):
        for s in range(slots):
            source = inverse[layout[t * slots + s]]
            picked[pl.ds(t * BLOCK + s, 1), :] = wide[pl.ds(source, 1), :]
        return carry

    lax.fori_loop(0, row_count, pick, 0)

    rows = picked[...]
    squares = jnp.sum(rows * rows, axis=1, keepdims=True)
    scaled = (rows * gain[...].astype(F32)).astype(BF16)

    acc_x[...] = dot(scaled, w_z[...]).reshape(acc_x.shape)
    acc_bc[...] = dot(scaled, w_bc[...]).reshape(acc_bc.shape)
    for m in range(moves):
        slot, target = move_slot[me, m], move_target[me, m]
        acc_x[target, slots : slots + KW - 1, :] = conv_x[slot].astype(F32)
        acc_bc[target, slots : slots + KW - 1, :] = conv_bc[slot].astype(F32)
    total = row_count * BLOCK
    out[:, cols.z : cols.x] = acc_x[...].reshape(total, inner).astype(BF16)
    out[:, cols.bc : cols.q] = acc_bc[...].reshape(total, 2 * NS).astype(BF16)
    out[:, cols.x : cols.bc] = dot(scaled, w_x[...]).astype(BF16)
    out[:, cols.q : cols.tail] = dot(scaled, w_qkv[...]).astype(BF16)
    tail[...] = jnp.zeros_like(tail)
    tail[:, :heads] = dot(scaled, w_dt[...])
    tail[:, heads : heads + 1] = squares
    high = tail[...].astype(BF16)
    out[:, cols.tail : cols.tail + LANES] = high
    out[:, cols.tail + LANES :] = (tail[...] - high.astype(F32)).astype(BF16)

    stays = 0
    for s in range(slots):
        request = layout[me * slots + s]
        source = lax.div(request, I32(slots))
        moved = jnp.where(source == me, 0, 1)
        plan[at.source + s] = source
        plan[at.moved + s] = moved
        plan[at.length + s] = lengths[request]

        @pl.when(moved == 0)
        def _(s=s, stays=stays):
            plan[at.stay_slot + stays] = s

        stays = stays + 1 - moved
    for m in range(moves):
        slot = move_slot[me, m]
        plan[at.arrive_slot + m] = slot
        plan[at.arrive_source + m] = lax.div(layout[me * slots + slot], I32(slots))

    for copy in copies:
        copy.wait()


def widen(per_head, inner):
    rows = per_head.shape[0]
    first = lane_iota((rows, 2 * HP)) < HP
    pieces = []
    for h in range(0, inner // HP, 2):
        pieces.append(jnp.where(first, per_head[:, h : h + 1], per_head[:, h + 1 : h + 2]))
    return pieces[0] if len(pieces) == 1 else jnp.concatenate(pieces, axis=1)


def advance_state(slot, prior, c_out, b_twice, drive, decay, readout, result):
    heads = prior.shape[0]
    flat = prior[...].reshape(heads * HP, NS)
    read = dot_t(c_out[...], flat)
    here = row_iota(read.shape) == slot
    readout[...] = jnp.where(here, read, readout[...])
    twice = b_twice[...]
    row = row_iota(twice.shape)
    selected = jnp.where((row == slot) | (row == slot + BLOCK), twice, 0.0).astype(BF16)
    outer = dot(drive[...], selected).reshape(heads, HP, NS)
    for h in range(heads):
        rate = decay[pl.ds(slot, 1), h : h + 1]
        result[h] = (rate * prior[h].astype(F32) + outer[h]).astype(BF16)


def mix_kernel(
    plan, received, conv_x, conv_bc, cw_x, cw_bc, dt_bias, a_log, d_skip, state,
    conv_x_next, conv_bc_next, state_next, queries, kv_new, drive, decay, b_twice, c_out,
    readout, scale, base,
    window_x, window_bc, held, made, in_sems, out_sems,
    *, row_count, moves, width,
):
    slots, inner = conv_x.shape[0], conv_x.shape[2]
    heads = dt_bias.shape[1]
    cols, at = Columns(inner), Plan(slots, moves)
    stays = slots - moves
    loads = []
    for j in range(stays):
        loads.append(pltpu.make_async_copy(state.at[plan[at.stay_slot + j]], held.at[j], in_sems.at[j]))
        loads[-1].start()

    def summed(start, stop):
        total = received[0:BLOCK, start:stop].astype(F32)
        for i in range(1, row_count):
            total = total + received[i * BLOCK : (i + 1) * BLOCK, start:stop].astype(F32)
        return total

    tail = summed(cols.tail, cols.tail + LANES) + summed(cols.tail + LANES, cols.width)
    root = jnp.sqrt(tail[:, heads : heads + 1] / width + EPSILON)

    def projected(start, stop):
        return (summed(start, stop) / root).astype(BF16).astype(F32)

    value_in = projected(cols.x, cols.bc)
    bc_in = projected(cols.bc, cols.q)
    step_in = (tail[:, :heads] / root).astype(BF16).astype(F32)

    for s in range(slots):
        start = pl.multiple_of(plan[at.source + s] * BLOCK, BLOCK)
        moved = plan[at.moved + s] == 1
        for own, fresh, begin, end, window, following in (
            (conv_x, value_in, cols.z, cols.x, window_x, conv_x_next),
            (conv_bc, bc_in, cols.bc, cols.q, window_bc, conv_bc_next),
        ):
            arrived = received[pl.ds(start, BLOCK), begin:end].astype(F32)[slots : slots + KW - 1]
            past = jnp.where(moved, arrived, own[s].astype(F32))
            for k in range(KW - 1):
                window[k, s : s + 1, :] = past[k : k + 1]
            following[s] = jnp.concatenate([past[1:], fresh[s : s + 1]], axis=0).astype(BF16)

    def convolved(window, taps, fresh):
        total = fresh * taps[KW - 1 : KW, :].astype(F32)
        for k in range(KW - 1):
            total = total + window[k] * taps[k : k + 1, :].astype(F32)
        return silu(total)

    window_x[:, slots:, :] = jnp.zeros((KW - 1, BLOCK - slots, inner), F32)
    window_bc[:, slots:, :] = jnp.zeros((KW - 1, BLOCK - slots, 2 * NS), F32)
    value_act = convolved(window_x, cw_x, value_in)
    bc_act = convolved(window_bc, cw_bc, bc_in).astype(BF16).astype(F32)
    b_in, c_val = bc_act[:, :NS], bc_act[:, NS:]
    b_twice[...] = jnp.concatenate([b_in, b_in], axis=0)
    c_out[...] = c_val.astype(BF16)

    shifted = step_in + dt_bias[...]
    step_size = jnp.maximum(shifted, 0.0) + jnp.log(1.0 + jnp.exp(-jnp.abs(shifted)))
    rate = jnp.exp(-jnp.exp(a_log[...]) * step_size)
    decay[...] = rate
    driven = widen(step_size, inner) * value_act
    high = driven.astype(BF16).astype(F32)
    drive[...] = jnp.transpose(jnp.concatenate([high, driven - high], axis=0)).astype(BF16)
    gate = silu(projected(cols.z, cols.x))
    b_dot_c = jnp.sum(b_in * c_val, axis=1, keepdims=True)
    skip = widen(jnp.broadcast_to(d_skip[...], (BLOCK, heads)), inner)
    base[...] = (driven * b_dot_c + skip * value_act) * gate
    scale[...] = widen(rate, inner) * gate

    q_in = projected(cols.q, cols.kv)
    for h in range(QH):
        queries[pl.ds(h, BLOCK, stride=QH), :] = q_in[:, h * HD : (h + 1) * HD]
    kv_new[...] = projected(cols.kv, cols.tail)

    readout[...] = jnp.zeros_like(readout)
    stores = []
    for j in range(stays):
        slot = plan[at.stay_slot + j]
        loads[j].wait()
        advance_state(slot, held.at[j], c_out, b_twice, drive, decay, readout, made.at[j])
        stores.append(pltpu.make_async_copy(made.at[j], state_next.at[slot], out_sems.at[j]))
        stores[-1].start()
    for store in stores:
        store.wait()


def attend_kernel(
    col_ref, plan, page_table, queries, kv_new, pool, arrived,
    pool_next, send,
    pages, scores, weighted, peaks, totals, in_sems, out_sems,
    *, moves, col_count,
):
    slots, pages_here = page_table.shape
    at = Plan(slots, moves)
    col = col_ref[0]
    tokens_here = pages_here * PAGE
    kv_width = KVH * HD
    for s in range(slots):
        moved = plan[at.moved + s] == 1

        @pl.when(moved)
        def _(s=s):
            pltpu.make_async_copy(arrived.at[plan[at.source + s]], pages.at[s], in_sems.at[s]).start()

        @pl.when(jnp.logical_not(moved))
        def _(s=s):
            for page in range(pages_here):
                pltpu.make_async_copy(
                    pool.at[page_table[s, page]], pages.at[s, page], in_sems.at[s]
                ).start()

    first_group = row_iota((QH, HD)) < QH // KVH
    lane = lane_iota((QH, tokens_here))
    position = (lax.shift_right_logical(lane, 5) * col_count + col) * PAGE + lax.bitwise_and(lane, PAGE - 1)
    stores = []
    for s in range(slots):
        pltpu.make_async_copy(arrived.at[0], pages.at[s], in_sems.at[s]).wait()
        length = plan[at.length + s]
        logical = lax.div(length, I32(PAGE))

        @pl.when(lax.rem(logical, I32(col_count)) == col)
        def _(s=s, length=length, logical=logical):
            local_page = lax.div(logical, I32(col_count))
            old = pages[s, local_page].astype(F32)
            here = row_iota(old.shape) == lax.rem(length, I32(PAGE))
            pages[s, local_page] = jnp.where(here, kv_new[s : s + 1, :], old).astype(BF16)

        for page in range(pages_here):
            stores.append(
                pltpu.make_async_copy(
                    pages.at[s, page], pool_next.at[page_table[s, page]], out_sems.at[s, page]
                )
            )
            stores[-1].start()
        keys = pages[s, :, :, :kv_width].reshape(tokens_here, kv_width)
        query = queries[s * QH : (s + 1) * QH, :]
        query = jnp.concatenate(
            [jnp.where(first_group, query, 0.0), jnp.where(first_group, 0.0, query)], axis=1
        ).astype(BF16)
        score = dot_t(query, keys) * (HD ** -0.5)
        scores[s * QH : (s + 1) * QH, :] = jnp.where(position <= length, score, FLOOR_SCORE)

    live_rows = slots * QH
    everything = scores[0:live_rows, :]
    peak = jnp.max(everything, axis=1, keepdims=True)
    weights = jnp.where(everything > 0.5 * FLOOR_SCORE, jnp.exp(everything - peak), 0.0)
    total = jnp.sum(weights, axis=1, keepdims=True)
    scores[0:live_rows, :] = weights
    for ref, value in ((weighted, None), (peaks, peak), (totals, total)):
        ref[live_rows:, :] = jnp.zeros((BLOCK * QH - live_rows, HD), F32)
        if value is not None:
            ref[0:live_rows, :] = jnp.broadcast_to(value, (live_rows, HD))
    for s in range(slots):
        values = pages[s, :, :, kv_width:].reshape(tokens_here, kv_width)
        weight = scores[s * QH : (s + 1) * QH, :]
        high = weight.astype(BF16).astype(F32)
        both = dot(jnp.concatenate([high, weight - high], axis=0).astype(BF16), values)
        joined = both[:QH] + both[QH:]
        weighted[s * QH : (s + 1) * QH, :] = jnp.where(first_group, joined[:, :HD], joined[:, HD:])

    share = QH * HD // col_count
    part = min(share, HD)
    lanes = lane_iota((BLOCK, LANES))
    for c in range(col_count):
        stats = jnp.zeros((BLOCK, LANES), F32)
        for j in range(share // part):
            head = (c * share + j * part) // HD
            begin = (c * share + j * part) % HD
            rows = pl.ds(head, BLOCK, stride=QH)
            send[c * BLOCK : (c + 1) * BLOCK, j * part : (j + 1) * part] = weighted[rows, :][
                :, begin : begin + part
            ]
            stats = jnp.where(lanes == 2 * j, peaks[rows, :], stats)
            stats = jnp.where(lanes == 2 * j + 1, totals[rows, :], stats)
        send[c * BLOCK : (c + 1) * BLOCK, share:] = stats
    for store in stores:
        store.wait()


def output_kernel(
    plan, arrived, state_in, drive, decay, b_twice, c_out, readout_in, scale, base, partials, w_ssm, w_attn,
    state_next, send,
    readout, held, made, in_sems, out_sems,
    *, slots, moves, col_count,
):
    del state_in
    at = Plan(slots, moves)
    loads = []
    for m in range(moves):
        loads.append(
            pltpu.make_async_copy(arrived.at[plan[at.arrive_source + m]], held.at[m], in_sems.at[m])
        )
        loads[-1].start()

    share = w_attn.shape[0]
    part = min(share, HD)
    pieces = []
    for j in range(share // part):
        block = [partials[c * BLOCK : (c + 1) * BLOCK, :] for c in range(col_count)]
        peaks = [b[:, share + 2 * j : share + 2 * j + 1] for b in block]
        joint = functools.reduce(jnp.maximum, peaks)
        factors = [jnp.exp(p - joint) for p in peaks]
        total = sum(f * b[:, share + 2 * j + 1 : share + 2 * j + 2] for f, b in zip(factors, block))
        value = sum(f * b[:, j * part : (j + 1) * part] for f, b in zip(factors, block))
        pieces.append(value / total)
    attended = pieces[0] if len(pieces) == 1 else jnp.concatenate(pieces, axis=1)
    attended = jnp.where(row_iota(attended.shape) < slots, attended, 0.0).astype(BF16)

    readout[...] = readout_in[...]
    stores = []
    for m in range(moves):
        slot = plan[at.arrive_slot + m]
        loads[m].wait()
        advance_state(slot, held.at[m], c_out, b_twice, drive, decay, readout, made.at[m])
        stores.append(pltpu.make_async_copy(made.at[m], state_next.at[slot], out_sems.at[m]))
        stores[-1].start()
    gated = (readout[...] * scale[...] + base[...]).astype(BF16)
    columns = w_ssm.shape[1] // col_count
    for c in range(col_count):
        span = slice(c * columns, (c + 1) * columns)
        send[c * BLOCK : (c + 1) * BLOCK, :] = dot(gated, w_ssm[:, span]) + dot(attended, w_attn[:, span])
    for store in stores:
        store.wait()


def sum_kernel(received, out, *, col_count):
    total = received[0:BLOCK, :]
    for c in range(1, col_count):
        total = total + received[c * BLOCK : (c + 1) * BLOCK, :]
    out[...] = total[: out.shape[0]].astype(BF16)


def shape(dims, dtype):
    return jax.ShapeDtypeStruct(tuple(dims), dtype)


def params():
    return pltpu.CompilerParams(vmem_limit_bytes=VMEM_LIMIT)


def cost(flops, moved):
    return pl.CostEstimate(flops=int(flops), bytes_accessed=int(moved), transcendentals=0)


def exchange(value, axis):
    return lax.all_to_all(value, axis, split_axis=0, concat_axis=0, tiled=True)


def local(
    tokens, arrival, cache_lengths, move_slot, move_target, page_table, kv_pool, ssm_state,
    conv_x, conv_bc, norm_gain, weight_z, weight_x, weight_dt, weight_bc, weight_qkv,
    conv_weight_x, conv_weight_bc, dt_bias, a_log, d_skip, weight_ssm_out, weight_attn_out,
):
    row_count = lax.axis_size("rows")
    col_count = lax.axis_size("cols")
    row_index = lax.axis_index("rows").astype(I32).reshape(1)
    col_index = lax.axis_index("cols").astype(I32).reshape(1)
    slots, heads = ssm_state.shape[0], ssm_state.shape[1]
    total, depth = tokens.shape
    moves = move_slot.shape[1]
    pages_here, width = page_table.shape[3], kv_pool.shape[3]
    inner = heads * HP
    stays = slots - moves
    cols, at = Columns(inner), Plan(slots, moves)
    table = page_table[0, 0]
    pool = kv_pool[:, 0]
    rows = row_count * BLOCK
    state_bytes = 2 * inner * NS
    page_bytes = 2 * pages_here * PAGE * width

    partial_sums, pages_send, state_send, plan = pl.pallas_call(
        project_kernel,
        out_shape=(
            shape((rows, cols.width), BF16),
            shape((row_count, pages_here, PAGE, width), BF16),
            shape((row_count, heads, HP, NS), BF16),
            shape((at.size,), I32),
        ),
        in_specs=[SMEM_SPEC] * 6 + [VMEM_SPEC] * 9 + [ANY_SPEC] * 2,
        out_specs=(VMEM_SPEC, ANY_SPEC, ANY_SPEC, SMEM_SPEC),
        scratch_shapes=[
            pltpu.SMEM((total,), I32),
            pltpu.SMEM((total,), I32),
            pltpu.SMEM((row_count,), I32),
            pltpu.VMEM((total, depth), F32),
            pltpu.VMEM((rows, depth), F32),
            pltpu.VMEM((row_count, BLOCK, inner), F32),
            pltpu.VMEM((row_count, BLOCK, 2 * NS), F32),
            pltpu.VMEM((rows, LANES), F32),
            pltpu.SemaphoreType.DMA((moves, pages_here + 1)),
        ],
        compiler_params=params(),
        cost_estimate=cost(2 * rows * depth * cols.width, 8e6),
        name="project",
    )(
        row_index, arrival, cache_lengths, move_slot, move_target, table,
        tokens, norm_gain.reshape(1, -1), conv_x, conv_bc,
        weight_z, weight_x, weight_dt, weight_bc, weight_qkv, pool, ssm_state,
    )
    received = exchange(partial_sums, "rows")
    pages_arrived = exchange(pages_send, "rows")
    state_arrived = exchange(state_send, "rows")

    (
        conv_x_next, conv_bc_next, state_partly, queries, kv_new, drive, decay, b_twice, c_out,
        readout, scale, base,
    ) = pl.pallas_call(
        functools.partial(mix_kernel, row_count=row_count, moves=moves, width=depth * row_count),
        out_shape=(
            shape(conv_x.shape, BF16),
            shape(conv_bc.shape, BF16),
            shape(ssm_state.shape, BF16),
            shape((BLOCK * QH, HD), F32),
            shape((BLOCK, 2 * KVH * HD), F32),
            shape((inner, 2 * BLOCK), BF16),
            shape((BLOCK, heads), F32),
            shape((2 * BLOCK, NS), F32),
            shape((BLOCK, NS), BF16),
            shape((BLOCK, inner), F32),
            shape((BLOCK, inner), F32),
            shape((BLOCK, inner), F32),
        ),
        in_specs=[SMEM_SPEC] + [VMEM_SPEC] * 8 + [ANY_SPEC],
        out_specs=(VMEM_SPEC, VMEM_SPEC, ANY_SPEC) + (VMEM_SPEC,) * 9,
        scratch_shapes=[
            pltpu.VMEM((KW - 1, BLOCK, inner), F32),
            pltpu.VMEM((KW - 1, BLOCK, 2 * NS), F32),
            pltpu.VMEM((stays, heads, HP, NS), BF16),
            pltpu.VMEM((stays, heads, HP, NS), BF16),
            pltpu.SemaphoreType.DMA((stays,)),
            pltpu.SemaphoreType.DMA((stays,)),
        ],
        compiler_params=params(),
        cost_estimate=cost(4 * stays * inner * NS * 32, 4 * stays * state_bytes),
        name="mix",
    )(
        plan, received, conv_x, conv_bc, conv_weight_x, conv_weight_bc,
        dt_bias.reshape(1, -1), a_log.reshape(1, -1), d_skip.reshape(1, -1), ssm_state,
    )

    share = QH * HD // col_count
    pool_next, partials_send = pl.pallas_call(
        functools.partial(attend_kernel, moves=moves, col_count=col_count),
        out_shape=(shape(pool.shape, BF16), shape((col_count * BLOCK, share + LANES), F32)),
        in_specs=[SMEM_SPEC] * 3 + [VMEM_SPEC] * 2 + [ANY_SPEC] * 2,
        out_specs=(ANY_SPEC, VMEM_SPEC),
        scratch_shapes=[
            pltpu.VMEM((slots, pages_here, PAGE, width), BF16),
            pltpu.VMEM((BLOCK * QH, pages_here * PAGE), F32),
            pltpu.VMEM((BLOCK * QH, HD), F32),
            pltpu.VMEM((BLOCK * QH, HD), F32),
            pltpu.VMEM((BLOCK * QH, HD), F32),
            pltpu.SemaphoreType.DMA((slots,)),
            pltpu.SemaphoreType.DMA((slots, pages_here)),
        ],
        compiler_params=params(),
        cost_estimate=cost(4 * slots * 16 * pages_here * PAGE * 256, 4 * slots * page_bytes),
        name="attend",
    )(col_index, plan, table, queries, kv_new, pool, pages_arrived)
    partials = exchange(partials_send, "cols")

    state_next, mixed_send = pl.pallas_call(
        functools.partial(output_kernel, slots=slots, moves=moves, col_count=col_count),
        out_shape=(
            shape(ssm_state.shape, BF16),
            shape((col_count * BLOCK, weight_ssm_out.shape[1] // col_count), F32),
        ),
        in_specs=[SMEM_SPEC] + [ANY_SPEC] * 2 + [VMEM_SPEC] * 10,
        out_specs=(ANY_SPEC, VMEM_SPEC),
        scratch_shapes=[
            pltpu.VMEM((BLOCK, inner), F32),
            pltpu.VMEM((moves, heads, HP, NS), BF16),
            pltpu.VMEM((moves, heads, HP, NS), BF16),
            pltpu.SemaphoreType.DMA((moves,)),
            pltpu.SemaphoreType.DMA((moves,)),
        ],
        input_output_aliases={2: 0},
        compiler_params=params(),
        cost_estimate=cost(2 * BLOCK * 768 * 2048, 4 * moves * state_bytes),
        name="output",
    )(
        plan, state_arrived, state_partly, drive, decay, b_twice, c_out, readout, scale, base,
        partials, weight_ssm_out, weight_attn_out,
    )
    mixed = pl.pallas_call(
        functools.partial(sum_kernel, col_count=col_count),
        out_shape=shape((slots, mixed_send.shape[1]), BF16),
        in_specs=[VMEM_SPEC],
        out_specs=VMEM_SPEC,
        name="total",
    )(exchange(mixed_send, "cols"))
    return (mixed, state_next, conv_x_next, conv_bc_next, pool_next[:, None])


def solution(mesh):
    in_specs = (
        P(None, "rows"),
        P(),
        P(),
        P(),
        P(),
        P("rows", "cols", None, None),
        P("rows", "cols", None, None),
        P("rows", "cols", None, None),
        P("rows", None, "cols"),
        P("rows", None, None),
        P("rows"),
        P("rows", "cols"),
        P("rows", "cols"),
        P("rows", "cols"),
        P("rows", None),
        P("rows", None),
        P(None, "cols"),
        P(),
        P("cols"),
        P("cols"),
        P("cols"),
        P("cols", None),
        P("cols", None),
    )
    out_specs = (
        P("rows", "cols"),
        P("rows", "cols", None, None),
        P("rows", None, "cols"),
        P("rows", None, None),
        P("rows", "cols", None, None),
    )
    return jax.shard_map(local, mesh=mesh, in_specs=in_specs, out_specs=out_specs, check_vma=False)
```

time: 301 us -> 135 us (0.45)
  other arithmetic: 68.2 us -> 0 us
  local copies, waits for them, and re-layouts: 81.7 us -> 34 us
  Pallas kernels: 0 us -> 23.4 us
  blocking collectives: 81 us -> 58.9 us
  matrix products: 18 us -> 0 us
  between operations: 15.8 us -> 0.85 us
  starting transfers between devices: 21.3 us -> 7.95 us
    all_to_all x0 -> x3, blocking collectives: none -> 58.9 us  [exchange(): return lax.all_to_all(value, axis, split_axis=0, concat_axis=0, tiled=True)]
    unnamed x2 -> x0, blocking collectives: 40.7 us -> none
    all_gather x3 -> x0, blocking collectives: 40.3 us -> none  [merged(): everything = jax.tree.map(lambda part: lax.all_gather(part, axis), value)]
    gather x13 -> x0, local copies, waits for them, and re-layouts: 30.8 us -> none  [the longest x4 11.4 us: migrate(): jnp.take(jnp.concatenate([resident_part, arrived_part], axis=0), placing,...]
    pallas_call x0 -> x5, Pallas kernels: none -> 23.4 us  [the longest x1 8.35 us: local(): pl.pallas_call(functools.partial(attend_kernel, moves=moves, col_count=co...]
    dot_general x7 -> x0, matrix products: 18 us -> none  [the longest x1 5.22 us: serve_rows(): jnp.einsum('shpn,sn->shp', state_new, c_out, precision=PRECISE)]
    select_n x18 -> x0, other arithmetic: 16.5 us -> none  [the longest x2 3.5 us: local(): jnp.take(kv_pool[:, 0], flat_table, axis=0)]
    unnamed x63 -> x91, local copies, waits for them, and re-layouts: 17 us -> 32.6 us
  transfers between devices with their start and end apart: 7 -> 2, of which waited for: 2 -> 2; matrix products, arithmetic and copies ran while one was open for 40% -> 1% of each run, Pallas kernels for 0% -> 10%
where the time goes in v1:
time: 135 us; the launch traced here: 134 us
  blocking collectives  58.9 us (44%)
  local copies, waits for them, and re-layouts  34 us (25%)
  Pallas kernels  23.4 us (17%)
  waiting for transfers between devices  8.83 us (7%)
  starting transfers between devices  7.95 us (6%)
    all_to_all x3, blocking collectives, exchange(): return lax.all_to_all(value, axis, split_axis=0, concat_axis=0, tiled=True)  58.9 us
    unnamed x91, local copies, waits for them, and re-layouts  32.6 us
    all_to_all x2, waiting for transfers between devices, exchange(): return lax.all_to_all(value, axis, split_axis=0, concat_axis=0, tiled=True)  8.83 us
    pallas_call x1, Pallas kernels, local(): pl.pallas_call(functools.partial(attend_kernel, moves=moves, col_count=co...  8.35 us
    all_to_all x2, starting transfers between devices, exchange(): return lax.all_to_all(value, axis, split_axis=0, concat_axis=0, tiled=True)  7.95 us
    pallas_call x1, Pallas kernels, local(): pl.pallas_call(project_kernel, out_shape=(shape((rows, cols.width), BF16)...  4.64 us
    pallas_call x1, Pallas kernels, local(): pl.pallas_call(functools.partial(mix_kernel, row_count=row_count, moves=m...  4.58 us
    pallas_call x1, Pallas kernels, local(): pl.pallas_call(functools.partial(output_kernel, slots=slots, moves=moves,...  4.3 us
  transfers between devices with their start and end apart: 2, of which 2 were waited for; matrix products, arithmetic and copies ran while one was open for 1% of the time, Pallas kernels for 10%

profile of v1, /device:TPU:0, one launch (start us, length us, event | category | flops | bytes accessed | tf_op | source)
XLA Modules:
  0.0 133.9 jit_solution(9667781715847107273)
XLA Ops:
  3.6 0.8 copy.32.conv_x
  4.4 0.8 copy.33.conv_bc
  6.1 2.0 %copy-done = bf16[104,1,32,512]{3,2,1,0:T(8,128)(2,1)S(1)} copy-done((bf16[104,1,32,512]{3,2,1,0:T(8,128)(2,1)S(1)}, bf16[104,1,32,512]{3,2,1,0:T(8,128)(2,1)}, u32[]{:S(2)}) %copy-start) | copy-done | bytes 3407896
  8.0 2.0 %copy-done.2 = bf16[13,8,64,256]{3,2,1,0:T(8,128)(2,1)S(1)} copy-done((bf16[13,8,64,256]{3,2,1,0:T(8,128)(2,1)S(1)}, bf16[13,8,64,256]{3,2,1,0:T(8,128)(2,1)}, u32[]{:S(2)}) %copy-start.2) | copy-done | bytes 3407896
  10.0 1.1 copy-done.9
  11.1 0.9 copy-done.10
  12.1 0.9 copy-done.11
  13.0 0.9 copy-done.12
  16.1 4.6 %project.1 = (bf16[128,3328]{1,0:T(8,128)(2,1)S(1)}, bf16[8,8,32,512]{3,2,1,0:T(8,128)(2,1)S(1)}, bf16[8,8,64,256]{3,2,1,0:T(8,128)(2,1)S(1)}, s32[56]{0:T(128)S(1)}) custom-call(s32[1]{0:T(128)} %bitcast.row_ref, s32[104]{0:T(128)S(1)} %copy-done.39, s32[104]{0:T(128)S(1)} %copy-done.40, s32[8,4]{1,0:T(8,128)S(1)} %copy.29.move_slot, ...), custom_call_target="tpu_custom_call" | custom-call | flops 218103808 | bytes 8000000 | tf_op jit(solution)/shard_map/project/pallas_call | solution.py:474
  20.8 18.3 %all_to_all.43 = bf16[8,16,3328]{2,1,0:T(8,128)(2,1)} all-to-all(bf16[8,16,3328]{2,1,0:T(8,128)(2,1)S(1)} %bitcast.19), channel_id=1, replica_groups=mesh['rows'=8,'cols'=4] {'rows'}, dimensions={0} | all-to-all | bytes 1703936 | tf_op jit(solution)/shard_map/all_to_all | solution.py:449
  39.1 29.9 %all_to_all.44.arrived = bf16[8,8,32,512]{3,2,1,0:T(8,128)(2,1)} all-to-all(bf16[8,8,32,512]{3,2,1,0:T(8,128)(2,1)S(1)} %get-tuple-element.38), channel_id=1, replica_groups=mesh['rows'=8,'cols'=4] {'rows'}, dimensions={0} | all-to-all | bytes 4194304 | tf_op jit(solution)/shard_map/all_to_all | solution.py:449
  69.0 4.6 %all-to-all-start = ((bf16[8,8,64,256]{3,2,1,0:T(8,128)(2,1)}), bf16[8,8,64,256]{3,2,1,0:T(8,128)(2,1)}, u32[]{:S(2)}, u32[]{:S(2)}) async-start(bf16[8,8,64,256]{3,2,1,0:T(8,128)(2,1)} %copy-done.7), calls=%async_computation | async-start | bytes 4194304 | tf_op jit(solution)/shard_map/all_to_all | solution.py:449
  73.7 2.0 %copy-done.3 = bf16[13,8,64,256]{3,2,1,0:T(8,128)(2,1)S(1)} copy-done((bf16[13,8,64,256]{3,2,1,0:T(8,128)(2,1)S(1)}, bf16[13,8,64,256]{3,2,1,0:T(8,128)(2,1)}, u32[]{:S(2)}) %copy-start.3) | copy-done | bytes 3407896
  75.7 1.2 copy-done.5
  76.8 4.6 %mix.1 = (bf16[13,3,512]{2,1,0:T(4,128)(2,1)S(1)}, bf16[13,3,512]{2,1,0:T(4,128)(2,1)S(1)}, bf16[13,8,64,256]{3,2,1,0:T(8,128)(2,1)}, f32[128,128]{1,0:T(8,128)S...) custom-call(s32[56]{0:T(128)S(1)} %get-tuple-element.25.plan, ...), custom_call_target="tpu_custom_call" | custom-call | flops 150994944 | bytes 9437184 | tf_op jit(solution)/shard_map/mix/pallas_call | solution.py:510
  87.1 8.4 %attend.1 = (bf16[104,32,512]{2,1,0:T(8,128)(2,1)}, f32[64,384]{1,0:T(8,128)S(1)}) custom-call(s32[1]{0:T(128)} %bitcast.8.col_ref, s32[56]{0:T(128)S(1)} %copy-done.32, s32[13,8]{1,0:T(8,128)S(1)} %copy.31.page_table, f32[128,128]{1,0:T(8,128)S(1)} %get-tuple-element.36.queries, f32[16,512]{1,0:T(8,128)S(1)} %get-tuple-element.37.kv_new, ...), custom_call_target="tpu_custom_call" | custom-call | flops 54525952 | bytes 13631488 | tf_op jit(solution)/shard_map/attend/pallas_call | solution.py:545
  96.1 4.2 %all-to-all-done.arrived = bf16[8,8,64,256]{3,2,1,0:T(8,128)(2,1)} async-done(((bf16[8,8,64,256]{3,2,1,0:T(8,128)(2,1)}), bf16[8,8,64,256]{3,2,1,0:T(8,128)(2,1)}, u32[]{:S(2)}, u32[]{:S(2)}) %all-to-all-start) | async-done | bytes 2097184 | tf_op jit(solution)/shard_map/all_to_all | solution.py:449
  100.3 10.7 %all_to_all.45 = f32[4,16,384]{2,1,0:T(8,128)S(1)} all-to-all(f32[4,16,384]{2,1,0:T(8,128)} %bitcast.21), channel_id=1, replica_groups=mesh['rows'=8,'cols'=4] {'cols'}, dimensions={0} | all-to-all | bytes 196608 | tf_op jit(solution)/shard_map/all_to_all | solution.py:449
  111.0 1.6 %copy-done.6 = bf16[512,2048]{1,0:T(8,128)(2,1)S(1)} copy-done((bf16[512,2048]{1,0:T(8,128)(2,1)S(1)}, bf16[512,2048]{1,0:T(8,128)(2,1)}, u32[]{:S(2)}) %copy-start.6) | copy-done | bytes 2097176
  112.6 1.2 copy-done.8
  118.2 4.3 %output.1 = (bf16[13,8,64,256]{3,2,1,0:T(8,128)(2,1)}, f32[64,512]{1,0:T(8,128)}) custom-call(s32[56]{0:T(128)S(1)} %copy-done.33, bf16[8,8,64,256]{3,2,1,0:T(8,128)(2,1)} %all-to-all-done.arrived, bf16[13,8,64,256]{3,2,1,0:T(8,128)(2,1)} %get-tuple-element.28.state_in, bf16[512,32]{1,0:T(8,128)(2,1)S(1)} %copy-done.14, ...), custom_call_target="tpu_custom_call", output_to_operand_aliasing={{0}: (2, {})} | custom-call | flops 50331648 | bytes 4194304 | tf_op jit(solution)/shard_map/output/pallas_call | solution.py:565
  122.5 3.3 %all-to-all-start.4 = ((f32[4,16,512]{2,1,0:T(8,128)}), f32[4,16,512]{2,1,0:T(8,128)S(1)}, u32[]{:S(2)}, u32[]{:S(2)}) async-start(f32[4,16,512]{2,1,0:T(8,128)} %bitcast.11), calls=%async_computation.4 | async-start | bytes 262144 | tf_op jit(solution)/shard_map/all_to_all | solution.py:449
  127.2 4.6 %all-to-all-done.4 = f32[4,16,512]{2,1,0:T(8,128)S(1)} async-done(((f32[4,16,512]{2,1,0:T(8,128)}), f32[4,16,512]{2,1,0:T(8,128)S(1)}, u32[]{:S(2)}, u32[]{:S(2)}) %all-to-all-start.4) | async-done | bytes 131104 | tf_op jit(solution)/shard_map/all_to_all | solution.py:449
  132.4 1.5 %total.1 = bf16[13,512]{1,0:T(8,128)(2,1)} custom-call(f32[64,512]{1,0:T(8,128)} %bitcast.25), custom_call_target="tpu_custom_call" | custom-call | tf_op jit(solution)/shard_map/total/pallas_call | solution.py:588
  (81 shorter events, 18.5 us)
Async XLA Ops:
  6.1 2.0 %copy-start = (bf16[104,1,32,512]{3,2,1,0:T(8,128)(2,1)S(1)}, bf16[104,1,32,512]{3,2,1,0:T(8,128)(2,1)}, u32[]{:S(2)}) copy-start(bf16[104,1,32,512]{3,2,1,0:T(8,128)(2,1)} %param.29) | copy-start | bytes 10223620
  8.0 2.0 %copy-start.2 = (bf16[13,8,64,256]{3,2,1,0:T(8,128)(2,1)S(1)}, bf16[13,8,64,256]{3,2,1,0:T(8,128)(2,1)}, u32[]{:S(2)}) copy-start(bf16[13,8,64,256]{3,2,1,0:T(8,128)(2,1)} %state.3) | copy-start | bytes 10223620
  10.0 1.1 copy-start.9
  11.1 0.9 copy-start.10
  12.1 0.9 copy-start.11
  13.0 0.9 copy-start.12
  20.7 48.3 %copy-start.7 = (bf16[8,8,64,256]{3,2,1,0:T(8,128)(2,1)}, bf16[8,8,64,256]{3,2,1,0:T(8,128)(2,1)S(1)}, u32[]{:S(2)}) copy-start(bf16[8,8,64,256]{3,2,1,0:T(8,128)(2,1)S(1)} %get-tuple-element.26) | copy-start | bytes 6291460
  20.8 52.9 %copy-start.31 = (s32[56]{0:T(128)}, s32[56]{0:T(128)S(1)}, u32[]{:S(2)}) copy-start(s32[56]{0:T(128)S(1)} %get-tuple-element.25.plan) | copy-start | bytes 676
  39.1 34.6 %copy-start.34 = (bf16[4,512]{1,0:T(4,128)(2,1)S(1)}, bf16[4,512]{1,0:T(4,128)(2,1)}, u32[]{:S(2)}) copy-start(bf16[4,512]{1,0:T(4,128)(2,1)} %cw_x.1) | copy-start | bytes 12292
  39.1 34.6 %copy-start.35 = (bf16[4,512]{1,0:T(4,128)(2,1)S(1)}, bf16[4,512]{1,0:T(4,128)(2,1)}, u32[]{:S(2)}) copy-start(bf16[4,512]{1,0:T(4,128)(2,1)} %cw_bc.1) | copy-start | bytes 12292
  39.1 34.6 %copy-start.36 = (f32[8]{0:T(128)S(1)}, f32[8]{0:T(128)}, u32[]{:S(2)}) copy-start(f32[8]{0:T(128)} %param.41) | copy-start | bytes 100
  39.1 34.6 %copy-start.37 = (f32[8]{0:T(128)S(1)}, f32[8]{0:T(128)}, u32[]{:S(2)}) copy-start(f32[8]{0:T(128)} %param.42) | copy-start | bytes 100
  39.1 34.6 %copy-start.38 = (f32[8]{0:T(128)S(1)}, f32[8]{0:T(128)}, u32[]{:S(2)}) copy-start(f32[8]{0:T(128)} %param.43) | copy-start | bytes 100
  69.0 17.3 %copy-start.1 = (bf16[104,1,32,512]{3,2,1,0:T(8,128)(2,1)S(1)}, bf16[104,1,32,512]{3,2,1,0:T(8,128)(2,1)}, u32[]{:S(2)}) copy-start(bf16[104,1,32,512]{3,2,1,0:T(8,128)(2,1)} %param.29) | copy-start | bytes 10223620
  69.0 31.3 %all-to-all-start = ((bf16[8,8,64,256]{3,2,1,0:T(8,128)(2,1)}), bf16[8,8,64,256]{3,2,1,0:T(8,128)(2,1)}, u32[]{:S(2)}, u32[]{:S(2)}) async-start(bf16[8,8,64,256]{3,2,1,0:T(8,128)(2,1)} %copy-done.7), calls=%async_computation | async-start | bytes 4194304 | tf_op jit(solution)/shard_map/all_to_all | solution.py:449
  73.7 2.0 %copy-start.3 = (bf16[13,8,64,256]{3,2,1,0:T(8,128)(2,1)S(1)}, bf16[13,8,64,256]{3,2,1,0:T(8,128)(2,1)}, u32[]{:S(2)}) copy-start(bf16[13,8,64,256]{3,2,1,0:T(8,128)(2,1)} %state.3) | copy-start | bytes 10223620
  75.7 1.2 copy-start.5
  76.8 9.5 %copy-start.4 = (bf16[8,8,32,512]{3,2,1,0:T(8,128)(2,1)S(1)}, bf16[8,8,32,512]{3,2,1,0:T(8,128)(2,1)}, u32[]{:S(2)}) copy-start(bf16[8,8,32,512]{3,2,1,0:T(8,128)(2,1)} %all_to_all.44.arrived) | copy-start | bytes 6291460
  86.3 24.7 %copy-start.14 = (bf16[512,32]{1,0:T(8,128)(2,1)S(1)}, bf16[512,32]{1,0:T(8,128)(2,1)}, u32[]{:S(2)}) copy-start(bf16[512,32]{1,0:T(8,128)(2,1)} %copy-done.13) | copy-start | bytes 98308
  111.0 1.6 %copy-start.6 = (bf16[512,2048]{1,0:T(8,128)(2,1)S(1)}, bf16[512,2048]{1,0:T(8,128)(2,1)}, u32[]{:S(2)}) copy-start(bf16[512,2048]{1,0:T(8,128)(2,1)} %w_ssm.1) | copy-start | bytes 6291460
  112.6 1.2 copy-start.8
  118.2 7.7 %copy-start.20 = (bf16[13,3,512]{2,1,0:T(4,128)(2,1)S(1)}, bf16[13,3,512]{2,1,0:T(4,128)(2,1)}, u32[]{:S(2)}) copy-start(bf16[13,3,512]{2,1,0:T(4,128)(2,1)} %copy-done.19) | copy-start | bytes 119812
  118.2 8.3 %copy-start.18 = (bf16[13,3,512]{2,1,0:T(4,128)(2,1)S(1)}, bf16[13,3,512]{2,1,0:T(4,128)(2,1)}, u32[]{:S(2)}) copy-start(bf16[13,3,512]{2,1,0:T(4,128)(2,1)} %copy-done.17) | copy-start | bytes 119812
  122.5 9.2 %all-to-all-start.4 = ((f32[4,16,512]{2,1,0:T(8,128)}), f32[4,16,512]{2,1,0:T(8,128)S(1)}, u32[]{:S(2)}, u32[]{:S(2)}) async-start(f32[4,16,512]{2,1,0:T(8,128)} %bitcast.11), calls=%async_computation.4 | async-start | bytes 262144 | tf_op jit(solution)/shard_map/all_to_all | solution.py:449
  (20 other events, 13.5 us)

commit v2 on v1

v2 whole, which is shorter than its diff:
```python
import functools

import jax
import jax.numpy as jnp
from jax import lax
from jax.experimental import pallas as pl
from jax.experimental.pallas import tpu as pltpu
from jax.sharding import PartitionSpec as P

HP = 64
NS = 256
KW = 4
QH = 8
KVH = 2
HD = 128
PAGE = 32
LANES = 128
BLOCK = 16

EPSILON = 1e-05
FLOOR_SCORE = -1e30
VMEM_LIMIT = 60 * 1024 * 1024

F32 = jnp.float32
BF16 = jnp.bfloat16
I32 = jnp.int32

SMEM_SPEC = pl.BlockSpec(memory_space=pltpu.SMEM)
VMEM_SPEC = pl.BlockSpec(memory_space=pltpu.VMEM)
ANY_SPEC = pl.BlockSpec(memory_space=pl.ANY)


def silu(v):
    return v / (1.0 + jnp.exp(-v))


def dot(a, b):
    return jnp.dot(a, b, preferred_element_type=F32)


def dot_t(a, b):
    return lax.dot_general(a, b, (((1,), (1,)), ((), ())), preferred_element_type=F32)


def row_iota(shape):
    return lax.broadcasted_iota(I32, shape, 0)


def lane_iota(shape):
    return lax.broadcasted_iota(I32, shape, 1)


class Columns:
    def __init__(self, inner):
        self.z = 0
        self.x = inner
        self.bc = 2 * inner
        self.q = self.bc + 2 * NS
        self.kv = self.q + QH * HD
        self.tail = self.kv + 2 * KVH * HD
        self.width = self.tail + 2 * LANES


class Plan:
    def __init__(self, slots, moves):
        self.length = 0
        self.slot = slots
        self.target = self.slot + moves
        self.source = self.target + moves
        self.arrived_length = self.source + moves
        self.stay = self.arrived_length + moves
        self.size = self.stay + slots - moves


class Note:
    gated, key_value, drive, drive_low, mixing, conv_x, conv_bc, attended = 0, 1, 2, 3, 4, 5, 8, 11
    decay, decay_low = NS, NS + LANES


def project_kernel(
    row_ref, arrival, lengths, move_slot, move_target, table,
    tokens, gain, w_z, w_x, w_dt, w_bc, w_qkv, pool, state,
    out, plan, *rest,
    slots,
):
    moves, row_count = move_slot.shape
    pages_here = table.shape[0]
    heads, depth = w_dt.shape
    inner = heads * HP
    cols, at = Columns(inner), Plan(slots, moves)
    parcels = rest[: row_count - 1]
    inverse, wide, picked, tail, packed, in_sems, out_sems = rest[row_count - 1 :]
    me = row_ref[0]

    loads = []
    for m in range(moves):
        slot = move_slot[m, me]
        for page in range(pages_here):
            loads.append(
                pltpu.make_async_copy(pool.at[table[page, slot]], packed.at[m, page], in_sems.at[m, page])
            )
        for half in range(2):
            loads.append(
                pltpu.make_async_copy(
                    state.at[slot, :, half * PAGE : (half + 1) * PAGE, :],
                    packed.at[m, pages_here:, :, half * NS : (half + 1) * NS],
                    in_sems.at[m, pages_here + half],
                )
            )
    for load in loads:
        load.start()

    wide[...] = tokens[...].astype(F32)
    picked[...] = jnp.zeros_like(picked)

    def invert(t, carry):
        for s in range(slots):
            inverse[arrival[t * slots + s]] = t * slots + s
        return carry

    lax.fori_loop(0, row_count, invert, 0)

    def pick(t, carry):
        for s in range(slots):
            picked[pl.ds(t * BLOCK + s, 1), :] = wide[pl.ds(inverse[t * slots + s], 1), :]
        return carry

    lax.fori_loop(0, row_count, pick, 0)

    for load in loads:
        load.wait()
    for m in range(moves):
        away = lax.bitwise_xor(move_target[m, me], me)
        for d in range(1, row_count):

            @pl.when(away == d)
            def _(m=m, d=d):
                pltpu.make_async_copy(packed.at[m], parcels[d - 1], out_sems.at[m]).start()

    rows = picked[...]
    squares = jnp.sum(rows * rows, axis=1, keepdims=True)
    scaled = (rows * gain[...].astype(F32).reshape(1, depth)).astype(BF16)
    out[:, cols.z : cols.x] = dot(scaled, w_z[...]).astype(BF16)
    out[:, cols.x : cols.bc] = dot(scaled, w_x[...]).astype(BF16)
    out[:, cols.bc : cols.q] = dot(scaled, w_bc[...]).astype(BF16)
    out[:, cols.q : cols.tail] = dot(scaled, w_qkv[...]).astype(BF16)
    tail[...] = jnp.zeros_like(tail)
    tail[:, :heads] = dot_t(scaled, w_dt[...])
    tail[:, heads : heads + 1] = squares
    high = tail[...].astype(BF16)
    out[:, cols.tail : cols.tail + LANES] = high
    out[:, cols.tail + LANES :] = (tail[...] - high.astype(F32)).astype(BF16)

    stays = 0
    for s in range(slots):
        plan[at.length + s] = lengths[me * slots + s]
        leaves = move_slot[0, me] == s
        for m in range(1, moves):
            leaves = jnp.logical_or(leaves, move_slot[m, me] == s)

        @pl.when(jnp.logical_not(leaves))
        def _(s=s, stays=stays):
            plan[at.stay + stays] = s

        stays = stays + jnp.where(leaves, 0, 1)
    for m in range(moves):
        plan[at.slot + m] = move_slot[m, me]
        plan[at.target + m] = move_target[m, me]

    def seek(i, turn):
        for m in range(moves):
            comes = move_target[m, i] == me

            @pl.when(comes)
            def _(m=m, turn=turn):
                plan[at.source + turn] = i
                plan[at.arrived_length + turn] = lengths[i * slots + move_slot[m, i]]

            turn = turn + jnp.where(comes, 1, 0)
        return turn

    lax.fori_loop(0, row_count, seek, I32(0))
    for m in range(moves):
        pltpu.make_async_copy(packed.at[m], parcels[0], out_sems.at[m]).wait()


def widen(per_head, inner):
    rows = per_head.shape[0]
    first = lane_iota((rows, 2 * HP)) < HP
    pieces = []
    for h in range(0, inner // HP, 2):
        pieces.append(jnp.where(first, per_head[:, h : h + 1], per_head[:, h + 1 : h + 2]))
    return pieces[0] if len(pieces) == 1 else jnp.concatenate(pieces, axis=1)


class Sums:
    def __init__(self, received, heads, row_count, width):
        self.received, self.row_count = received, row_count
        cols = Columns(heads * HP)
        tail = self.total(cols.tail, cols.tail + LANES) + self.total(cols.tail + LANES, cols.width)
        self.root = jnp.sqrt(tail[:, heads : heads + 1] / width + EPSILON)
        self.step_in = (tail[:, :heads] / self.root).astype(BF16).astype(F32)

    def total(self, start, stop):
        result = self.received[0:BLOCK, start:stop].astype(F32)
        for i in range(1, self.row_count):
            result = result + self.received[i * BLOCK : (i + 1) * BLOCK, start:stop].astype(F32)
        return result

    def projected(self, start, stop):
        return (self.total(start, stop) / self.root).astype(BF16).astype(F32)


def insert_row(page, row, offset):
    old = page[...].astype(F32)
    page[...] = jnp.where(row_iota(old.shape) == offset, row, old).astype(BF16)


def place_of(length, col_count):
    logical = lax.div(length, I32(PAGE))
    return lax.rem(logical, I32(col_count)), lax.div(logical, I32(col_count)), lax.rem(length, I32(PAGE))


def attend_kernel(
    col_ref, plan, table, received, pool,
    pool_next, send, kv_new,
    pages, queries, scores, weighted, peaks, totals, in_sems, out_sems,
    *, moves, heads, row_count, col_count, width,
):
    pages_here, slots = table.shape
    cols, at = Columns(heads * HP), Plan(slots, moves)
    col = col_ref[0]
    tokens_here = pages_here * PAGE
    kv_width = KVH * HD
    loads = []
    for s in range(slots):
        for page in range(pages_here):
            loads.append(
                pltpu.make_async_copy(pool.at[table[page, s]], pages.at[s, page], in_sems.at[s, page])
            )
            loads[-1].start()

    sums = Sums(received, heads, row_count, width)
    kv_new[...] = sums.projected(cols.kv, cols.tail)
    q_in = sums.projected(cols.q, cols.kv)
    for h in range(QH):
        queries[pl.ds(h, BLOCK, stride=QH), :] = q_in[:, h * HD : (h + 1) * HD]

    first_group = row_iota((QH, HD)) < QH // KVH
    lane = lane_iota((QH, tokens_here))
    position = (lax.shift_right_logical(lane, 5) * col_count + col) * PAGE + lax.bitwise_and(lane, PAGE - 1)
    for s in range(slots):
        for load in loads[s * pages_here : (s + 1) * pages_here]:
            load.wait()
        length = plan[at.length + s]
        owner, local_page, offset = place_of(length, col_count)

        @pl.when(owner == col)
        def _(s=s, local_page=local_page, offset=offset):
            insert_row(pages.at[s, local_page], kv_new[s : s + 1, :], offset)

        keys = pages[s, :, :, :kv_width].reshape(tokens_here, kv_width)
        query = queries[s * QH : (s + 1) * QH, :]
        query = jnp.concatenate(
            [jnp.where(first_group, query, 0.0), jnp.where(first_group, 0.0, query)], axis=1
        ).astype(BF16)
        score = dot_t(query, keys) * (HD ** -0.5)
        scores[s * QH : (s + 1) * QH, :] = jnp.where(position <= length, score, FLOOR_SCORE)

    stores = []
    for j in range(slots - moves):
        slot = plan[at.stay + j]
        for page in range(pages_here):
            stores.append(
                pltpu.make_async_copy(
                    pages.at[slot, page], pool_next.at[table[page, slot]], out_sems.at[j, page]
                )
            )
            stores[-1].start()

    live_rows = slots * QH
    everything = scores[0:live_rows, :]
    peak = jnp.max(everything, axis=1, keepdims=True)
    weights = jnp.where(everything > 0.5 * FLOOR_SCORE, jnp.exp(everything - peak), 0.0)
    total = jnp.sum(weights, axis=1, keepdims=True)
    scores[0:live_rows, :] = weights
    for ref, value in ((weighted, None), (peaks, peak), (totals, total)):
        ref[live_rows:, :] = jnp.zeros((BLOCK * QH - live_rows, HD), F32)
        if value is not None:
            ref[0:live_rows, :] = jnp.broadcast_to(value, (live_rows, HD))
    for s in range(slots):
        values = pages[s, :, :, kv_width:].reshape(tokens_here, kv_width)
        weight = scores[s * QH : (s + 1) * QH, :]
        high = weight.astype(BF16).astype(F32)
        both = dot(jnp.concatenate([high, weight - high], axis=0).astype(BF16), values)
        joined = both[:QH] + both[QH:]
        weighted[s * QH : (s + 1) * QH, :] = jnp.where(first_group, joined[:, :HD], joined[:, HD:])

    share = QH * HD // col_count
    part = min(share, HD)
    lanes = lane_iota((BLOCK, LANES))
    for c in range(col_count):
        stats = jnp.zeros((BLOCK, LANES), F32)
        for j in range(share // part):
            head = (c * share + j * part) // HD
            begin = (c * share + j * part) % HD
            rows = pl.ds(head, BLOCK, stride=QH)
            send[c * BLOCK : (c + 1) * BLOCK, j * part : (j + 1) * part] = weighted[rows, :][
                :, begin : begin + part
            ]
            stats = jnp.where(lanes == 2 * j, peaks[rows, :], stats)
            stats = jnp.where(lanes == 2 * j + 1, totals[rows, :], stats)
        send[c * BLOCK : (c + 1) * BLOCK, share:] = stats
    for store in stores:
        store.wait()


def mix_kernel(
    plan, received, conv_x, conv_bc, cw_x, cw_bc, dt_bias, a_log, d_skip, state,
    conv_x_next, conv_bc_next, state_next, gated, driven_out, decay, b_out,
    readout, held, made, drive, b_twice, in_sems, out_sems,
    *, moves, row_count, width,
):
    slots, inner = conv_x.shape[1], conv_x.shape[2]
    heads = dt_bias.shape[0]
    cols, at = Columns(inner), Plan(slots, moves)
    loads = []
    for s in range(slots):
        loads.append(pltpu.make_async_copy(state.at[s], held.at[s], in_sems.at[s]))
        loads[-1].start()

    sums = Sums(received, heads, row_count, width)

    def convolved(past, taps, fresh, following):
        past_rows = [past[k].astype(F32) for k in range(KW - 1)]
        total = fresh[:slots] * taps[KW - 1 : KW, :].astype(F32)
        for k in range(KW - 1):
            total = total + past_rows[k] * taps[k : k + 1, :].astype(F32)
            following[k] = past_rows[k + 1] if k < KW - 2 else fresh[:slots]
        return jnp.concatenate([silu(total), jnp.zeros((BLOCK - slots, total.shape[1]), F32)], axis=0)

    value_act = convolved(conv_x, cw_x, sums.projected(cols.x, cols.bc), conv_x_next)
    bc_act = convolved(conv_bc, cw_bc, sums.projected(cols.bc, cols.q), conv_bc_next)
    bc_act = bc_act.astype(BF16).astype(F32)
    b_in, c_val = bc_act[:, :NS], bc_act[:, NS:]
    b_out[...] = b_in
    b_twice[...] = jnp.concatenate([b_in, b_in], axis=0)
    c_out = c_val.astype(BF16)

    shifted = sums.step_in + dt_bias[...].reshape(1, heads)
    step_size = jnp.maximum(shifted, 0.0) + jnp.log(1.0 + jnp.exp(-jnp.abs(shifted)))
    rate = jnp.exp(-jnp.exp(a_log[...].reshape(1, heads)) * step_size)
    decay[...] = rate
    driven = widen(step_size, inner) * value_act
    driven_out[...] = driven
    high = driven.astype(BF16).astype(F32)
    drive[...] = jnp.transpose(jnp.concatenate([high, driven - high], axis=0)).astype(BF16)

    readout[...] = jnp.zeros_like(readout)

    def read(s, carry):
        pltpu.make_async_copy(state.at[s], held.at[s], in_sems.at[s]).wait()
        value = dot_t(c_out, held[s].reshape(inner, NS))
        readout[...] = jnp.where(row_iota(value.shape) == s, value, readout[...])
        return carry

    for s in range(slots):
        read(s, 0)

    stores = []
    for j in range(slots - moves):
        slot = plan[at.stay + j]
        advance_state(slot, held.at[slot], b_twice, drive, decay, made.at[j])
        stores.append(pltpu.make_async_copy(made.at[j], state_next.at[slot], out_sems.at[j]))
        stores[-1].start()

    gate = silu(sums.projected(cols.z, cols.x))
    b_dot_c = jnp.sum(b_in * c_val, axis=1, keepdims=True)
    skip = widen(jnp.broadcast_to(d_skip[...].reshape(1, heads), (BLOCK, heads)), inner)
    total = widen(rate, inner) * readout[...] + driven * b_dot_c + skip * value_act
    gated[...] = (total * gate).astype(BF16).astype(F32)
    for store in stores:
        store.wait()


def advance_state(slot, prior, b_twice, drive, decay, result):
    heads = result.shape[0]
    twice = b_twice[...]
    half = twice.shape[0] // 2
    row = row_iota(twice.shape)
    selected = jnp.where((row == slot) | (row == slot + half), twice, 0.0).astype(BF16)
    outer = dot(drive[...], selected).reshape(heads, HP, NS)
    for h in range(heads):
        rate = decay[pl.ds(slot, 1), h : h + 1]
        result[h] = (rate * prior[h].astype(F32) + outer[h]).astype(BF16)


def merge_kernel(
    plan, partials, gated, kv_new, driven, decay, b_in, conv_x, conv_bc,
    attended, send,
    block, attended_wide,
    *, moves, row_count, col_count,
):
    slots, inner = conv_x.shape[1], conv_x.shape[2]
    heads, share = decay.shape[1], attended.shape[1]
    at = Plan(slots, moves)
    part = min(share, HD)
    pieces = []
    for j in range(share // part):
        blocks = [partials[c * BLOCK : (c + 1) * BLOCK, :] for c in range(col_count)]
        peaks = [b[:, share + 2 * j : share + 2 * j + 1] for b in blocks]
        joint = functools.reduce(jnp.maximum, peaks)
        factors = [jnp.exp(p - joint) for p in peaks]
        total = sum(f * b[:, share + 2 * j + 1 : share + 2 * j + 2] for f, b in zip(factors, blocks))
        value = sum(f * b[:, j * part : (j + 1) * part] for f, b in zip(factors, blocks))
        pieces.append(value / total)
    joined = pieces[0] if len(pieces) == 1 else jnp.concatenate(pieces, axis=1)
    joined = jnp.where(row_iota(joined.shape) < slots, joined, 0.0).astype(BF16)
    attended[...] = joined.astype(F32)

    block[...] = jnp.zeros_like(block)
    for m in range(moves):
        slot = plan[at.slot + m]
        row = pl.ds(slot, 1)

        def put(index, value, start=0):
            block[index : index + 1, start : start + value.shape[1]] = value

        put(Note.gated, gated[row, :])
        put(Note.key_value, kv_new[row, :])
        for index, value, start, low_index, low_start in (
            (Note.drive, driven[row, :], 0, Note.drive_low, 0),
            (Note.mixing, decay[row, :], Note.decay, Note.mixing, Note.decay_low),
        ):
            high = value.astype(BF16).astype(F32)
            put(index, high, start)
            put(low_index, value - high, low_start)
        put(Note.mixing, b_in[row, :])
        for k in range(KW - 1):
            put(Note.conv_x + k, conv_x[k, row, :])
            put(Note.conv_bc + k, conv_bc[k, row, :])
        put(Note.attended, attended[row, :])
        start = pl.multiple_of(plan[at.target + m] * BLOCK, BLOCK)
        send[pl.ds(start, BLOCK), :] = block[...].astype(BF16)


def output_kernel(plan, gated, attended, notes, w_ssm, w_attn, send, gated_here, attended_here, *, slots, moves, col_count):
    at = Plan(slots, moves)
    inner, share = gated.shape[1], attended.shape[1]
    gated_here[...] = gated[...]
    attended_here[...] = attended[...]
    for m in range(moves):
        start = pl.multiple_of(plan[at.source + m] * BLOCK, BLOCK)
        note = notes[pl.ds(start, BLOCK), :].astype(F32)
        row = pl.ds(plan[at.slot + m], 1)
        gated_here[row, :] = note[Note.gated : Note.gated + 1, :inner]
        attended_here[row, :] = note[Note.attended : Note.attended + 1, :share]
    columns = w_ssm.shape[1] // col_count
    left, right = gated_here[...].astype(BF16), attended_here[...].astype(BF16)
    for c in range(col_count):
        span = slice(c * columns, (c + 1) * columns)
        send[c * BLOCK : (c + 1) * BLOCK, :] = dot(left, w_ssm[:, span]) + dot(right, w_attn[:, span])


def sum_kernel(received, out, *, col_count):
    total = received[0:BLOCK, :]
    for c in range(1, col_count):
        total = total + received[c * BLOCK : (c + 1) * BLOCK, :]
    out[...] = total[: out.shape[0]].astype(BF16)


def arrive_kernel(
    row_ref, col_ref, plan, table, notes, conv_x, conv_bc, state_in, pool_in, *rest, moves, row_count, col_count
):
    del state_in, pool_in
    pages_here, slots = table.shape
    inner = conv_x.shape[2]
    heads = inner // HP
    at = Plan(slots, moves)
    parcels = rest[: row_count - 1]
    conv_x_next, conv_bc_next, state_next, pool_next = rest[row_count - 1 : row_count + 3]
    packed, made, drive, decay, b_twice, window_x, window_bc, in_sems, out_sems = rest[row_count + 3 :]
    me, col = row_ref[0], col_ref[0]
    for m in range(moves):
        away = lax.bitwise_xor(plan[at.source + m], me)
        for d in range(1, row_count):

            @pl.when(away == d)
            def _(m=m, d=d):
                pltpu.make_async_copy(parcels[d - 1], packed.at[m], in_sems.at[m]).start()

    for k in range(KW - 1):
        window_x[k] = conv_x[k]
        window_bc[k] = conv_bc[k]
    rows = []
    b_twice[...] = jnp.zeros_like(b_twice)
    half = b_twice.shape[0] // 2
    for m in range(moves):
        start = pl.multiple_of(plan[at.source + m] * BLOCK, BLOCK)
        note = notes[pl.ds(start, BLOCK), :].astype(F32)
        rows.append(note)
        row = pl.ds(plan[at.slot + m], 1)
        for k in range(KW - 1):
            window_x[k, row, :] = note[Note.conv_x + k : Note.conv_x + k + 1, :inner]
            window_bc[k, row, :] = note[Note.conv_bc + k : Note.conv_bc + k + 1, : 2 * NS]
        mixing = note[Note.mixing : Note.mixing + 1, :]
        b_twice[m : m + 1, :] = mixing[:, :NS]
        b_twice[half + m : half + m + 1, :] = mixing[:, :NS]
        decay[m : m + 1, :] = (
            mixing[:, Note.decay : Note.decay + heads] + mixing[:, Note.decay_low : Note.decay_low + heads]
        )
    padding = [jnp.zeros((half - moves, inner), F32)]
    stacked = [note[Note.drive : Note.drive + 1, :inner] for note in rows] + padding
    stacked += [note[Note.drive_low : Note.drive_low + 1, :inner] for note in rows] + padding
    drive[...] = jnp.transpose(jnp.concatenate(stacked, axis=0)).astype(BF16)
    for k in range(KW - 1):
        conv_x_next[k] = window_x[k].astype(BF16)
        conv_bc_next[k] = window_bc[k].astype(BF16)

    stores = []
    for m in range(moves):
        slot = plan[at.slot + m]
        pltpu.make_async_copy(parcels[0], packed.at[m], in_sems.at[m]).wait()
        owner, local_page, offset = place_of(plan[at.arrived_length + m], col_count)
        key_value = rows[m][Note.key_value : Note.key_value + 1, : 2 * KVH * HD]

        @pl.when(owner == col)
        def _(m=m, local_page=local_page, offset=offset, key_value=key_value):
            insert_row(packed.at[m, local_page], key_value, offset)

        for page in range(pages_here):
            stores.append(
                pltpu.make_async_copy(
                    packed.at[m, page], pool_next.at[table[page, slot]], out_sems.at[m, page]
                )
            )
            stores[-1].start()
        prior = [
            jnp.concatenate([packed[m, pages_here + h, :, :NS], packed[m, pages_here + h, :, NS:]], axis=0)
            for h in range(heads)
        ]
        advance_state(m, prior, b_twice, drive, decay, made.at[m])
        stores.append(pltpu.make_async_copy(made.at[m], state_next.at[slot], out_sems.at[m, pages_here]))
        stores[-1].start()
    for store in stores:
        store.wait()


def shape(dims, dtype):
    return jax.ShapeDtypeStruct(tuple(dims), dtype)


def params():
    return pltpu.CompilerParams(vmem_limit_bytes=VMEM_LIMIT)


def cost(flops, moved):
    return pl.CostEstimate(flops=int(flops), bytes_accessed=int(moved), transcendentals=0)


def exchange(value, axis):
    return lax.all_to_all(value, axis, split_axis=0, concat_axis=0, tiled=True)


def local(
    tokens, arrival, cache_lengths, move_slot, move_target, page_table, kv_pool, ssm_state,
    conv_x, conv_bc, norm_gain, weight_z, weight_x, weight_dt, weight_bc, weight_qkv,
    conv_weight_x, conv_weight_bc, dt_bias, a_log, d_skip, weight_ssm_out, weight_attn_out,
):
    row_count = lax.axis_size("rows")
    col_count = lax.axis_size("cols")
    row_index = lax.axis_index("rows").astype(I32).reshape(1)
    col_index = lax.axis_index("cols").astype(I32).reshape(1)
    slots, heads = ssm_state.shape[0], ssm_state.shape[1]
    total, depth = tokens.shape
    moves = move_slot.shape[1]
    pages_here, width = page_table.shape[3], kv_pool.shape[3]
    inner = heads * HP
    stays = slots - moves
    cols, at = Columns(inner), Plan(slots, moves)
    table = page_table[0, 0].T
    pool = kv_pool[:, 0]
    past_x, past_bc = conv_x.transpose(1, 0, 2), conv_bc.transpose(1, 0, 2)
    rows = row_count * BLOCK
    model = depth * row_count
    share = QH * HD // col_count
    state_bytes = 2 * inner * NS
    page_bytes = 2 * pages_here * PAGE * width
    parcel = shape((pages_here + heads, PAGE, width), BF16)
    parcels_here = pltpu.VMEM((moves,) + parcel.shape, BF16)

    partial_sums, plan, *parcels = pl.pallas_call(
        functools.partial(project_kernel, slots=slots),
        out_shape=[shape((rows, cols.width), BF16), shape((at.size,), I32)] + [parcel] * (row_count - 1),
        in_specs=[SMEM_SPEC] * 6 + [VMEM_SPEC] * 7 + [ANY_SPEC] * 2,
        out_specs=[VMEM_SPEC, SMEM_SPEC] + [ANY_SPEC] * (row_count - 1),
        scratch_shapes=[
            pltpu.SMEM((total,), I32),
            pltpu.VMEM((total, depth), F32),
            pltpu.VMEM((rows, depth), F32),
            pltpu.VMEM((rows, LANES), F32),
            parcels_here,
            pltpu.SemaphoreType.DMA((moves, pages_here + 2)),
            pltpu.SemaphoreType.DMA((moves,)),
        ],
        compiler_params=params(),
        cost_estimate=cost(2 * rows * depth * cols.width, 8e6),
        name="project",
    )(
        row_index, arrival, cache_lengths, move_slot.T, move_target.T, table,
        tokens, norm_gain, weight_z, weight_x, weight_dt.T, weight_bc, weight_qkv, pool, ssm_state,
    )
    received = exchange(partial_sums, "rows")
    parcels = [
        lax.ppermute(sent, "rows", [(i, i ^ (d + 1)) for i in range(row_count)])
        for d, sent in enumerate(parcels)
    ]

    pool_next, partials_send, kv_new = pl.pallas_call(
        functools.partial(
            attend_kernel, moves=moves, heads=heads, row_count=row_count, col_count=col_count, width=model
        ),
        out_shape=(
            shape(pool.shape, BF16),
            shape((col_count * BLOCK, share + LANES), F32),
            shape((BLOCK, 2 * KVH * HD), F32),
        ),
        in_specs=[SMEM_SPEC] * 3 + [VMEM_SPEC, ANY_SPEC],
        out_specs=(ANY_SPEC, VMEM_SPEC, VMEM_SPEC),
        scratch_shapes=[
            pltpu.VMEM((slots, pages_here, PAGE, width), BF16),
            pltpu.VMEM((BLOCK * QH, HD), F32),
            pltpu.VMEM((BLOCK * QH, pages_here * PAGE), F32),
            pltpu.VMEM((BLOCK * QH, HD), F32),
            pltpu.VMEM((BLOCK * QH, HD), F32),
            pltpu.VMEM((BLOCK * QH, HD), F32),
            pltpu.SemaphoreType.DMA((slots, pages_here)),
            pltpu.SemaphoreType.DMA((stays, pages_here)),
        ],
        compiler_params=params(),
        cost_estimate=cost(4 * slots * 16 * pages_here * PAGE * 256, 4 * slots * page_bytes),
        name="attend",
    )(col_index, plan, table, received, pool)
    partials = exchange(partials_send, "cols")

    next_x, next_bc, state_next, gated, driven, decay, b_in = pl.pallas_call(
        functools.partial(mix_kernel, moves=moves, row_count=row_count, width=model),
        out_shape=(
            shape(past_x.shape, F32),
            shape(past_bc.shape, F32),
            shape(ssm_state.shape, BF16),
            shape((BLOCK, inner), F32),
            shape((BLOCK, inner), F32),
            shape((BLOCK, heads), F32),
            shape((BLOCK, NS), F32),
        ),
        in_specs=[SMEM_SPEC] + [VMEM_SPEC] * 8 + [ANY_SPEC],
        out_specs=(VMEM_SPEC, VMEM_SPEC, ANY_SPEC) + (VMEM_SPEC,) * 4,
        scratch_shapes=[
            pltpu.VMEM((BLOCK, inner), F32),
            pltpu.VMEM((slots, heads, HP, NS), BF16),
            pltpu.VMEM((stays, heads, HP, NS), BF16),
            pltpu.VMEM((inner, 2 * BLOCK), BF16),
            pltpu.VMEM((2 * BLOCK, NS), F32),
            pltpu.SemaphoreType.DMA((slots,)),
            pltpu.SemaphoreType.DMA((stays,)),
        ],
        compiler_params=params(),
        cost_estimate=cost(4 * slots * inner * NS * 32, 4 * slots * state_bytes),
        name="mix",
    )(plan, received, past_x, past_bc, conv_weight_x, conv_weight_bc, dt_bias, a_log, d_skip, ssm_state)

    note_width = max(inner, 2 * NS, 2 * KVH * HD, share)
    attended, notes_send = pl.pallas_call(
        functools.partial(merge_kernel, moves=moves, row_count=row_count, col_count=col_count),
        out_shape=(shape((BLOCK, share), F32), shape((rows, note_width), BF16)),
        in_specs=[SMEM_SPEC] + [VMEM_SPEC] * 8,
        out_specs=(VMEM_SPEC, VMEM_SPEC),
        scratch_shapes=[pltpu.VMEM((BLOCK, note_width), F32), pltpu.VMEM((BLOCK, share), F32)],
        compiler_params=params(),
        cost_estimate=cost(1e6, 1e6),
        name="merge",
    )(plan, partials, gated, kv_new, driven, decay, b_in, next_x, next_bc)
    notes = exchange(notes_send, "rows")

    mixed_send = pl.pallas_call(
        functools.partial(output_kernel, slots=slots, moves=moves, col_count=col_count),
        out_shape=shape((col_count * BLOCK, weight_ssm_out.shape[1] // col_count), F32),
        in_specs=[SMEM_SPEC] + [VMEM_SPEC] * 5,
        out_specs=VMEM_SPEC,
        scratch_shapes=[pltpu.VMEM((BLOCK, inner), F32), pltpu.VMEM((BLOCK, share), F32)],
        compiler_params=params(),
        cost_estimate=cost(2 * BLOCK * (inner + share) * weight_ssm_out.shape[1], 4e6),
        name="output",
    )(plan, gated, attended, notes, weight_ssm_out, weight_attn_out)
    mixed_parts = exchange(mixed_send, "cols")

    conv_x_next, conv_bc_next, state_next, pool_next = pl.pallas_call(
        functools.partial(arrive_kernel, moves=moves, row_count=row_count, col_count=col_count),
        out_shape=(
            shape(past_x.shape, BF16),
            shape(past_bc.shape, BF16),
            shape(ssm_state.shape, BF16),
            shape(pool.shape, BF16),
        ),
        in_specs=[SMEM_SPEC] * 4 + [VMEM_SPEC] * 3 + [ANY_SPEC] * (row_count + 1),
        out_specs=(VMEM_SPEC, VMEM_SPEC, ANY_SPEC, ANY_SPEC),
        scratch_shapes=[
            parcels_here,
            pltpu.VMEM((moves, heads, HP, NS), BF16),
            pltpu.VMEM((inner, 2 * BLOCK), BF16),
            pltpu.VMEM((BLOCK, heads), F32),
            pltpu.VMEM((2 * BLOCK, NS), F32),
            pltpu.VMEM((KW - 1, slots, inner), F32),
            pltpu.VMEM((KW - 1, slots, 2 * NS), F32),
            pltpu.SemaphoreType.DMA((moves,)),
            pltpu.SemaphoreType.DMA((moves, pages_here + 1)),
        ],
        input_output_aliases={7: 2, 8: 3},
        compiler_params=params(),
        cost_estimate=cost(1e6, 4 * moves * (state_bytes + page_bytes)),
        name="arrive",
    )(row_index, col_index, plan, table, notes, next_x, next_bc, state_next, pool_next, *parcels)

    mixed = pl.pallas_call(
        functools.partial(sum_kernel, col_count=col_count),
        out_shape=shape((slots, mixed_send.shape[1]), BF16),
        in_specs=[VMEM_SPEC],
        out_specs=VMEM_SPEC,
        compiler_params=params(),
        name="total",
    )(mixed_parts)
    return (
        mixed, state_next, conv_x_next.transpose(1, 0, 2), conv_bc_next.transpose(1, 0, 2), pool_next[:, None]
    )


def solution(mesh):
    in_specs = (
        P(None, "rows"),
        P(),
        P(),
        P(),
        P(),
        P("rows", "cols", None, None),
        P("rows", "cols", None, None),
        P("rows", "cols", None, None),
        P("rows", None, "cols"),
        P("rows", None, None),
        P("rows"),
        P("rows", "cols"),
        P("rows", "cols"),
        P("rows", "cols"),
        P("rows", None),
        P("rows", None),
        P(None, "cols"),
        P(),
        P("cols"),
        P("cols"),
        P("cols"),
        P("cols", None),
        P("cols", None),
    )
    out_specs = (
        P("rows", "cols"),
        P("rows", "cols", None, None),
        P("rows", None, "cols"),
        P("rows", None, None),
        P("rows", "cols", None, None),
    )
    return jax.shard_map(local, mesh=mesh, in_specs=in_specs, out_specs=out_specs, check_vma=False)
```

time: 135 us -> 88.4 us (0.65)
  blocking collectives: 58.9 us -> 11.7 us
  local copies, waits for them, and re-layouts: 34 us -> 3.23 us
  starting transfers between devices: 7.95 us -> 21.8 us
  Pallas kernels: 23.4 us -> 32.5 us
  waiting for transfers between devices: 8.83 us -> 17.7 us
    all_to_all x3 -> x1, blocking collectives: 58.9 us -> 11.7 us  [exchange(): return lax.all_to_all(value, axis, split_axis=0, concat_axis=0, tiled=True)]
    unnamed x91 -> x16, local copies, waits for them, and re-layouts: 32.6 us -> 3.23 us
    ppermute x0 -> x7, waiting for transfers between devices: none -> 17.6 us  [local(): lax.ppermute(sent, 'rows', [(i, i ^ d + 1) for i in range(row_count)])]
    pallas_call x3 -> x5, Pallas kernels: 17.6 us -> 27.9 us  [the longest x1 8.21 us: local(): pl.pallas_call(functools.partial(attend_kernel, moves=moves, heads=heads,...]
    all_to_all x2 -> x3, waiting for transfers between devices: 8.83 us -> 0.08 us  [exchange(): return lax.all_to_all(value, axis, split_axis=0, concat_axis=0, tiled=True)]
    all_to_all x2 -> x3, starting transfers between devices: 7.95 us -> 15 us  [exchange(): return lax.all_to_all(value, axis, split_axis=0, concat_axis=0, tiled=True)]
    ppermute x0 -> x7, starting transfers between devices: none -> 6.81 us  [local(): lax.ppermute(sent, 'rows', [(i, i ^ d + 1) for i in range(row_count)])]
  transfers between devices with their start and end apart: 2 -> 10, of which waited for: 2 -> 2; matrix products, arithmetic and copies ran while one was open for 1% -> 0% of each run, Pallas kernels for 10% -> 29%
where the time goes in v2:
time: 88.4 us; the launch traced here: 87.7 us
  Pallas kernels  32.5 us (37%)
  starting transfers between devices  21.8 us (25%)
  waiting for transfers between devices  17.7 us (20%)
  blocking collectives  11.7 us (13%)
  local copies, waits for them, and re-layouts  3.23 us (4%)
    ppermute x7, waiting for transfers between devices, local(): lax.ppermute(sent, 'rows', [(i, i ^ d + 1) for i in range(row_count)])  17.6 us
    all_to_all x3, starting transfers between devices, exchange(): return lax.all_to_all(value, axis, split_axis=0, concat_axis=0, tiled=True)  15 us
    all_to_all x1, blocking collectives, exchange(): return lax.all_to_all(value, axis, split_axis=0, concat_axis=0, tiled=True)  11.7 us
    pallas_call x1, Pallas kernels, local(): pl.pallas_call(functools.partial(attend_kernel, moves=moves, heads=heads,...  8.21 us
    pallas_call x1, Pallas kernels, local(): pl.pallas_call(functools.partial(mix_kernel, moves=moves, row_count=row_c...  7.11 us
    ppermute x7, starting transfers between devices, local(): lax.ppermute(sent, 'rows', [(i, i ^ d + 1) for i in range(row_count)])  6.81 us
    pallas_call x1, Pallas kernels, local(): pl.pallas_call(functools.partial(project_kernel, slots=slots), out_shape=...  5.79 us
    pallas_call x1, Pallas kernels, local(): pl.pallas_call(functools.partial(arrive_kernel, moves=moves, row_count=ro...  4.87 us
  transfers between devices with their start and end apart: 10, of which 2 were waited for; matrix products, arithmetic and copies ran while one was open for 0% of the time, Pallas kernels for 29%

profile of v2, /device:TPU:0, one launch (start us, length us, event | category | flops | bytes accessed | tf_op | source)
XLA Modules:
  0.0 87.7 jit_solution(1092204182485294364)
XLA Ops:
  0.6 5.8 %project.1 = (bf16[128,3328]{1,0:T(8,128)(2,1)}, s32[38]{0:T(128)}, bf16[16,32,512]{2,1,0:T(8,128)(2,1)}, bf16[16,32,512]{2,1,0:T(8,128)(2,1)}, bf16[16,32,512]{...) custom-call(s32[1]{0:T(128)} %bitcast.row_ref, ...), custom_call_target="tpu_custom_call" | custom-call | flops 218103808 | bytes 8000000 | tf_op jit(solution)/shard_map/project/pallas_call | solution.py:592
  6.4 5.2 %all-to-all-start = ((bf16[8,16,3328]{2,1,0:T(8,128)(2,1)}), bf16[8,16,3328]{2,1,0:T(8,128)(2,1)S(1)}, u32[]{:S(2)}, u32[]{:S(2)}) async-start(bf16[8,16,3328]{2,1,0:T(8,128)(2,1)} %bitcast.31), calls=%async_computation | async-start | bytes 1703936 | tf_op jit(solution)/shard_map/all_to_all | solution.py:562
  11.6 0.5 collective-permute-start
  12.1 1.7 %collective-permute-start.1 = (bf16[16,32,512]{2,1,0:T(8,128)(2,1)}, bf16[16,32,512]{2,1,0:T(8,128)(2,1)S(1)}, u32[]{:S(2)}, u32[]{:S(2)}) collective-permute-start(bf16[16,32,512]{2,1,0:T(8,128)(2,1)} %get-tuple-element.45), channel_id=1, source_target_pairs={{0,8},{4,12},{8,0},{12,4},{16,24},{20,28},{24,16},{28,20},{1,9},{5... | collective-permute-start | bytes 1572872 | tf_op jit(solution)/shard_map/ppermute | solution.py:615
  13.8 1.7 %collective-permute-start.3 = (bf16[16,32,512]{2,1,0:T(8,128)(2,1)}, bf16[16,32,512]{2,1,0:T(8,128)(2,1)S(1)}, u32[]{:S(2)}, u32[]{:S(2)}) collective-permute-start(bf16[16,32,512]{2,1,0:T(8,128)(2,1)} %get-tuple-element.47), channel_id=1, source_target_pairs={{0,16},{4,20},{8,24},{12,28},{16,0},{20,4},{24,8},{28,12},{1,17},{... | collective-permute-start | bytes 1572872 | tf_op jit(solution)/shard_map/ppermute | solution.py:615
  15.5 0.1 collective-permute-start.4
  15.6 2.6 %collective-permute-start.5 = (bf16[16,32,512]{2,1,0:T(8,128)(2,1)}, bf16[16,32,512]{2,1,0:T(8,128)(2,1)}, u32[]{:S(2)}, u32[]{:S(2)}) collective-permute-start(bf16[16,32,512]{2,1,0:T(8,128)(2,1)} %get-tuple-element.49), channel_id=1, source_target_pairs={{0,24},{4,28},{8,16},{12,20},{16,8},{20,12},{24,0},{28,4},{1,25},{... | collective-permute-start | bytes 1572872 | tf_op jit(solution)/shard_map/ppermute | solution.py:615
  18.2 17.6 %collective-permute-done.1.rest_1_ = bf16[16,32,512]{2,1,0:T(8,128)(2,1)S(1)} collective-permute-done((bf16[16,32,512]{2,1,0:T(8,128)(2,1)}, bf16[16,32,512]{2,1,0:T(8,128)(2,1)S(1)}, u32[]{:S(2)}, u32[]{:S(2)}) %collective-permute-start.1) | collective-permute-done | bytes 524320 | tf_op jit(solution)/shard_map/ppermute | solution.py:615
  35.8 0.2 collective-permute-start.6
  36.0 0.9 %copy-done = bf16[8,16,3328]{2,1,0:T(8,128)(2,1)} copy-done((bf16[8,16,3328]{2,1,0:T(8,128)(2,1)}, bf16[8,16,3328]{2,1,0:T(8,128)(2,1)S(1)}, u32[]{:S(2)}) %copy-start) | copy-done | bytes 851992
  36.9 8.2 %attend.1 = (bf16[104,32,512]{2,1,0:T(8,128)(2,1)}, f32[64,384]{1,0:T(8,128)}, f32[16,512]{1,0:T(8,128)}) custom-call(s32[1]{0:T(128)} %bitcast.11.col_ref, s32[38]{0:T(128)} %get-tuple-element.30.plan, s32[8,13]{1,0:T(8,128)} %bitcast.40, bf16[128,3328]{1,0:T(8,128)(2,1)} %bitcast.26, bf16[104,32,512]{2,1,0:T(8,128)(2,1)} %bitcast.25), custom_call_target="tpu_custom_call" | custom-call | flops 54525952 | bytes 13631488 | tf_op jit(solution)/shard_map/attend/pallas_call | solution.py:619
  45.2 4.9 %all-to-all-start.1 = ((f32[4,16,384]{2,1,0:T(8,128)}), f32[4,16,384]{2,1,0:T(8,128)S(1)}, u32[]{:S(2)}, u32[]{:S(2)}) async-start(f32[4,16,384]{2,1,0:T(8,128)} %bitcast.36), calls=%async_computation.1 | async-start | bytes 196608 | tf_op jit(solution)/shard_map/all_to_all | solution.py:562
  50.1 7.1 %mix.1 = (f32[3,13,512]{2,1,0:T(8,128)}, f32[3,13,512]{2,1,0:T(8,128)}, bf16[13,8,64,256]{3,2,1,0:T(8,128)(2,1)}, f32[16,512]{1,0:T(8,128)}, f32[16,512]{1,0:T(8...) custom-call(s32[38]{0:T(128)} %get-tuple-element.30.plan, bf16[128,3328]{1,0:T(8,128)(2,1)} %bitcast.27, ...), custom_call_target="tpu_custom_call" | custom-call | flops 218103808 | bytes 13631488 | tf_op jit(solution)/shard_map/mix/pallas_call | solution.py:646
  57.2 0.6 copy-done.7
  57.8 1.9 %merge.1 = (f32[16,256]{1,0:T(8,128)}, bf16[128,512]{1,0:T(8,128)(2,1)}) custom-call(s32[38]{0:T(128)} %get-tuple-element.30.plan, f32[64,384]{1,0:T(8,128)} %bitcast.34, f32[16,512]{1,0:T(8,128)} %get-tuple-element.32.gated, f32[16,512]{1,0:T(8,128)} %get-tuple-element.34.kv_new, f32[16,512]{1,0:T(8,128)} %get-tuple-element.35.driven, ...), custom_call_target="tpu_custom_call" | custom-call | flops 1000000 | bytes 1000000 | tf_op jit(solution)/shard_map/merge/pallas_call | solution.py:674
  59.7 11.7 %all_to_all.44 = bf16[8,16,512]{2,1,0:T(8,128)(2,1)} all-to-all(bf16[8,16,512]{2,1,0:T(8,128)(2,1)} %bitcast.35), channel_id=1, replica_groups=mesh['rows'=8,'cols'=4] {'rows'}, dimensions={0} | all-to-all | bytes 262144 | tf_op jit(solution)/shard_map/all_to_all | solution.py:562
  71.5 3.1 %output.1 = f32[64,512]{1,0:T(8,128)} custom-call(s32[38]{0:T(128)} %get-tuple-element.30.plan, f32[16,512]{1,0:T(8,128)} %get-tuple-element.32.gated, f32[16,256]{1,0:T(8,128)} %get-tuple-element.40.attended, bf16[128,512]{1,0:T(8,128)(2,1)} %bitcast.29, bf16[512,2048]{1,0:T(8,128)(2,1)} %w_ssm.1, bf16[256,2048]{1,0:T(8,128)(2,1)} %w_attn.1), custom_call_target="tpu_custom_call" | custom-call | flops 50331648 | bytes 4000000 | tf_op jit(solution)/shard_map/output/pallas_call | solution.py:686
  74.6 4.9 %all-to-all-start.3 = ((f32[4,16,512]{2,1,0:T(8,128)}), f32[4,16,512]{2,1,0:T(8,128)S(1)}, u32[]{:S(2)}, u32[]{:S(2)}) async-start(f32[4,16,512]{2,1,0:T(8,128)} %bitcast.32), calls=%async_computation.3 | async-start | bytes 262144 | tf_op jit(solution)/shard_map/all_to_all | solution.py:562
  79.6 0.7 copy-done.4
  80.3 0.2 copy-done.5
  80.4 0.2 copy-done.6
  80.6 4.9 %arrive.1 = (bf16[3,13,512]{2,1,0:T(8,128)(2,1)}, bf16[3,13,512]{2,1,0:T(8,128)(2,1)}, bf16[13,8,64,256]{3,2,1,0:T(8,128)(2,1)}, bf16[104,32,512]{2,1,0:T(8,128)(2,1)}) custom-call(s32[1]{0:T(128)} %bitcast.row_ref, s32[1]{0:T(128)} %bitcast.11.col_ref, s32[38]{0:T(128)} %get-tuple-element.30.plan, ...), custom_call_target="tpu_custom_call", output_to_operand_aliasing={{2}: (7, {}), {3}: (8, {})} | custom-call | flops 1000000 | bytes 8388608 | tf_op jit(solution)/shard_map/arrive/pallas_call | solution.py:698
  85.5 0.6 copy-done.1
  86.2 1.5 %total.1 = bf16[13,512]{1,0:T(8,128)(2,1)} custom-call(f32[64,512]{1,0:T(8,128)} %bitcast.33), custom_call_target="tpu_custom_call" | custom-call | tf_op jit(solution)/shard_map/total/pallas_call | solution.py:725
  (20 shorter events, 0.1 us)
Async XLA Ops:
  6.4 29.6 %all-to-all-start = ((bf16[8,16,3328]{2,1,0:T(8,128)(2,1)}), bf16[8,16,3328]{2,1,0:T(8,128)(2,1)S(1)}, u32[]{:S(2)}, u32[]{:S(2)}) async-start(bf16[8,16,3328]{2,1,0:T(8,128)(2,1)} %bitcast.31), calls=%async_computation | async-start | bytes 1703936 | tf_op jit(solution)/shard_map/all_to_all | solution.py:562
  11.6 4.0 %collective-permute-start = (bf16[16,32,512]{2,1,0:T(8,128)(2,1)}, bf16[16,32,512]{2,1,0:T(8,128)(2,1)S(1)}, u32[]{:S(2)}, u32[]{:S(2)}) collective-permute-start(bf16[16,32,512]{2,1,0:T(8,128)(2,1)} %get-tuple-element.44), channel_id=1, source_target_pairs={{0,4},{4,0},{8,12},{12,8},{16,20},{20,16},{24,28},{28,24},{1,5},{5... | collective-permute-start | bytes 1572872 | tf_op jit(solution)/shard_map/ppermute | solution.py:615
  12.1 23.6 %collective-permute-start.1 = (bf16[16,32,512]{2,1,0:T(8,128)(2,1)}, bf16[16,32,512]{2,1,0:T(8,128)(2,1)S(1)}, u32[]{:S(2)}, u32[]{:S(2)}) collective-permute-start(bf16[16,32,512]{2,1,0:T(8,128)(2,1)} %get-tuple-element.45), channel_id=1, source_target_pairs={{0,8},{4,12},{8,0},{12,4},{16,24},{20,28},{24,16},{28,20},{1,9},{5... | collective-permute-start | bytes 1572872 | tf_op jit(solution)/shard_map/ppermute | solution.py:615
  13.8 65.6 %collective-permute-start.2 = (bf16[16,32,512]{2,1,0:T(8,128)(2,1)}, bf16[16,32,512]{2,1,0:T(8,128)(2,1)S(1)}, u32[]{:S(2)}, u32[]{:S(2)}) collective-permute-start(bf16[16,32,512]{2,1,0:T(8,128)(2,1)} %get-tuple-element.46), channel_id=1, source_target_pairs={{0,12},{4,8},{8,4},{12,0},{16,28},{20,24},{24,20},{28,16},{1,13},{... | collective-permute-start | bytes 1572872 | tf_op jit(solution)/shard_map/ppermute | solution.py:615
  13.8 65.6 %collective-permute-start.3 = (bf16[16,32,512]{2,1,0:T(8,128)(2,1)}, bf16[16,32,512]{2,1,0:T(8,128)(2,1)S(1)}, u32[]{:S(2)}, u32[]{:S(2)}) collective-permute-start(bf16[16,32,512]{2,1,0:T(8,128)(2,1)} %get-tuple-element.47), channel_id=1, source_target_pairs={{0,16},{4,20},{8,24},{12,28},{16,0},{20,4},{24,8},{28,12},{1,17},{... | collective-permute-start | bytes 1572872 | tf_op jit(solution)/shard_map/ppermute | solution.py:615
  15.5 64.0 %collective-permute-start.4 = (bf16[16,32,512]{2,1,0:T(8,128)(2,1)}, bf16[16,32,512]{2,1,0:T(8,128)(2,1)S(1)}, u32[]{:S(2)}, u32[]{:S(2)}) collective-permute-start(bf16[16,32,512]{2,1,0:T(8,128)(2,1)} %get-tuple-element.48), channel_id=1, source_target_pairs={{0,20},{4,16},{8,28},{12,24},{16,4},{20,0},{24,12},{28,8},{1,21},{... | collective-permute-start | bytes 1572872 | tf_op jit(solution)/shard_map/ppermute | solution.py:615
  15.6 63.9 %copy-start.2 = (bf16[16,32,512]{2,1,0:T(8,128)(2,1)}, bf16[16,32,512]{2,1,0:T(8,128)(2,1)S(1)}, u32[]{:S(2)}) copy-start(bf16[16,32,512]{2,1,0:T(8,128)(2,1)S(1)} %collective-permute-done.rest_0_) | copy-start | bytes 1572868
  15.6 63.9 %collective-permute-start.5 = (bf16[16,32,512]{2,1,0:T(8,128)(2,1)}, bf16[16,32,512]{2,1,0:T(8,128)(2,1)}, u32[]{:S(2)}, u32[]{:S(2)}) collective-permute-start(bf16[16,32,512]{2,1,0:T(8,128)(2,1)} %get-tuple-element.49), channel_id=1, source_target_pairs={{0,24},{4,28},{8,16},{12,20},{16,8},{20,12},{24,0},{28,4},{1,25},{... | collective-permute-start | bytes 1572872 | tf_op jit(solution)/shard_map/ppermute | solution.py:615
  35.8 43.8 %copy-start.3 = (bf16[16,32,512]{2,1,0:T(8,128)(2,1)}, bf16[16,32,512]{2,1,0:T(8,128)(2,1)S(1)}, u32[]{:S(2)}) copy-start(bf16[16,32,512]{2,1,0:T(8,128)(2,1)S(1)} %collective-permute-done.1.rest_1_) | copy-start | bytes 1572868
  35.8 43.7 %collective-permute-start.6 = (bf16[16,32,512]{2,1,0:T(8,128)(2,1)}, bf16[16,32,512]{2,1,0:T(8,128)(2,1)}, u32[]{:S(2)}, u32[]{:S(2)}) collective-permute-start(bf16[16,32,512]{2,1,0:T(8,128)(2,1)} %get-tuple-element.50), channel_id=1, source_target_pairs={{0,28},{4,24},{8,20},{12,16},{16,12},{20,8},{24,4},{28,0},{1,29},{... | collective-permute-start | bytes 1572872 | tf_op jit(solution)/shard_map/ppermute | solution.py:615
  36.0 0.9 %copy-start = (bf16[8,16,3328]{2,1,0:T(8,128)(2,1)}, bf16[8,16,3328]{2,1,0:T(8,128)(2,1)S(1)}, u32[]{:S(2)}) copy-start(bf16[8,16,3328]{2,1,0:T(8,128)(2,1)S(1)} %all-to-all-done) | copy-start | bytes 2555908
  45.2 12.0 %all-to-all-start.1 = ((f32[4,16,384]{2,1,0:T(8,128)}), f32[4,16,384]{2,1,0:T(8,128)S(1)}, u32[]{:S(2)}, u32[]{:S(2)}) async-start(f32[4,16,384]{2,1,0:T(8,128)} %bitcast.36), calls=%async_computation.1 | async-start | bytes 196608 | tf_op jit(solution)/shard_map/all_to_all | solution.py:562
  57.2 0.6 copy-start.7
  74.6 10.9 %all-to-all-start.3 = ((f32[4,16,512]{2,1,0:T(8,128)}), f32[4,16,512]{2,1,0:T(8,128)S(1)}, u32[]{:S(2)}, u32[]{:S(2)}) async-start(f32[4,16,512]{2,1,0:T(8,128)} %bitcast.32), calls=%async_computation.3 | async-start | bytes 262144 | tf_op jit(solution)/shard_map/all_to_all | solution.py:562
  79.5 0.8 copy-start.4
  79.5 1.0 %copy-start.5 = (bf16[16,32,512]{2,1,0:T(8,128)(2,1)}, bf16[16,32,512]{2,1,0:T(8,128)(2,1)S(1)}, u32[]{:S(2)}) copy-start(bf16[16,32,512]{2,1,0:T(8,128)(2,1)S(1)} %collective-permute-done.3.rest_3_) | copy-start | bytes 1572868
  79.5 1.1 %copy-start.6 = (bf16[16,32,512]{2,1,0:T(8,128)(2,1)}, bf16[16,32,512]{2,1,0:T(8,128)(2,1)S(1)}, u32[]{:S(2)}) copy-start(bf16[16,32,512]{2,1,0:T(8,128)(2,1)S(1)} %collective-permute-done.4.rest_4_) | copy-start | bytes 1572868
  85.5 0.6 copy-start.1

commit v3 on v2

--- a/solution.py
+++ b/solution.py
@@ -65,9 +65,10 @@
     def __init__(self, slots, moves):
         self.length = 0
         self.slot = slots
-        self.target = self.slot + moves
-        self.source = self.target + moves
-        self.arrived_length = self.source + moves
+        self.away = self.slot + moves
+        self.source = self.away + moves
+        self.from_away = self.source + moves
+        self.arrived_length = self.from_away + moves
         self.stay = self.arrived_length + moves
         self.size = self.stay + slots - moves
 
@@ -80,7 +81,7 @@
 def project_kernel(
     row_ref, arrival, lengths, move_slot, move_target, table,
     tokens, gain, w_z, w_x, w_dt, w_bc, w_qkv, pool, state,
-    out, plan, *rest,
+    parcels, plan, *rest,
     slots,
 ):
     moves, row_count = move_slot.shape
@@ -88,8 +89,8 @@
     heads, depth = w_dt.shape
     inner = heads * HP
     cols, at = Columns(inner), Plan(slots, moves)
-    parcels = rest[: row_count - 1]
-    inverse, wide, picked, tail, packed, in_sems, out_sems = rest[row_count - 1 :]
+    outs = rest[:row_count]
+    inverse, wide, picked, tail, packed, in_sems, out_sems = rest[row_count:]
     me = row_ref[0]
 
     loads = []
@@ -120,36 +121,42 @@
 
     lax.fori_loop(0, row_count, invert, 0)
 
-    def pick(t, carry):
+    def pick(d, carry):
+        first = lax.bitwise_xor(me, d) * slots
         for s in range(slots):
-            picked[pl.ds(t * BLOCK + s, 1), :] = wide[pl.ds(inverse[t * slots + s], 1), :]
+            picked[pl.ds(d * BLOCK + s, 1), :] = wide[pl.ds(inverse[first + s], 1), :]
         return carry
 
     lax.fori_loop(0, row_count, pick, 0)
 
     for load in loads:
         load.wait()
-    for m in range(moves):
-        away = lax.bitwise_xor(move_target[m, me], me)
-        for d in range(1, row_count):
-
-            @pl.when(away == d)
-            def _(m=m, d=d):
-                pltpu.make_async_copy(packed.at[m], parcels[d - 1], out_sems.at[m]).start()
+    stores = [
+        pltpu.make_async_copy(packed.at[m], parcels.at[move_target[m, me]], out_sems.at[m])
+        for m in range(moves)
+    ]
+    for store in stores:
+        store.start()
 
     rows = picked[...]
     squares = jnp.sum(rows * rows, axis=1, keepdims=True)
     scaled = (rows * gain[...].astype(F32).reshape(1, depth)).astype(BF16)
-    out[:, cols.z : cols.x] = dot(scaled, w_z[...]).astype(BF16)
-    out[:, cols.x : cols.bc] = dot(scaled, w_x[...]).astype(BF16)
-    out[:, cols.bc : cols.q] = dot(scaled, w_bc[...]).astype(BF16)
-    out[:, cols.q : cols.tail] = dot(scaled, w_qkv[...]).astype(BF16)
+
+    def put(start, value):
+        value = value.astype(BF16)
+        for d, out in enumerate(outs):
+            out[:, start : start + value.shape[1]] = value[d * BLOCK : (d + 1) * BLOCK]
+
+    put(cols.z, dot(scaled, w_z[...]))
+    put(cols.x, dot(scaled, w_x[...]))
+    put(cols.bc, dot(scaled, w_bc[...]))
+    put(cols.q, dot(scaled, w_qkv[...]))
     tail[...] = jnp.zeros_like(tail)
     tail[:, :heads] = dot_t(scaled, w_dt[...])
     tail[:, heads : heads + 1] = squares
     high = tail[...].astype(BF16)
-    out[:, cols.tail : cols.tail + LANES] = high
-    out[:, cols.tail + LANES :] = (tail[...] - high.astype(F32)).astype(BF16)
+    put(cols.tail, high)
+    put(cols.tail + LANES, tail[...] - high.astype(F32))
 
     stays = 0
     for s in range(slots):
@@ -165,7 +172,7 @@
         stays = stays + jnp.where(leaves, 0, 1)
     for m in range(moves):
         plan[at.slot + m] = move_slot[m, me]
-        plan[at.target + m] = move_target[m, me]
+        plan[at.away + m] = lax.bitwise_xor(move_target[m, me], me)
 
     def seek(i, turn):
         for m in range(moves):
@@ -174,14 +181,15 @@
             @pl.when(comes)
             def _(m=m, turn=turn):
                 plan[at.source + turn] = i
+                plan[at.from_away + turn] = lax.bitwise_xor(i, me)
                 plan[at.arrived_length + turn] = lengths[i * slots + move_slot[m, i]]
 
             turn = turn + jnp.where(comes, 1, 0)
         return turn
 
     lax.fori_loop(0, row_count, seek, I32(0))
-    for m in range(moves):
-        pltpu.make_async_copy(packed.at[m], parcels[0], out_sems.at[m]).wait()
+    for store in stores:
+        store.wait()
 
 
 def widen(per_head, inner):
@@ -194,18 +202,15 @@
 
 
 class Sums:
-    def __init__(self, received, heads, row_count, width):
-        self.received, self.row_count = received, row_count
+    def __init__(self, received, heads, width):
+        self.received = received
         cols = Columns(heads * HP)
         tail = self.total(cols.tail, cols.tail + LANES) + self.total(cols.tail + LANES, cols.width)
         self.root = jnp.sqrt(tail[:, heads : heads + 1] / width + EPSILON)
         self.step_in = (tail[:, :heads] / self.root).astype(BF16).astype(F32)
 
     def total(self, start, stop):
-        result = self.received[0:BLOCK, start:stop].astype(F32)
-        for i in range(1, self.row_count):
-            result = result + self.received[i * BLOCK : (i + 1) * BLOCK, start:stop].astype(F32)
-        return result
+        return sum(part[:, start:stop].astype(F32) for part in self.received)
 
     def projected(self, start, stop):
         return (self.total(start, stop) / self.root).astype(BF16).astype(F32)
@@ -222,11 +227,12 @@
 
 
 def attend_kernel(
-    col_ref, plan, table, received, pool,
-    pool_next, send, kv_new,
-    pages, queries, scores, weighted, peaks, totals, in_sems, out_sems,
-    *, moves, heads, row_count, col_count, width,
+    col_ref, plan, table, pool, *rest, moves, heads, row_count, col_count, width
 ):
+    received = rest[:row_count]
+    pool_next, kv_new = rest[row_count : row_count + 2]
+    sends = rest[row_count + 2 : row_count + 2 + col_count]
+    pages, queries, scores, weighted, peaks, totals, in_sems, out_sems = rest[row_count + 2 + col_count :]
     pages_here, slots = table.shape
     cols, at = Columns(heads * HP), Plan(slots, moves)
     col = col_ref[0]
@@ -240,7 +246,7 @@
             )
             loads[-1].start()
 
-    sums = Sums(received, heads, row_count, width)
+    sums = Sums(received, heads, width)
     kv_new[...] = sums.projected(cols.kv, cols.tail)
     q_in = sums.projected(cols.q, cols.kv)
     for h in range(QH):
@@ -299,28 +305,29 @@
     share = QH * HD // col_count
     part = min(share, HD)
     lanes = lane_iota((BLOCK, LANES))
-    for c in range(col_count):
+    for d, send in enumerate(sends):
+        first = lax.bitwise_xor(col, d) * share
         stats = jnp.zeros((BLOCK, LANES), F32)
         for j in range(share // part):
-            head = (c * share + j * part) // HD
-            begin = (c * share + j * part) % HD
-            rows = pl.ds(head, BLOCK, stride=QH)
-            send[c * BLOCK : (c + 1) * BLOCK, j * part : (j + 1) * part] = weighted[rows, :][
-                :, begin : begin + part
-            ]
+            rows = pl.ds(lax.div(first + j * part, I32(HD)), BLOCK, stride=QH)
+            whole = weighted[rows, :]
+            piece = whole[:, :part]
+            for begin in range(part, HD, part):
+                piece = jnp.where(lax.rem(first, I32(HD)) == begin, whole[:, begin : begin + part], piece)
+            send[:, j * part : (j + 1) * part] = piece
             stats = jnp.where(lanes == 2 * j, peaks[rows, :], stats)
             stats = jnp.where(lanes == 2 * j + 1, totals[rows, :], stats)
-        send[c * BLOCK : (c + 1) * BLOCK, share:] = stats
+        send[:, share:] = stats
     for store in stores:
         store.wait()
 
 
 def mix_kernel(
-    plan, received, conv_x, conv_bc, cw_x, cw_bc, dt_bias, a_log, d_skip, state,
-    conv_x_next, conv_bc_next, state_next, gated, driven_out, decay, b_out,
-    readout, held, made, drive, b_twice, in_sems, out_sems,
-    *, moves, row_count, width,
+    plan, conv_x, conv_bc, cw_x, cw_bc, dt_bias, a_log, d_skip, state, *rest, moves, row_count, width
 ):
+    received = rest[:row_count]
+    conv_x_next, conv_bc_next, state_next, gated, driven_out, decay, b_out = rest[row_count : row_count + 7]
+    readout, held, made, drive, b_twice, in_sems, out_sems = rest[row_count + 7 :]
     slots, inner = conv_x.shape[1], conv_x.shape[2]
     heads = dt_bias.shape[0]
     cols, at = Columns(inner), Plan(slots, moves)
@@ -329,7 +336,7 @@
         loads.append(pltpu.make_async_copy(state.at[s], held.at[s], in_sems.at[s]))
         loads[-1].start()
 
-    sums = Sums(received, heads, row_count, width)
+    sums = Sums(received, heads, width)
 
     def convolved(past, taps, fresh, following):
         past_rows = [past[k].astype(F32) for k in range(KW - 1)]
@@ -358,14 +365,10 @@
 
     readout[...] = jnp.zeros_like(readout)
 
-    def read(s, carry):
-        pltpu.make_async_copy(state.at[s], held.at[s], in_sems.at[s]).wait()
+    for s in range(slots):
+        loads[s].wait()
         value = dot_t(c_out, held[s].reshape(inner, NS))
-        readout[...] = jnp.where(row_iota(value.shape) == s, value, readout[...])
-        return carry
-
-    for s in range(slots):
-        read(s, 0)
+        readout[s : s + 1, :] = value[s : s + 1]
 
     stores = []
     for j in range(slots - moves):
@@ -396,18 +399,17 @@
 
 
 def merge_kernel(
-    plan, partials, gated, kv_new, driven, decay, b_in, conv_x, conv_bc,
-    attended, send,
-    block, attended_wide,
-    *, moves, row_count, col_count,
+    plan, gated, kv_new, driven, decay, b_in, conv_x, conv_bc, *rest, moves, row_count, col_count
 ):
+    partials, attended = rest[:col_count], rest[col_count]
+    sends, block = rest[col_count + 1 : -1], rest[-1]
     slots, inner = conv_x.shape[1], conv_x.shape[2]
     heads, share = decay.shape[1], attended.shape[1]
     at = Plan(slots, moves)
     part = min(share, HD)
     pieces = []
     for j in range(share // part):
-        blocks = [partials[c * BLOCK : (c + 1) * BLOCK, :] for c in range(col_count)]
+        blocks = [partial[...] for partial in partials]
         peaks = [b[:, share + 2 * j : share + 2 * j + 1] for b in blocks]
         joint = functools.reduce(jnp.maximum, peaks)
         factors = [jnp.exp(p - joint) for p in peaks]
@@ -440,54 +442,62 @@
             put(Note.conv_x + k, conv_x[k, row, :])
             put(Note.conv_bc + k, conv_bc[k, row, :])
         put(Note.attended, attended[row, :])
-        start = pl.multiple_of(plan[at.target + m] * BLOCK, BLOCK)
-        send[pl.ds(start, BLOCK), :] = block[...].astype(BF16)
-
-
-def output_kernel(plan, gated, attended, notes, w_ssm, w_attn, send, gated_here, attended_here, *, slots, moves, col_count):
+        for d, send in enumerate(sends, 1):
+
+            @pl.when(plan[at.away + m] == d)
+            def _(send=send):
+                send[...] = block[...].astype(BF16)
+
+
+def pick_note(plan, at, m, notes, note):
+    for d, sent in enumerate(notes, 1):
+
+        @pl.when(plan[at.from_away + m] == d)
+        def _(sent=sent):
+            note[...] = sent[...].astype(F32)
+
+
+def output_kernel(col_ref, plan, gated, attended, w_ssm, w_attn, *rest, slots, moves, row_count, col_count):
+    notes, sends = rest[: row_count - 1], rest[row_count - 1 : row_count - 1 + col_count]
+    gated_here, attended_here, note = rest[row_count - 1 + col_count :]
     at = Plan(slots, moves)
     inner, share = gated.shape[1], attended.shape[1]
     gated_here[...] = gated[...]
     attended_here[...] = attended[...]
     for m in range(moves):
-        start = pl.multiple_of(plan[at.source + m] * BLOCK, BLOCK)
-        note = notes[pl.ds(start, BLOCK), :].astype(F32)
+        pick_note(plan, at, m, notes, note)
         row = pl.ds(plan[at.slot + m], 1)
         gated_here[row, :] = note[Note.gated : Note.gated + 1, :inner]
         attended_here[row, :] = note[Note.attended : Note.attended + 1, :share]
     columns = w_ssm.shape[1] // col_count
     left, right = gated_here[...].astype(BF16), attended_here[...].astype(BF16)
-    for c in range(col_count):
-        span = slice(c * columns, (c + 1) * columns)
-        send[c * BLOCK : (c + 1) * BLOCK, :] = dot(left, w_ssm[:, span]) + dot(right, w_attn[:, span])
-
-
-def sum_kernel(received, out, *, col_count):
-    total = received[0:BLOCK, :]
-    for c in range(1, col_count):
-        total = total + received[c * BLOCK : (c + 1) * BLOCK, :]
-    out[...] = total[: out.shape[0]].astype(BF16)
+    for d, send in enumerate(sends):
+        first = pl.multiple_of(lax.bitwise_xor(col_ref[0], d) * columns, columns)
+        span = pl.ds(first, columns)
+        send[...] = dot(left, w_ssm[:, span]) + dot(right, w_attn[:, span])
+
+
+def sum_kernel(*refs):
+    parts, out = refs[:-1], refs[-1]
+    out[...] = sum(part[...] for part in parts)[: out.shape[0]].astype(BF16)
 
 
 def arrive_kernel(
-    row_ref, col_ref, plan, table, notes, conv_x, conv_bc, state_in, pool_in, *rest, moves, row_count, col_count
+    col_ref, plan, table, conv_x, conv_bc, state_in, pool_in, parcels, *rest, moves, row_count, col_count
 ):
     del state_in, pool_in
+    notes, rest = rest[: row_count - 1], rest[row_count - 1 :]
     pages_here, slots = table.shape
     inner = conv_x.shape[2]
     heads = inner // HP
     at = Plan(slots, moves)
-    parcels = rest[: row_count - 1]
-    conv_x_next, conv_bc_next, state_next, pool_next = rest[row_count - 1 : row_count + 3]
-    packed, made, drive, decay, b_twice, window_x, window_bc, in_sems, out_sems = rest[row_count + 3 :]
-    me, col = row_ref[0], col_ref[0]
+    conv_x_next, conv_bc_next, state_next, pool_next = rest[:4]
+    packed, made, drive, decay, b_twice, window_x, window_bc, picked, in_sems, out_sems = rest[4:]
+    col = col_ref[0]
+    loads = []
     for m in range(moves):
-        away = lax.bitwise_xor(plan[at.source + m], me)
-        for d in range(1, row_count):
-
-            @pl.when(away == d)
-            def _(m=m, d=d):
-                pltpu.make_async_copy(parcels[d - 1], packed.at[m], in_sems.at[m]).start()
+        loads.append(pltpu.make_async_copy(parcels.at[plan[at.source + m]], packed.at[m], in_sems.at[m]))
+        loads[-1].start()
 
     for k in range(KW - 1):
         window_x[k] = conv_x[k]
@@ -496,8 +506,8 @@
     b_twice[...] = jnp.zeros_like(b_twice)
     half = b_twice.shape[0] // 2
     for m in range(moves):
-        start = pl.multiple_of(plan[at.source + m] * BLOCK, BLOCK)
-        note = notes[pl.ds(start, BLOCK), :].astype(F32)
+        pick_note(plan, at, m, notes, picked)
+        note = picked[...]
         rows.append(note)
         row = pl.ds(plan[at.slot + m], 1)
         for k in range(KW - 1):
@@ -520,7 +530,7 @@
     stores = []
     for m in range(moves):
         slot = plan[at.slot + m]
-        pltpu.make_async_copy(parcels[0], packed.at[m], in_sems.at[m]).wait()
+        loads[m].wait()
         owner, local_page, offset = place_of(plan[at.arrived_length + m], col_count)
         key_value = rows[m][Note.key_value : Note.key_value + 1, : 2 * KVH * HD]
 
@@ -550,8 +560,8 @@
     return jax.ShapeDtypeStruct(tuple(dims), dtype)
 
 
-def params():
-    return pltpu.CompilerParams(vmem_limit_bytes=VMEM_LIMIT)
+def params(limit=VMEM_LIMIT):
+    return pltpu.CompilerParams(vmem_limit_bytes=limit)
 
 
 def cost(flops, moved):
@@ -560,6 +570,14 @@
 
 def exchange(value, axis):
     return lax.all_to_all(value, axis, split_axis=0, concat_axis=0, tiled=True)
+
+
+def trade(blocks, axis, first=0):
+    count = lax.axis_size(axis)
+    return [
+        block if d == 0 else lax.ppermute(block, axis, [(i, i ^ d) for i in range(count)])
+        for d, block in enumerate(blocks, first)
+    ]
 
 
 def local(
@@ -586,14 +604,15 @@
     share = QH * HD // col_count
     state_bytes = 2 * inner * NS
     page_bytes = 2 * pages_here * PAGE * width
-    parcel = shape((pages_here + heads, PAGE, width), BF16)
-    parcels_here = pltpu.VMEM((moves,) + parcel.shape, BF16)
-
-    partial_sums, plan, *parcels = pl.pallas_call(
+    parcel = (pages_here + heads, PAGE, width)
+    parcels_here = pltpu.VMEM((moves,) + parcel, BF16)
+
+    parcels, plan, *partial_sums = pl.pallas_call(
         functools.partial(project_kernel, slots=slots),
-        out_shape=[shape((rows, cols.width), BF16), shape((at.size,), I32)] + [parcel] * (row_count - 1),
+        out_shape=[shape((row_count,) + parcel, BF16), shape((at.size,), I32)]
+        + [shape((BLOCK, cols.width), BF16)] * row_count,
         in_specs=[SMEM_SPEC] * 6 + [VMEM_SPEC] * 7 + [ANY_SPEC] * 2,
-        out_specs=[VMEM_SPEC, SMEM_SPEC] + [ANY_SPEC] * (row_count - 1),
+        out_specs=[ANY_SPEC, SMEM_SPEC] + [VMEM_SPEC] * row_count,
         scratch_shapes=[
             pltpu.SMEM((total,), I32),
             pltpu.VMEM((total, depth), F32),
@@ -610,23 +629,17 @@
         row_index, arrival, cache_lengths, move_slot.T, move_target.T, table,
         tokens, norm_gain, weight_z, weight_x, weight_dt.T, weight_bc, weight_qkv, pool, ssm_state,
     )
-    received = exchange(partial_sums, "rows")
-    parcels = [
-        lax.ppermute(sent, "rows", [(i, i ^ (d + 1)) for i in range(row_count)])
-        for d, sent in enumerate(parcels)
-    ]
-
-    pool_next, partials_send, kv_new = pl.pallas_call(
+    received = trade(partial_sums, "rows")
+    parcels = exchange(parcels, "rows")
+
+    pool_next, kv_new, *partials = pl.pallas_call(
         functools.partial(
             attend_kernel, moves=moves, heads=heads, row_count=row_count, col_count=col_count, width=model
         ),
-        out_shape=(
-            shape(pool.shape, BF16),
-            shape((col_count * BLOCK, share + LANES), F32),
-            shape((BLOCK, 2 * KVH * HD), F32),
-        ),
-        in_specs=[SMEM_SPEC] * 3 + [VMEM_SPEC, ANY_SPEC],
-        out_specs=(ANY_SPEC, VMEM_SPEC, VMEM_SPEC),
+        out_shape=[shape(pool.shape, BF16), shape((BLOCK, 2 * KVH * HD), F32)]
+        + [shape((BLOCK, share + LANES), F32)] * col_count,
+        in_specs=[SMEM_SPEC] * 3 + [ANY_SPEC] + [VMEM_SPEC] * row_count,
+        out_specs=[ANY_SPEC] + [VMEM_SPEC] * (1 + col_count),
         scratch_shapes=[
             pltpu.VMEM((slots, pages_here, PAGE, width), BF16),
             pltpu.VMEM((BLOCK * QH, HD), F32),
@@ -640,8 +653,8 @@
         compiler_params=params(),
         cost_estimate=cost(4 * slots * 16 * pages_here * PAGE * 256, 4 * slots * page_bytes),
         name="attend",
-    )(col_index, plan, table, received, pool)
-    partials = exchange(partials_send, "cols")
+    )(col_index, plan, table, pool, *received)
+    partials = trade(partials, "cols")
 
     next_x, next_bc, state_next, gated, driven, decay, b_in = pl.pallas_call(
         functools.partial(mix_kernel, moves=moves, row_count=row_count, width=model),
@@ -654,7 +667,7 @@
             shape((BLOCK, heads), F32),
             shape((BLOCK, NS), F32),
         ),
-        in_specs=[SMEM_SPEC] + [VMEM_SPEC] * 8 + [ANY_SPEC],
+        in_specs=[SMEM_SPEC] + [VMEM_SPEC] * 7 + [ANY_SPEC] + [VMEM_SPEC] * row_count,
         out_specs=(VMEM_SPEC, VMEM_SPEC, ANY_SPEC) + (VMEM_SPEC,) * 4,
         scratch_shapes=[
             pltpu.VMEM((BLOCK, inner), F32),
@@ -668,32 +681,37 @@
         compiler_params=params(),
         cost_estimate=cost(4 * slots * inner * NS * 32, 4 * slots * state_bytes),
         name="mix",
-    )(plan, received, past_x, past_bc, conv_weight_x, conv_weight_bc, dt_bias, a_log, d_skip, ssm_state)
-
-    note_width = max(inner, 2 * NS, 2 * KVH * HD, share)
-    attended, notes_send = pl.pallas_call(
+    )(plan, past_x, past_bc, conv_weight_x, conv_weight_bc, dt_bias, a_log, d_skip, ssm_state, *received)
+
+    note = (BLOCK, max(inner, 2 * NS, 2 * KVH * HD, share))
+    attended, *notes = pl.pallas_call(
         functools.partial(merge_kernel, moves=moves, row_count=row_count, col_count=col_count),
-        out_shape=(shape((BLOCK, share), F32), shape((rows, note_width), BF16)),
-        in_specs=[SMEM_SPEC] + [VMEM_SPEC] * 8,
-        out_specs=(VMEM_SPEC, VMEM_SPEC),
-        scratch_shapes=[pltpu.VMEM((BLOCK, note_width), F32), pltpu.VMEM((BLOCK, share), F32)],
+        out_shape=[shape((BLOCK, share), F32)] + [shape(note, BF16)] * (row_count - 1),
+        in_specs=[SMEM_SPEC] + [VMEM_SPEC] * (7 + col_count),
+        out_specs=[VMEM_SPEC] * row_count,
+        scratch_shapes=[pltpu.VMEM(note, F32)],
         compiler_params=params(),
         cost_estimate=cost(1e6, 1e6),
         name="merge",
-    )(plan, partials, gated, kv_new, driven, decay, b_in, next_x, next_bc)
-    notes = exchange(notes_send, "rows")
-
-    mixed_send = pl.pallas_call(
-        functools.partial(output_kernel, slots=slots, moves=moves, col_count=col_count),
-        out_shape=shape((col_count * BLOCK, weight_ssm_out.shape[1] // col_count), F32),
-        in_specs=[SMEM_SPEC] + [VMEM_SPEC] * 5,
-        out_specs=VMEM_SPEC,
-        scratch_shapes=[pltpu.VMEM((BLOCK, inner), F32), pltpu.VMEM((BLOCK, share), F32)],
+    )(plan, gated, kv_new, driven, decay, b_in, next_x, next_bc, *partials)
+    notes = trade(notes, "rows", 1)
+
+    columns = weight_ssm_out.shape[1] // col_count
+    terms = pl.pallas_call(
+        functools.partial(
+            output_kernel, slots=slots, moves=moves, row_count=row_count, col_count=col_count
+        ),
+        out_shape=[shape((BLOCK, columns), F32)] * col_count,
+        in_specs=[SMEM_SPEC] * 2 + [VMEM_SPEC] * (4 + row_count - 1),
+        out_specs=[VMEM_SPEC] * col_count,
+        scratch_shapes=[
+            pltpu.VMEM((BLOCK, inner), F32), pltpu.VMEM((BLOCK, share), F32), pltpu.VMEM(note, F32)
+        ],
         compiler_params=params(),
         cost_estimate=cost(2 * BLOCK * (inner + share) * weight_ssm_out.shape[1], 4e6),
         name="output",
-    )(plan, gated, attended, notes, weight_ssm_out, weight_attn_out)
-    mixed_parts = exchange(mixed_send, "cols")
+    )(col_index, plan, gated, attended, weight_ssm_out, weight_attn_out, *notes)
+    terms = trade(terms, "cols")
 
     conv_x_next, conv_bc_next, state_next, pool_next = pl.pallas_call(
         functools.partial(arrive_kernel, moves=moves, row_count=row_count, col_count=col_count),
@@ -703,7 +721,7 @@
             shape(ssm_state.shape, BF16),
             shape(pool.shape, BF16),
         ),
-        in_specs=[SMEM_SPEC] * 4 + [VMEM_SPEC] * 3 + [ANY_SPEC] * (row_count + 1),
+        in_specs=[SMEM_SPEC] * 3 + [VMEM_SPEC] * 2 + [ANY_SPEC] * 3 + [VMEM_SPEC] * (row_count - 1),
         out_specs=(VMEM_SPEC, VMEM_SPEC, ANY_SPEC, ANY_SPEC),
         scratch_shapes=[
             parcels_here,
@@ -713,23 +731,24 @@
             pltpu.VMEM((2 * BLOCK, NS), F32),
             pltpu.VMEM((KW - 1, slots, inner), F32),
             pltpu.VMEM((KW - 1, slots, 2 * NS), F32),
+            pltpu.VMEM(note, F32),
             pltpu.SemaphoreType.DMA((moves,)),
             pltpu.SemaphoreType.DMA((moves, pages_here + 1)),
         ],
-        input_output_aliases={7: 2, 8: 3},
+        input_output_aliases={5: 2, 6: 3},
         compiler_params=params(),
         cost_estimate=cost(1e6, 4 * moves * (state_bytes + page_bytes)),
         name="arrive",
-    )(row_index, col_index, plan, table, notes, next_x, next_bc, state_next, pool_next, *parcels)
+    )(col_index, plan, table, next_x, next_bc, state_next, pool_next, parcels, *notes)
 
     mixed = pl.pallas_call(
-        functools.partial(sum_kernel, col_count=col_count),
-        out_shape=shape((slots, mixed_send.shape[1]), BF16),
-        in_specs=[VMEM_SPEC],
+        sum_kernel,
+        out_shape=shape((slots, columns), BF16),
+        in_specs=[VMEM_SPEC] * col_count,
         out_specs=VMEM_SPEC,
         compiler_params=params(),
         name="total",
-    )(mixed_parts)
+    )(*terms)
     return (
         mixed, state_next, conv_x_next.transpose(1, 0, 2), conv_bc_next.transpose(1, 0, 2), pool_next[:, None]
     )

time: 88.4 us -> 124 us (1.40)
  waiting for transfers between devices: 17.7 us -> 58.8 us
  blocking collectives: 11.7 us -> 0 us
  starting transfers between devices: 21.8 us -> 28.2 us
    ppermute x7 -> x20, waiting for transfers between devices: 17.6 us -> 58.8 us  [trade(): lax.ppermute(block, axis, [(i, i ^ d) for i in range(count)])]
    ppermute x7 -> x20, starting transfers between devices: 6.81 us -> 22.8 us  [trade(): lax.ppermute(block, axis, [(i, i ^ d) for i in range(count)])]
    all_to_all x1 -> x0, blocking collectives: 11.7 us -> none  [exchange(): return lax.all_to_all(value, axis, split_axis=0, concat_axis=0, tiled=True)]
    all_to_all x3 -> x1, starting transfers between devices: 15 us -> 5.36 us  [exchange(): return lax.all_to_all(value, axis, split_axis=0, concat_axis=0, tiled=True)]
    unnamed x16 -> x54, local copies, waits for them, and re-layouts: 3.23 us -> 2.46 us
  transfers between devices with their start and end apart: 10 -> 21, of which waited for: 2 -> 8; matrix products, arithmetic and copies ran while one was open for 0% -> 0% of each run, Pallas kernels for 29% -> 18%
where the time goes in v3:
time: 124 us
  waiting for transfers between devices  58.8 us (47%)
  Pallas kernels  33.2 us (27%)
  starting transfers between devices  28.2 us (23%)
  local copies, waits for them, and re-layouts  2.46 us (2%)
    ppermute x20, waiting for transfers between devices, trade(): lax.ppermute(block, axis, [(i, i ^ d) for i in range(count)])  58.8 us
    ppermute x20, starting transfers between devices, trade(): lax.ppermute(block, axis, [(i, i ^ d) for i in range(count)])  22.8 us
    pallas_call x1, Pallas kernels, local(): pl.pallas_call(functools.partial(attend_kernel, moves=moves, heads=heads,...  8.38 us
    pallas_call x1, Pallas kernels, local(): pl.pallas_call(functools.partial(mix_kernel, moves=moves, row_count=row_c...  7.25 us
    pallas_call x1, Pallas kernels, local(): pl.pallas_call(functools.partial(project_kernel, slots=slots), out_shape=...  5.8 us
    all_to_all x1, starting transfers between devices, exchange(): return lax.all_to_all(value, axis, split_axis=0, concat_axis=0, tiled=True)  5.36 us
    pallas_call x1, Pallas kernels, local(): pl.pallas_call(functools.partial(arrive_kernel, moves=moves, row_count=ro...  4.84 us
    pallas_call x1, Pallas kernels, local(): pl.pallas_call(functools.partial(output_kernel, slots=slots, moves=moves,...  3.39 us
  transfers between devices with their start and end apart: 21, of which 8 were waited for; matrix products, arithmetic and copies ran while one was open for 0% of the time, Pallas kernels for 18%

profile of v3, /device:TPU:0, one launch (start us, length us, event | category | flops | bytes accessed | tf_op | source)
XLA Modules:
  0.0 123.6 jit_solution(5167942073291446586)
XLA Ops:
  0.6 5.8 %project.1 = (bf16[8,16,32,512]{3,2,1,0:T(8,128)(2,1)}, s32[42]{0:T(128)}, bf16[16,3328]{1,0:T(8,128)(2,1)}, bf16[16,3328]{1,0:T(8,128)(2,1)}, bf16[16,3328]{1,0...) custom-call(s32[1]{0:T(128)} %bitcast.1.row_ref, ...), custom_call_target="tpu_custom_call" | custom-call | flops 218103808 | bytes 8000000 | tf_op jit(solution)/shard_map/project/pallas_call | solution.py:610
  6.5 5.4 %all-to-all-start = ((bf16[8,16,32,512]{3,2,1,0:T(8,128)(2,1)}), bf16[8,16,32,512]{3,2,1,0:T(8,128)(2,1)}, u32[]{:S(2)}, u32[]{:S(2)}) async-start(bf16[8,16,32,512]{3,2,1,0:T(8,128)(2,1)} %get-tuple-element.78), calls=%async_computation | async-start | bytes 8388608 | tf_op jit(solution)/shard_map/all_to_all | solution.py:572
  12.4 1.9 %collective-permute-start.1 = (bf16[16,3328]{1,0:T(8,128)(2,1)S(1)}, bf16[16,3328]{1,0:T(8,128)(2,1)S(1)}, u32[]{:S(2)}, u32[]{:S(2)}) collective-permute-start(bf16[16,3328]{1,0:T(8,128)(2,1)S(1)} %copy-done.25), channel_id=1, source_target_pairs={{0,8},{4,12},{8,0},{12,4},{16,24},{20,28},{24,16},{28,20},{1,9},{5... | collective-permute-start | bytes 319496 | tf_op jit(solution)/shard_map/ppermute | solution.py:578
  14.4 1.7 %collective-permute-start.3 = (bf16[16,3328]{1,0:T(8,128)(2,1)S(1)}, bf16[16,3328]{1,0:T(8,128)(2,1)S(1)}, u32[]{:S(2)}, u32[]{:S(2)}) collective-permute-start(bf16[16,3328]{1,0:T(8,128)(2,1)S(1)} %copy-done.23), channel_id=1, source_target_pairs={{0,16},{4,20},{8,24},{12,28},{16,0},{20,4},{24,8},{28,12},{1,17},{... | collective-permute-start | bytes 319496 | tf_op jit(solution)/shard_map/ppermute | solution.py:578
  16.2 2.7 %collective-permute-start.5 = (bf16[16,3328]{1,0:T(8,128)(2,1)S(1)}, bf16[16,3328]{1,0:T(8,128)(2,1)S(1)}, u32[]{:S(2)}, u32[]{:S(2)}) collective-permute-start(bf16[16,3328]{1,0:T(8,128)(2,1)S(1)} %copy-done.21), channel_id=1, source_target_pairs={{0,24},{4,28},{8,16},{12,20},{16,8},{20,12},{24,0},{28,4},{1,25},{... | collective-permute-start | bytes 319496 | tf_op jit(solution)/shard_map/ppermute | solution.py:578
  18.9 44.2 %collective-permute-done.1.rest_2_ = bf16[16,3328]{1,0:T(8,128)(2,1)S(1)} collective-permute-done((bf16[16,3328]{1,0:T(8,128)(2,1)S(1)}, bf16[16,3328]{1,0:T(8,128)(2,1)S(1)}, u32[]{:S(2)}, u32[]{:S(2)}) %collective-permute-start.1) | collective-permute-done | bytes 106528 | tf_op jit(solution)/shard_map/ppermute | solution.py:578
  63.1 0.9 collective-permute-done.2.rest_3_
  64.1 4.6 %collective-permute-done.5.rest_6_ = bf16[16,3328]{1,0:T(8,128)(2,1)S(1)} collective-permute-done((bf16[16,3328]{1,0:T(8,128)(2,1)S(1)}, bf16[16,3328]{1,0:T(8,128)(2,1)S(1)}, u32[]{:S(2)}, u32[]{:S(2)}) %collective-permute-start.5) | collective-permute-done | bytes 106528 | tf_op jit(solution)/shard_map/ppermute | solution.py:578
  70.1 8.4 %attend.1 = (bf16[104,32,512]{2,1,0:T(8,128)(2,1)}, f32[16,512]{1,0:T(8,128)}, f32[16,384]{1,0:T(8,128)}, f32[16,384]{1,0:T(8,128)}, f32[16,384]{1,0:T(8,128)}, /*index=5*/f32[16,384]{1,0:T(8,128)}) custom-call(s32[1]{0:T(128)} %bitcast.col_ref, s32[42]{0:T(128)} %get-tuple-element.44.plan, s32[8,13]{1,0:T(8,128)} %bitcast.22, ...), custom_call_target="tpu_custom_call" | custom-call | flops 54525952 | bytes 13631488 | tf_op jit(solution)/shard_map/attend/pallas_call | solution.py:635
  78.5 2.6 %collective-permute-start.7 = (f32[16,384]{1,0:T(8,128)}, f32[16,384]{1,0:T(8,128)S(1)}, u32[]{:S(2)}, u32[]{:S(2)}) collective-permute-start(f32[16,384]{1,0:T(8,128)} %get-tuple-element.61), channel_id=1, source_target_pairs={{0,1},{1,0},{2,3},{3,2},{4,5},{5,4},{6,7},{7,6},{8,9},{9,8},{10,11... | collective-permute-start | bytes 73736 | tf_op jit(solution)/shard_map/ppermute | solution.py:578
  81.0 2.6 %collective-permute-start.8 = (f32[16,384]{1,0:T(8,128)}, f32[16,384]{1,0:T(8,128)S(1)}, u32[]{:S(2)}, u32[]{:S(2)}) collective-permute-start(f32[16,384]{1,0:T(8,128)} %get-tuple-element.62), channel_id=1, source_target_pairs={{0,2},{1,3},{2,0},{3,1},{4,6},{5,7},{6,4},{7,5},{8,10},{9,11},{10,... | collective-permute-start | bytes 73736 | tf_op jit(solution)/shard_map/ppermute | solution.py:578
  83.6 7.2 %mix.1 = (f32[3,13,512]{2,1,0:T(8,128)}, f32[3,13,512]{2,1,0:T(8,128)}, bf16[13,8,64,256]{3,2,1,0:T(8,128)(2,1)}, f32[16,512]{1,0:T(8,128)}, f32[16,512]{1,0:T(8...) custom-call(s32[42]{0:T(128)} %get-tuple-element.44.plan, bf16[3,13,512]{2,1,0:T(8,128)(2,1)} %bitcast.19, ...), custom_call_target="tpu_custom_call" | custom-call | flops 218103808 | bytes 13631488 | tf_op jit(solution)/shard_map/mix/pallas_call | solution.py:659
  91.6 2.1 %merge.1 = (f32[16,256]{1,0:T(8,128)}, bf16[16,512]{1,0:T(8,128)(2,1)}, bf16[16,512]{1,0:T(8,128)(2,1)}, bf16[16,512]{1,0:T(8,128)(2,1)}, bf16[16,512]{1,0:T(8,1...) custom-call(s32[42]{0:T(128)} %get-tuple-element.44.plan, ...), custom_call_target="tpu_custom_call" | custom-call | flops 1000000 | bytes 1000000 | tf_op jit(solution)/shard_map/merge/pallas_call | solution.py:687
  94.4 1.2 %collective-permute-start.12 = (bf16[16,512]{1,0:T(8,128)(2,1)}, bf16[16,512]{1,0:T(8,128)(2,1)S(1)}, u32[]{:S(2)}, u32[]{:S(2)}) collective-permute-start(bf16[16,512]{1,0:T(8,128)(2,1)} %get-tuple-element.67), channel_id=1, source_target_pairs={{0,12},{4,8},{8,4},{12,0},{16,28},{20,24},{24,20},{28,16},{1,13},{... | collective-permute-start | bytes 49160 | tf_op jit(solution)/shard_map/ppermute | solution.py:578
  95.6 0.9 collective-permute-start.13
  98.1 1.9 %collective-permute-start.16 = (bf16[16,512]{1,0:T(8,128)(2,1)}, bf16[16,512]{1,0:T(8,128)(2,1)S(1)}, u32[]{:S(2)}, u32[]{:S(2)}) collective-permute-start(bf16[16,512]{1,0:T(8,128)(2,1)} %get-tuple-element.71), channel_id=1, source_target_pairs={{0,28},{4,24},{8,20},{12,16},{16,12},{20,8},{24,4},{28,0},{1,29},{... | collective-permute-start | bytes 49160 | tf_op jit(solution)/shard_map/ppermute | solution.py:578
  100.1 2.1 %collective-permute-done.15.rest_5_ = bf16[16,512]{1,0:T(8,128)(2,1)S(1)} collective-permute-done((bf16[16,512]{1,0:T(8,128)(2,1)}, bf16[16,512]{1,0:T(8,128)(2,1)S(1)}, u32[]{:S(2)}, u32[]{:S(2)}) %collective-permute-start.15) | collective-permute-done | bytes 16416 | tf_op jit(solution)/shard_map/ppermute | solution.py:578
  103.0 3.4 %output.1 = (f32[16,512]{1,0:T(8,128)}, f32[16,512]{1,0:T(8,128)}, f32[16,512]{1,0:T(8,128)}, f32[16,512]{1,0:T(8,128)}) custom-call(s32[1]{0:T(128)} %bitcast.col_ref, s32[42]{0:T(128)} %get-tuple-element.44.plan, f32[16,512]{1,0:T(8,128)} %get-tuple-element.53.gated, f32[16,256]{1,0:T(8,128)} %get-tuple-element.64.attended, bf16[512,2048]{1,0:T(8,128)(2,1)} %w_ssm.1, ...), custom_call_target="tpu_custom_call" | custom-call | flops 50331648 | bytes 4000000 | tf_op jit(solution)/shard_map/output/pallas_call | solution.py:700
  106.4 0.9 collective-permute-start.17
  107.3 3.5 %collective-permute-start.18 = (f32[16,512]{1,0:T(8,128)}, f32[16,512]{1,0:T(8,128)S(1)}, u32[]{:S(2)}, u32[]{:S(2)}) collective-permute-start(f32[16,512]{1,0:T(8,128)} %get-tuple-element.74), channel_id=1, source_target_pairs={{0,2},{1,3},{2,0},{3,1},{4,6},{5,7},{6,4},{7,5},{8,10},{9,11},{10,... | collective-permute-start | bytes 98312 | tf_op jit(solution)/shard_map/ppermute | solution.py:578
  110.8 2.7 %collective-permute-done.18.refs_2_ = f32[16,512]{1,0:T(8,128)S(1)} collective-permute-done((f32[16,512]{1,0:T(8,128)}, f32[16,512]{1,0:T(8,128)S(1)}, u32[]{:S(2)}, u32[]{:S(2)}) %collective-permute-start.18) | collective-permute-done | bytes 32800 | tf_op jit(solution)/shard_map/ppermute | solution.py:578
  113.5 3.2 %collective-permute-done.19.refs_3_ = f32[16,512]{1,0:T(8,128)S(1)} collective-permute-done((f32[16,512]{1,0:T(8,128)}, f32[16,512]{1,0:T(8,128)S(1)}, u32[]{:S(2)}, u32[]{:S(2)}) %collective-permute-start.19) | collective-permute-done | bytes 32800 | tf_op jit(solution)/shard_map/ppermute | solution.py:578
  117.3 1.4 %total.1 = bf16[13,512]{1,0:T(8,128)(2,1)} custom-call(f32[16,512]{1,0:T(8,128)} %get-tuple-element.72.refs_0_, f32[16,512]{1,0:T(8,128)} %copy-done.14, f32[16,512]{1,0:T(8,128)} %copy-done.15, f32[16,512]{1,0:T(8,128)} %copy-done.16), custom_call_target="tpu_custom_call" | custom-call | tf_op jit(solution)/shard_map/total/pallas_call | solution.py:744
  118.7 4.8 %arrive.1 = (bf16[3,13,512]{2,1,0:T(8,128)(2,1)}, bf16[3,13,512]{2,1,0:T(8,128)(2,1)}, bf16[13,8,64,256]{3,2,1,0:T(8,128)(2,1)}, bf16[104,32,512]{2,1,0:T(8,128)(2,1)}) custom-call(s32[1]{0:T(128)} %bitcast.col_ref, s32[42]{0:T(128)} %get-tuple-element.44.plan, s32[8,13]{1,0:T(8,128)} %bitcast.23, ...), custom_call_target="tpu_custom_call", output_to_operand_aliasing={{2}: (5, {}), {3}: (6, {})} | custom-call | flops 1000000 | bytes 8388608 | tf_op jit(solution)/shard_map/arrive/pallas_call | solution.py:716
  (79 shorter events, 6.5 us)
Async XLA Ops:
  6.5 9.7 %copy-start.21 = (bf16[16,3328]{1,0:T(8,128)(2,1)S(1)}, bf16[16,3328]{1,0:T(8,128)(2,1)}, u32[]{:S(2)}) copy-start(bf16[16,3328]{1,0:T(8,128)(2,1)} %get-tuple-element.51) | copy-start | bytes 319492
  6.5 56.6 %copy-start.20 = (bf16[16,3328]{1,0:T(8,128)(2,1)S(1)}, bf16[16,3328]{1,0:T(8,128)(2,1)}, u32[]{:S(2)}) copy-start(bf16[16,3328]{1,0:T(8,128)(2,1)} %get-tuple-element.52) | copy-start | bytes 319492
  6.5 112.2 %all-to-all-start = ((bf16[8,16,32,512]{3,2,1,0:T(8,128)(2,1)}), bf16[8,16,32,512]{3,2,1,0:T(8,128)(2,1)}, u32[]{:S(2)}, u32[]{:S(2)}) async-start(bf16[8,16,32,512]{3,2,1,0:T(8,128)(2,1)} %get-tuple-element.78), calls=%async_computation | async-start | bytes 8388608 | tf_op jit(solution)/shard_map/all_to_all | solution.py:572
  11.9 4.3 %collective-permute-start = (bf16[16,3328]{1,0:T(8,128)(2,1)S(1)}, bf16[16,3328]{1,0:T(8,128)(2,1)S(1)}, u32[]{:S(2)}, u32[]{:S(2)}) collective-permute-start(bf16[16,3328]{1,0:T(8,128)(2,1)S(1)} %copy-done.26), channel_id=1, source_target_pairs={{0,4},{4,0},{8,12},{12,8},{16,20},{20,16},{24,28},{28,24},{1,5},{5... | collective-permute-start | bytes 319496 | tf_op jit(solution)/shard_map/ppermute | solution.py:578
  12.4 50.7 %collective-permute-start.1 = (bf16[16,3328]{1,0:T(8,128)(2,1)S(1)}, bf16[16,3328]{1,0:T(8,128)(2,1)S(1)}, u32[]{:S(2)}, u32[]{:S(2)}) collective-permute-start(bf16[16,3328]{1,0:T(8,128)(2,1)S(1)} %copy-done.25), channel_id=1, source_target_pairs={{0,8},{4,12},{8,0},{12,4},{16,24},{20,28},{24,16},{28,20},{1,9},{5... | collective-permute-start | bytes 319496 | tf_op jit(solution)/shard_map/ppermute | solution.py:578
  14.3 49.7 %collective-permute-start.2 = (bf16[16,3328]{1,0:T(8,128)(2,1)S(1)}, bf16[16,3328]{1,0:T(8,128)(2,1)S(1)}, u32[]{:S(2)}, u32[]{:S(2)}) collective-permute-start(bf16[16,3328]{1,0:T(8,128)(2,1)S(1)} %copy-done.24), channel_id=1, source_target_pairs={{0,12},{4,8},{8,4},{12,0},{16,28},{20,24},{24,20},{28,16},{1,13},{... | collective-permute-start | bytes 319496 | tf_op jit(solution)/shard_map/ppermute | solution.py:578
  14.4 49.6 %collective-permute-start.3 = (bf16[16,3328]{1,0:T(8,128)(2,1)S(1)}, bf16[16,3328]{1,0:T(8,128)(2,1)S(1)}, u32[]{:S(2)}, u32[]{:S(2)}) collective-permute-start(bf16[16,3328]{1,0:T(8,128)(2,1)S(1)} %copy-done.23), channel_id=1, source_target_pairs={{0,16},{4,20},{8,24},{12,28},{16,0},{20,4},{24,8},{28,12},{1,17},{... | collective-permute-start | bytes 319496 | tf_op jit(solution)/shard_map/ppermute | solution.py:578
  16.1 47.9 %collective-permute-start.4 = (bf16[16,3328]{1,0:T(8,128)(2,1)S(1)}, bf16[16,3328]{1,0:T(8,128)(2,1)S(1)}, u32[]{:S(2)}, u32[]{:S(2)}) collective-permute-start(bf16[16,3328]{1,0:T(8,128)(2,1)S(1)} %copy-done.22), channel_id=1, source_target_pairs={{0,20},{4,16},{8,28},{12,24},{16,4},{20,0},{24,12},{28,8},{1,21},{... | collective-permute-start | bytes 319496 | tf_op jit(solution)/shard_map/ppermute | solution.py:578
  16.2 53.3 %copy-start = (bf16[16,3328]{1,0:T(8,128)(2,1)}, bf16[16,3328]{1,0:T(8,128)(2,1)S(1)}, u32[]{:S(2)}) copy-start(bf16[16,3328]{1,0:T(8,128)(2,1)S(1)} %collective-permute-done.rest_1_) | copy-start | bytes 319492
  16.2 52.5 %collective-permute-start.5 = (bf16[16,3328]{1,0:T(8,128)(2,1)S(1)}, bf16[16,3328]{1,0:T(8,128)(2,1)S(1)}, u32[]{:S(2)}, u32[]{:S(2)}) collective-permute-start(bf16[16,3328]{1,0:T(8,128)(2,1)S(1)} %copy-done.21), channel_id=1, source_target_pairs={{0,24},{4,28},{8,16},{12,20},{16,8},{20,12},{24,0},{28,4},{1,25},{... | collective-permute-start | bytes 319496 | tf_op jit(solution)/shard_map/ppermute | solution.py:578
  63.1 6.3 %collective-permute-start.6 = (bf16[16,3328]{1,0:T(8,128)(2,1)S(1)}, bf16[16,3328]{1,0:T(8,128)(2,1)S(1)}, u32[]{:S(2)}, u32[]{:S(2)}) collective-permute-start(bf16[16,3328]{1,0:T(8,128)(2,1)S(1)} %copy-done.20), channel_id=1, source_target_pairs={{0,28},{4,24},{8,20},{12,16},{16,12},{20,8},{24,4},{28,0},{1,29},{... | collective-permute-start | bytes 319496 | tf_op jit(solution)/shard_map/ppermute | solution.py:578
  78.5 12.4 %collective-permute-start.7 = (f32[16,384]{1,0:T(8,128)}, f32[16,384]{1,0:T(8,128)S(1)}, u32[]{:S(2)}, u32[]{:S(2)}) collective-permute-start(f32[16,384]{1,0:T(8,128)} %get-tuple-element.61), channel_id=1, source_target_pairs={{0,1},{1,0},{2,3},{3,2},{4,5},{5,4},{6,7},{7,6},{8,9},{9,8},{10,11... | collective-permute-start | bytes 73736 | tf_op jit(solution)/shard_map/ppermute | solution.py:578
  81.0 9.9 %collective-permute-start.8 = (f32[16,384]{1,0:T(8,128)}, f32[16,384]{1,0:T(8,128)S(1)}, u32[]{:S(2)}, u32[]{:S(2)}) collective-permute-start(f32[16,384]{1,0:T(8,128)} %get-tuple-element.62), channel_id=1, source_target_pairs={{0,2},{1,3},{2,0},{3,1},{4,6},{5,7},{6,4},{7,5},{8,10},{9,11},{10,... | collective-permute-start | bytes 73736 | tf_op jit(solution)/shard_map/ppermute | solution.py:578
  83.6 7.3 %collective-permute-start.9 = (f32[16,384]{1,0:T(8,128)}, f32[16,384]{1,0:T(8,128)S(1)}, u32[]{:S(2)}, u32[]{:S(2)}) collective-permute-start(f32[16,384]{1,0:T(8,128)} %get-tuple-element.63), channel_id=1, source_target_pairs={{0,3},{1,2},{2,1},{3,0},{4,7},{5,6},{6,5},{7,4},{8,11},{9,10},{10,... | collective-permute-start | bytes 73736 | tf_op jit(solution)/shard_map/ppermute | solution.py:578
  93.7 3.6 %collective-permute-start.10 = (bf16[16,512]{1,0:T(8,128)(2,1)}, bf16[16,512]{1,0:T(8,128)(2,1)S(1)}, u32[]{:S(2)}, u32[]{:S(2)}) collective-permute-start(bf16[16,512]{1,0:T(8,128)(2,1)} %get-tuple-element.65), channel_id=1, source_target_pairs={{0,4},{4,0},{8,12},{12,8},{16,20},{20,16},{24,28},{28,24},{1,5},{5... | collective-permute-start | bytes 49160 | tf_op jit(solution)/shard_map/ppermute | solution.py:578
  93.8 4.4 %collective-permute-start.11 = (bf16[16,512]{1,0:T(8,128)(2,1)}, bf16[16,512]{1,0:T(8,128)(2,1)S(1)}, u32[]{:S(2)}, u32[]{:S(2)}) collective-permute-start(bf16[16,512]{1,0:T(8,128)(2,1)} %get-tuple-element.66), channel_id=1, source_target_pairs={{0,8},{4,12},{8,0},{12,4},{16,24},{20,28},{24,16},{28,20},{1,9},{5... | collective-permute-start | bytes 49160 | tf_op jit(solution)/shard_map/ppermute | solution.py:578
  94.4 5.6 %collective-permute-start.12 = (bf16[16,512]{1,0:T(8,128)(2,1)}, bf16[16,512]{1,0:T(8,128)(2,1)S(1)}, u32[]{:S(2)}, u32[]{:S(2)}) collective-permute-start(bf16[16,512]{1,0:T(8,128)(2,1)} %get-tuple-element.67), channel_id=1, source_target_pairs={{0,12},{4,8},{8,4},{12,0},{16,28},{20,24},{24,20},{28,16},{1,13},{... | collective-permute-start | bytes 49160 | tf_op jit(solution)/shard_map/ppermute | solution.py:578
  95.6 4.4 %collective-permute-start.13 = (bf16[16,512]{1,0:T(8,128)(2,1)}, bf16[16,512]{1,0:T(8,128)(2,1)S(1)}, u32[]{:S(2)}, u32[]{:S(2)}) collective-permute-start(bf16[16,512]{1,0:T(8,128)(2,1)} %get-tuple-element.68), channel_id=1, source_target_pairs={{0,16},{4,20},{8,24},{12,28},{16,0},{20,4},{24,8},{28,12},{1,17},{... | collective-permute-start | bytes 49160 | tf_op jit(solution)/shard_map/ppermute | solution.py:578
  96.5 3.5 %collective-permute-start.14 = (bf16[16,512]{1,0:T(8,128)(2,1)}, bf16[16,512]{1,0:T(8,128)(2,1)S(1)}, u32[]{:S(2)}, u32[]{:S(2)}) collective-permute-start(bf16[16,512]{1,0:T(8,128)(2,1)} %get-tuple-element.69), channel_id=1, source_target_pairs={{0,20},{4,16},{8,28},{12,24},{16,4},{20,0},{24,12},{28,8},{1,21},{... | collective-permute-start | bytes 49160 | tf_op jit(solution)/shard_map/ppermute | solution.py:578
  97.3 4.8 %collective-permute-start.15 = (bf16[16,512]{1,0:T(8,128)(2,1)}, bf16[16,512]{1,0:T(8,128)(2,1)S(1)}, u32[]{:S(2)}, u32[]{:S(2)}) collective-permute-start(bf16[16,512]{1,0:T(8,128)(2,1)} %get-tuple-element.70), channel_id=1, source_target_pairs={{0,24},{4,28},{8,16},{12,20},{16,8},{20,12},{24,0},{28,4},{1,25},{... | collective-permute-start | bytes 49160 | tf_op jit(solution)/shard_map/ppermute | solution.py:578
  98.1 4.3 %collective-permute-start.16 = (bf16[16,512]{1,0:T(8,128)(2,1)}, bf16[16,512]{1,0:T(8,128)(2,1)S(1)}, u32[]{:S(2)}, u32[]{:S(2)}) collective-permute-start(bf16[16,512]{1,0:T(8,128)(2,1)} %get-tuple-element.71), channel_id=1, source_target_pairs={{0,28},{4,24},{8,20},{12,16},{16,12},{20,8},{24,4},{28,0},{1,29},{... | collective-permute-start | bytes 49160 | tf_op jit(solution)/shard_map/ppermute | solution.py:578
  106.4 4.4 %collective-permute-start.17 = (f32[16,512]{1,0:T(8,128)}, f32[16,512]{1,0:T(8,128)S(1)}, u32[]{:S(2)}, u32[]{:S(2)}) collective-permute-start(f32[16,512]{1,0:T(8,128)} %get-tuple-element.73), channel_id=1, source_target_pairs={{0,1},{1,0},{2,3},{3,2},{4,5},{5,4},{6,7},{7,6},{8,9},{9,8},{10,11... | collective-permute-start | bytes 98312 | tf_op jit(solution)/shard_map/ppermute | solution.py:578
  107.3 6.2 %collective-permute-start.18 = (f32[16,512]{1,0:T(8,128)}, f32[16,512]{1,0:T(8,128)S(1)}, u32[]{:S(2)}, u32[]{:S(2)}) collective-permute-start(f32[16,512]{1,0:T(8,128)} %get-tuple-element.74), channel_id=1, source_target_pairs={{0,2},{1,3},{2,0},{3,1},{4,6},{5,7},{6,4},{7,5},{8,10},{9,11},{10,... | collective-permute-start | bytes 98312 | tf_op jit(solution)/shard_map/ppermute | solution.py:578
  110.8 5.9 %collective-permute-start.19 = (f32[16,512]{1,0:T(8,128)}, f32[16,512]{1,0:T(8,128)S(1)}, u32[]{:S(2)}, u32[]{:S(2)}) collective-permute-start(f32[16,512]{1,0:T(8,128)} %get-tuple-element.75), channel_id=1, source_target_pairs={{0,3},{1,2},{2,1},{3,0},{4,7},{5,6},{6,5},{7,4},{8,11},{9,10},{10,... | collective-permute-start | bytes 98312 | tf_op jit(solution)/shard_map/ppermute | solution.py:578
  (24 other events, 90.2 us)

commit v4 on v3

--- a/solution.py
+++ b/solution.py
@@ -19,7 +19,8 @@
 
 EPSILON = 1e-05
 FLOOR_SCORE = -1e30
-VMEM_LIMIT = 60 * 1024 * 1024
+FIRST_LIMIT = 60 * 1024 * 1024
+VMEM_LIMIT = 57 * 1024 * 1024
 
 F32 = jnp.float32
 BF16 = jnp.bfloat16
@@ -74,7 +75,7 @@
 
 
 class Note:
-    gated, key_value, drive, drive_low, mixing, conv_x, conv_bc, attended = 0, 1, 2, 3, 4, 5, 8, 11
+    mixed, key_value, drive, drive_low, mixing, conv_x, conv_bc = 0, 1, 2, 3, 4, 5, 8
     decay, decay_low = NS, NS + LANES
 
 
@@ -398,18 +399,13 @@
         result[h] = (rate * prior[h].astype(F32) + outer[h]).astype(BF16)
 
 
-def merge_kernel(
-    plan, gated, kv_new, driven, decay, b_in, conv_x, conv_bc, *rest, moves, row_count, col_count
-):
-    partials, attended = rest[:col_count], rest[col_count]
-    sends, block = rest[col_count + 1 : -1], rest[-1]
-    slots, inner = conv_x.shape[1], conv_x.shape[2]
-    heads, share = decay.shape[1], attended.shape[1]
-    at = Plan(slots, moves)
+def output_kernel(col_ref, gated, w_ssm, w_attn, *rest, slots, col_count):
+    partials, sends = rest[:col_count], rest[col_count:]
+    share = w_attn.shape[0]
     part = min(share, HD)
+    blocks = [partial[...] for partial in partials]
     pieces = []
     for j in range(share // part):
-        blocks = [partial[...] for partial in partials]
         peaks = [b[:, share + 2 * j : share + 2 * j + 1] for b in blocks]
         joint = functools.reduce(jnp.maximum, peaks)
         factors = [jnp.exp(p - joint) for p in peaks]
@@ -417,18 +413,31 @@
         value = sum(f * b[:, j * part : (j + 1) * part] for f, b in zip(factors, blocks))
         pieces.append(value / total)
     joined = pieces[0] if len(pieces) == 1 else jnp.concatenate(pieces, axis=1)
-    joined = jnp.where(row_iota(joined.shape) < slots, joined, 0.0).astype(BF16)
-    attended[...] = joined.astype(F32)
+    right = jnp.where(row_iota(joined.shape) < slots, joined, 0.0).astype(BF16)
+    left = gated[...].astype(BF16)
+    columns = w_ssm.shape[1] // col_count
+    for d, send in enumerate(sends):
+        first = pl.multiple_of(lax.bitwise_xor(col_ref[0], d) * columns, columns)
+        span = pl.ds(first, columns)
+        send[...] = dot(left, w_ssm[:, span]) + dot(right, w_attn[:, span])
+
+
+def total_kernel(
+    plan, kv_new, driven, decay, b_in, conv_x, conv_bc, *rest, moves, row_count, col_count
+):
+    terms, mixed = rest[:col_count], rest[col_count]
+    sends, block = rest[col_count + 1 : -1], rest[-1]
+    at = Plan(conv_x.shape[1], moves)
+    mixed[...] = sum(term[...] for term in terms).astype(BF16).astype(F32)
 
     block[...] = jnp.zeros_like(block)
     for m in range(moves):
-        slot = plan[at.slot + m]
-        row = pl.ds(slot, 1)
+        row = pl.ds(plan[at.slot + m], 1)
 
         def put(index, value, start=0):
             block[index : index + 1, start : start + value.shape[1]] = value
 
-        put(Note.gated, gated[row, :])
+        put(Note.mixed, mixed[row, :])
         put(Note.key_value, kv_new[row, :])
         for index, value, start, low_index, low_start in (
             (Note.drive, driven[row, :], 0, Note.drive_low, 0),
@@ -441,7 +450,6 @@
         for k in range(KW - 1):
             put(Note.conv_x + k, conv_x[k, row, :])
             put(Note.conv_bc + k, conv_bc[k, row, :])
-        put(Note.attended, attended[row, :])
         for d, send in enumerate(sends, 1):
 
             @pl.when(plan[at.away + m] == d)
@@ -457,33 +465,9 @@
             note[...] = sent[...].astype(F32)
 
 
-def output_kernel(col_ref, plan, gated, attended, w_ssm, w_attn, *rest, slots, moves, row_count, col_count):
-    notes, sends = rest[: row_count - 1], rest[row_count - 1 : row_count - 1 + col_count]
-    gated_here, attended_here, note = rest[row_count - 1 + col_count :]
-    at = Plan(slots, moves)
-    inner, share = gated.shape[1], attended.shape[1]
-    gated_here[...] = gated[...]
-    attended_here[...] = attended[...]
-    for m in range(moves):
-        pick_note(plan, at, m, notes, note)
-        row = pl.ds(plan[at.slot + m], 1)
-        gated_here[row, :] = note[Note.gated : Note.gated + 1, :inner]
-        attended_here[row, :] = note[Note.attended : Note.attended + 1, :share]
-    columns = w_ssm.shape[1] // col_count
-    left, right = gated_here[...].astype(BF16), attended_here[...].astype(BF16)
-    for d, send in enumerate(sends):
-        first = pl.multiple_of(lax.bitwise_xor(col_ref[0], d) * columns, columns)
-        span = pl.ds(first, columns)
-        send[...] = dot(left, w_ssm[:, span]) + dot(right, w_attn[:, span])
-
-
-def sum_kernel(*refs):
-    parts, out = refs[:-1], refs[-1]
-    out[...] = sum(part[...] for part in parts)[: out.shape[0]].astype(BF16)
-
-
 def arrive_kernel(
-    col_ref, plan, table, conv_x, conv_bc, state_in, pool_in, parcels, *rest, moves, row_count, col_count
+    col_ref, plan, table, mixed_home, conv_x, conv_bc, state_in, pool_in, parcels, *rest,
+    moves, row_count, col_count,
 ):
     del state_in, pool_in
     notes, rest = rest[: row_count - 1], rest[row_count - 1 :]
@@ -491,8 +475,8 @@
     inner = conv_x.shape[2]
     heads = inner // HP
     at = Plan(slots, moves)
-    conv_x_next, conv_bc_next, state_next, pool_next = rest[:4]
-    packed, made, drive, decay, b_twice, window_x, window_bc, picked, in_sems, out_sems = rest[4:]
+    mixed, conv_x_next, conv_bc_next, state_next, pool_next = rest[:5]
+    packed, made, drive, decay, b_twice, window_x, window_bc, window_mixed, picked, in_sems, out_sems = rest[5:]
     col = col_ref[0]
     loads = []
     for m in range(moves):
@@ -502,6 +486,7 @@
     for k in range(KW - 1):
         window_x[k] = conv_x[k]
         window_bc[k] = conv_bc[k]
+    window_mixed[...] = mixed_home[...]
     rows = []
     b_twice[...] = jnp.zeros_like(b_twice)
     half = b_twice.shape[0] // 2
@@ -510,6 +495,7 @@
         note = picked[...]
         rows.append(note)
         row = pl.ds(plan[at.slot + m], 1)
+        window_mixed[row, :] = note[Note.mixed : Note.mixed + 1, : window_mixed.shape[1]]
         for k in range(KW - 1):
             window_x[k, row, :] = note[Note.conv_x + k : Note.conv_x + k + 1, :inner]
             window_bc[k, row, :] = note[Note.conv_bc + k : Note.conv_bc + k + 1, : 2 * NS]
@@ -523,6 +509,7 @@
     stacked = [note[Note.drive : Note.drive + 1, :inner] for note in rows] + padding
     stacked += [note[Note.drive_low : Note.drive_low + 1, :inner] for note in rows] + padding
     drive[...] = jnp.transpose(jnp.concatenate(stacked, axis=0)).astype(BF16)
+    mixed[...] = window_mixed[0:slots, :].astype(BF16)
     for k in range(KW - 1):
         conv_x_next[k] = window_x[k].astype(BF16)
         conv_bc_next[k] = window_bc[k].astype(BF16)
@@ -622,7 +609,7 @@
             pltpu.SemaphoreType.DMA((moves, pages_here + 2)),
             pltpu.SemaphoreType.DMA((moves,)),
         ],
-        compiler_params=params(),
+        compiler_params=params(FIRST_LIMIT),
         cost_estimate=cost(2 * rows * depth * cols.width, 8e6),
         name="project",
     )(
@@ -630,6 +617,7 @@
         tokens, norm_gain, weight_z, weight_x, weight_dt.T, weight_bc, weight_qkv, pool, ssm_state,
     )
     received = trade(partial_sums, "rows")
+    parcels, received = lax.optimization_barrier((parcels, received))
     parcels = exchange(parcels, "rows")
 
     pool_next, kv_new, *partials = pl.pallas_call(
@@ -683,46 +671,42 @@
         name="mix",
     )(plan, past_x, past_bc, conv_weight_x, conv_weight_bc, dt_bias, a_log, d_skip, ssm_state, *received)
 
-    note = (BLOCK, max(inner, 2 * NS, 2 * KVH * HD, share))
-    attended, *notes = pl.pallas_call(
-        functools.partial(merge_kernel, moves=moves, row_count=row_count, col_count=col_count),
-        out_shape=[shape((BLOCK, share), F32)] + [shape(note, BF16)] * (row_count - 1),
-        in_specs=[SMEM_SPEC] + [VMEM_SPEC] * (7 + col_count),
+    columns = weight_ssm_out.shape[1] // col_count
+    terms = pl.pallas_call(
+        functools.partial(output_kernel, slots=slots, col_count=col_count),
+        out_shape=[shape((BLOCK, columns), F32)] * col_count,
+        in_specs=[SMEM_SPEC] + [VMEM_SPEC] * (3 + col_count),
+        out_specs=[VMEM_SPEC] * col_count,
+        compiler_params=params(),
+        cost_estimate=cost(2 * BLOCK * (inner + share) * weight_ssm_out.shape[1], 4e6),
+        name="output",
+    )(col_index, gated, weight_ssm_out, weight_attn_out, *partials)
+    terms = trade(terms, "cols")
+
+    note = (BLOCK, max(inner, 2 * NS, 2 * KVH * HD, columns))
+    mixed_home, *notes = pl.pallas_call(
+        functools.partial(total_kernel, moves=moves, row_count=row_count, col_count=col_count),
+        out_shape=[shape((BLOCK, columns), F32)] + [shape(note, BF16)] * (row_count - 1),
+        in_specs=[SMEM_SPEC] + [VMEM_SPEC] * (6 + col_count),
         out_specs=[VMEM_SPEC] * row_count,
         scratch_shapes=[pltpu.VMEM(note, F32)],
         compiler_params=params(),
         cost_estimate=cost(1e6, 1e6),
-        name="merge",
-    )(plan, gated, kv_new, driven, decay, b_in, next_x, next_bc, *partials)
+        name="total",
+    )(plan, kv_new, driven, decay, b_in, next_x, next_bc, *terms)
     notes = trade(notes, "rows", 1)
 
-    columns = weight_ssm_out.shape[1] // col_count
-    terms = pl.pallas_call(
-        functools.partial(
-            output_kernel, slots=slots, moves=moves, row_count=row_count, col_count=col_count
-        ),
-        out_shape=[shape((BLOCK, columns), F32)] * col_count,
-        in_specs=[SMEM_SPEC] * 2 + [VMEM_SPEC] * (4 + row_count - 1),
-        out_specs=[VMEM_SPEC] * col_count,
-        scratch_shapes=[
-            pltpu.VMEM((BLOCK, inner), F32), pltpu.VMEM((BLOCK, share), F32), pltpu.VMEM(note, F32)
-        ],
-        compiler_params=params(),
-        cost_estimate=cost(2 * BLOCK * (inner + share) * weight_ssm_out.shape[1], 4e6),
-        name="output",
-    )(col_index, plan, gated, attended, weight_ssm_out, weight_attn_out, *notes)
-    terms = trade(terms, "cols")
-
-    conv_x_next, conv_bc_next, state_next, pool_next = pl.pallas_call(
+    mixed, conv_x_next, conv_bc_next, state_next, pool_next = pl.pallas_call(
         functools.partial(arrive_kernel, moves=moves, row_count=row_count, col_count=col_count),
         out_shape=(
+            shape((slots, columns), BF16),
             shape(past_x.shape, BF16),
             shape(past_bc.shape, BF16),
             shape(ssm_state.shape, BF16),
             shape(pool.shape, BF16),
         ),
-        in_specs=[SMEM_SPEC] * 3 + [VMEM_SPEC] * 2 + [ANY_SPEC] * 3 + [VMEM_SPEC] * (row_count - 1),
-        out_specs=(VMEM_SPEC, VMEM_SPEC, ANY_SPEC, ANY_SPEC),
+        in_specs=[SMEM_SPEC] * 3 + [VMEM_SPEC] * 3 + [ANY_SPEC] * 3 + [VMEM_SPEC] * (row_count - 1),
+        out_specs=[VMEM_SPEC] * 3 + [ANY_SPEC] * 2,
         scratch_shapes=[
             parcels_here,
             pltpu.VMEM((moves, heads, HP, NS), BF16),
@@ -731,24 +715,16 @@
             pltpu.VMEM((2 * BLOCK, NS), F32),
             pltpu.VMEM((KW - 1, slots, inner), F32),
             pltpu.VMEM((KW - 1, slots, 2 * NS), F32),
+            pltpu.VMEM((BLOCK, columns), F32),
             pltpu.VMEM(note, F32),
             pltpu.SemaphoreType.DMA((moves,)),
             pltpu.SemaphoreType.DMA((moves, pages_here + 1)),
         ],
-        input_output_aliases={5: 2, 6: 3},
+        input_output_aliases={6: 3, 7: 4},
         compiler_params=params(),
         cost_estimate=cost(1e6, 4 * moves * (state_bytes + page_bytes)),
         name="arrive",
-    )(col_index, plan, table, next_x, next_bc, state_next, pool_next, parcels, *notes)
-
-    mixed = pl.pallas_call(
-        sum_kernel,
-        out_shape=shape((slots, columns), BF16),
-        in_specs=[VMEM_SPEC] * col_count,
-        out_specs=VMEM_SPEC,
-        compiler_params=params(),
-        name="total",
-    )(*terms)
+    )(col_index, plan, table, mixed_home, next_x, next_bc, state_next, pool_next, parcels, *notes)
     return (
         mixed, state_next, conv_x_next.transpose(1, 0, 2), conv_bc_next.transpose(1, 0, 2), pool_next[:, None]
     )

time: 124 us -> 85.6 us (0.69)
  waiting for transfers between devices: 58.8 us -> 21.3 us
  Pallas kernels: 33.2 us -> 31.4 us
    ppermute x20, waiting for transfers between devices: 58.8 us -> 21.3 us  [trade(): lax.ppermute(block, axis, [(i, i ^ d) for i in range(count)])]
    pallas_call x3 -> x2, Pallas kernels: 6.94 us -> 5.13 us  [the longest x1 3.16 us: local(): pl.pallas_call(functools.partial(output_kernel, slots=slots, col_count=co...]
    ppermute x20, starting transfers between devices: 22.8 us -> 24.6 us  [trade(): lax.ppermute(block, axis, [(i, i ^ d) for i in range(count)])]
  transfers between devices with their start and end apart: 21 -> 21, of which waited for: 8 -> 10; matrix products, arithmetic and copies ran while one was open for 0% -> 0% of each run, Pallas kernels for 18% -> 24%
where the time goes in v4:
time: 85.6 us; the launch traced here: 85.2 us
  Pallas kernels  31.4 us (37%)
  starting transfers between devices  29.2 us (34%)
  waiting for transfers between devices  21.3 us (25%)
  local copies, waits for them, and re-layouts  2.44 us (3%)
  between operations  0.86 us (1%)
    ppermute x20, starting transfers between devices, trade(): lax.ppermute(block, axis, [(i, i ^ d) for i in range(count)])  24.6 us
    ppermute x20, waiting for transfers between devices, trade(): lax.ppermute(block, axis, [(i, i ^ d) for i in range(count)])  21.3 us
    pallas_call x1, Pallas kernels, local(): pl.pallas_call(functools.partial(attend_kernel, moves=moves, heads=heads,...  8.35 us
    pallas_call x1, Pallas kernels, local(): pl.pallas_call(functools.partial(mix_kernel, moves=moves, row_count=row_c...  7.25 us
    pallas_call x1, Pallas kernels, local(): pl.pallas_call(functools.partial(project_kernel, slots=slots), out_shape=...  5.8 us
    pallas_call x1, Pallas kernels, local(): pl.pallas_call(functools.partial(arrive_kernel, moves=moves, row_count=ro...  4.84 us
    all_to_all x1, starting transfers between devices, exchange(): return lax.all_to_all(value, axis, split_axis=0, concat_axis=0, tiled=True)  4.56 us
    pallas_call x1, Pallas kernels, local(): pl.pallas_call(functools.partial(output_kernel, slots=slots, col_count=co...  3.16 us
  transfers between devices with their start and end apart: 21, of which 10 were waited for; matrix products, arithmetic and copies ran while one was open for 0% of the time, Pallas kernels for 24%

profile of v4, /device:TPU:0, one launch (start us, length us, event | category | flops | bytes accessed | tf_op | source)
XLA Modules:
  0.0 85.2 jit_solution(3304407388940626284)
XLA Ops:
  0.6 5.8 %project.1 = (bf16[8,16,32,512]{3,2,1,0:T(8,128)(2,1)}, s32[42]{0:T(128)}, bf16[16,3328]{1,0:T(8,128)(2,1)}, bf16[16,3328]{1,0:T(8,128)(2,1)}, bf16[16,3328]{1,0...) custom-call(s32[1]{0:T(128)} %bitcast.1.row_ref, ...), custom_call_target="tpu_custom_call" | custom-call | flops 218103808 | bytes 8000000 | tf_op jit(solution)/shard_map/project/pallas_call | solution.py:597
  6.9 2.6 %collective-permute-start.1 = (bf16[16,3328]{1,0:T(8,128)(2,1)}, bf16[16,3328]{1,0:T(8,128)(2,1)S(1)}, u32[]{:S(2)}, u32[]{:S(2)}) collective-permute-start(bf16[16,3328]{1,0:T(8,128)(2,1)} %get-tuple-element.58), channel_id=1, source_target_pairs={{0,8},{4,12},{8,0},{12,4},{16,24},{20,28},{24,16},{28,20},{1,9},{5... | collective-permute-start | bytes 319496 | tf_op jit(solution)/shard_map/ppermute | solution.py:565
  9.6 1.7 %collective-permute-start.3 = (bf16[16,3328]{1,0:T(8,128)(2,1)}, bf16[16,3328]{1,0:T(8,128)(2,1)S(1)}, u32[]{:S(2)}, u32[]{:S(2)}) collective-permute-start(bf16[16,3328]{1,0:T(8,128)(2,1)} %get-tuple-element.60), channel_id=1, source_target_pairs={{0,16},{4,20},{8,24},{12,28},{16,0},{20,4},{24,8},{28,12},{1,17},{... | collective-permute-start | bytes 319496 | tf_op jit(solution)/shard_map/ppermute | solution.py:565
  11.4 2.6 %collective-permute-start.5 = (bf16[16,3328]{1,0:T(8,128)(2,1)}, bf16[16,3328]{1,0:T(8,128)(2,1)S(1)}, u32[]{:S(2)}, u32[]{:S(2)}) collective-permute-start(bf16[16,3328]{1,0:T(8,128)(2,1)} %get-tuple-element.62), channel_id=1, source_target_pairs={{0,24},{4,28},{8,16},{12,20},{16,8},{20,12},{24,0},{28,4},{1,25},{... | collective-permute-start | bytes 319496 | tf_op jit(solution)/shard_map/ppermute | solution.py:565
  14.0 1.3 %collective-permute-start.6 = (bf16[16,3328]{1,0:T(8,128)(2,1)}, bf16[16,3328]{1,0:T(8,128)(2,1)S(1)}, u32[]{:S(2)}, u32[]{:S(2)}) collective-permute-start(bf16[16,3328]{1,0:T(8,128)(2,1)} %get-tuple-element.63), channel_id=1, source_target_pairs={{0,28},{4,24},{8,20},{12,16},{16,12},{20,8},{24,4},{28,0},{1,29},{... | collective-permute-start | bytes 319496 | tf_op jit(solution)/shard_map/ppermute | solution.py:565
  15.5 5.8 %collective-permute-done.4.rest_5_ = bf16[16,3328]{1,0:T(8,128)(2,1)S(1)} collective-permute-done((bf16[16,3328]{1,0:T(8,128)(2,1)}, bf16[16,3328]{1,0:T(8,128)(2,1)S(1)}, u32[]{:S(2)}, u32[]{:S(2)}) %collective-permute-start.4) | collective-permute-done | bytes 106528 | tf_op jit(solution)/shard_map/ppermute | solution.py:565
  22.0 4.6 %all-to-all-start = ((bf16[8,16,32,512]{3,2,1,0:T(8,128)(2,1)}), bf16[8,16,32,512]{3,2,1,0:T(8,128)(2,1)}, u32[]{:S(2)}, u32[]{:S(2)}) async-start(bf16[8,16,32,512]{3,2,1,0:T(8,128)(2,1)} %get-tuple-element.90), calls=%async_computation | async-start | bytes 8388608 | tf_op jit(solution)/shard_map/all_to_all | solution.py:559
  26.6 8.3 %attend.1 = (bf16[104,32,512]{2,1,0:T(8,128)(2,1)}, f32[16,512]{1,0:T(8,128)}, f32[16,384]{1,0:T(8,128)}, f32[16,384]{1,0:T(8,128)}, f32[16,384]{1,0:T(8,128)}, /*index=5*/f32[16,384]{1,0:T(8,128)}) custom-call(s32[1]{0:T(128)} %bitcast.col_ref, s32[42]{0:T(128)} %get-tuple-element.54.plan, s32[8,13]{1,0:T(8,128)} %bitcast.22, ...), custom_call_target="tpu_custom_call" | custom-call | flops 54525952 | bytes 13631488 | tf_op jit(solution)/shard_map/attend/pallas_call | solution.py:623
  34.9 1.9 %collective-permute-start.7 = (f32[16,384]{1,0:T(8,128)}, f32[16,384]{1,0:T(8,128)S(1)}, u32[]{:S(2)}, u32[]{:S(2)}) collective-permute-start(f32[16,384]{1,0:T(8,128)} %get-tuple-element.80), channel_id=1, source_target_pairs={{0,1},{1,0},{2,3},{3,2},{4,5},{5,4},{6,7},{7,6},{8,9},{9,8},{10,11... | collective-permute-start | bytes 73736 | tf_op jit(solution)/shard_map/ppermute | solution.py:565
  36.9 2.6 %collective-permute-start.8 = (f32[16,384]{1,0:T(8,128)}, f32[16,384]{1,0:T(8,128)S(1)}, u32[]{:S(2)}, u32[]{:S(2)}) collective-permute-start(f32[16,384]{1,0:T(8,128)} %get-tuple-element.81), channel_id=1, source_target_pairs={{0,2},{1,3},{2,0},{3,1},{4,6},{5,7},{6,4},{7,5},{8,10},{9,11},{10,... | collective-permute-start | bytes 73736 | tf_op jit(solution)/shard_map/ppermute | solution.py:565
  39.4 7.2 %mix.1 = (f32[3,13,512]{2,1,0:T(8,128)}, f32[3,13,512]{2,1,0:T(8,128)}, bf16[13,8,64,256]{3,2,1,0:T(8,128)(2,1)}, f32[16,512]{1,0:T(8,128)}, f32[16,512]{1,0:T(8...) custom-call(s32[42]{0:T(128)} %get-tuple-element.54.plan, bf16[3,13,512]{2,1,0:T(8,128)(2,1)} %bitcast.19, ...), custom_call_target="tpu_custom_call" | custom-call | flops 218103808 | bytes 13631488 | tf_op jit(solution)/shard_map/mix/pallas_call | solution.py:647
  47.3 3.2 %output.1 = (f32[16,512]{1,0:T(8,128)}, f32[16,512]{1,0:T(8,128)}, f32[16,512]{1,0:T(8,128)}, f32[16,512]{1,0:T(8,128)}) custom-call(s32[1]{0:T(128)} %bitcast.col_ref, f32[16,512]{1,0:T(8,128)} %get-tuple-element.78.gated, bf16[512,2048]{1,0:T(8,128)(2,1)} %w_ssm.1, bf16[256,2048]{1,0:T(8,128)(2,1)} %w_attn.1, f32[16,384]{1,0:T(8,128)} %get-tuple-element.79.rest_0_, ...), custom_call_target="tpu_custom_call" | custom-call | flops 50331648 | bytes 4000000 | tf_op jit(solution)/shard_map/output/pallas_call | solution.py:675
  50.5 0.9 %collective-permute-start.10 = (f32[16,512]{1,0:T(8,128)}, f32[16,512]{1,0:T(8,128)S(1)}, u32[]{:S(2)}, u32[]{:S(2)}) collective-permute-start(f32[16,512]{1,0:T(8,128)} %get-tuple-element.84), channel_id=1, source_target_pairs={{0,1},{1,0},{2,3},{3,2},{4,5},{5,4},{6,7},{7,6},{8,9},{9,8},{10,11... | collective-permute-start | bytes 98312 | tf_op jit(solution)/shard_map/ppermute | solution.py:565
  51.4 3.5 %collective-permute-start.11 = (f32[16,512]{1,0:T(8,128)}, f32[16,512]{1,0:T(8,128)S(1)}, u32[]{:S(2)}, u32[]{:S(2)}) collective-permute-start(f32[16,512]{1,0:T(8,128)} %get-tuple-element.85), channel_id=1, source_target_pairs={{0,2},{1,3},{2,0},{3,1},{4,6},{5,7},{6,4},{7,5},{8,10},{9,11},{10,... | collective-permute-start | bytes 98312 | tf_op jit(solution)/shard_map/ppermute | solution.py:565
  54.9 2.5 %collective-permute-done.11.rest_2_ = f32[16,512]{1,0:T(8,128)S(1)} collective-permute-done((f32[16,512]{1,0:T(8,128)}, f32[16,512]{1,0:T(8,128)S(1)}, u32[]{:S(2)}, u32[]{:S(2)}) %collective-permute-start.11) | collective-permute-done | bytes 32800 | tf_op jit(solution)/shard_map/ppermute | solution.py:565
  57.4 3.4 %collective-permute-done.12.rest_3_ = f32[16,512]{1,0:T(8,128)S(1)} collective-permute-done((f32[16,512]{1,0:T(8,128)}, f32[16,512]{1,0:T(8,128)S(1)}, u32[]{:S(2)}, u32[]{:S(2)}) %collective-permute-start.12) | collective-permute-done | bytes 32800 | tf_op jit(solution)/shard_map/ppermute | solution.py:565
  60.8 0.6 copy-done.9
  61.4 2.0 %total.1 = (f32[16,512]{1,0:T(8,128)}, bf16[16,512]{1,0:T(8,128)(2,1)}, bf16[16,512]{1,0:T(8,128)(2,1)}, bf16[16,512]{1,0:T(8,128)(2,1)}, bf16[16,512]{1,0:T(8,1...) custom-call(s32[42]{0:T(128)} %get-tuple-element.54.plan, ...), custom_call_target="tpu_custom_call" | custom-call | flops 1000000 | bytes 1000000 | tf_op jit(solution)/shard_map/total/pallas_call | solution.py:687
  63.5 1.9 %collective-permute-start.14 = (bf16[16,512]{1,0:T(8,128)(2,1)}, bf16[16,512]{1,0:T(8,128)(2,1)S(1)}, u32[]{:S(2)}, u32[]{:S(2)}) collective-permute-start(bf16[16,512]{1,0:T(8,128)(2,1)} %get-tuple-element.92), channel_id=1, source_target_pairs={{0,8},{4,12},{8,0},{12,4},{16,24},{20,28},{24,16},{28,20},{1,9},{5... | collective-permute-start | bytes 49160 | tf_op jit(solution)/shard_map/ppermute | solution.py:565
  65.4 1.7 %collective-permute-start.16 = (bf16[16,512]{1,0:T(8,128)(2,1)}, bf16[16,512]{1,0:T(8,128)(2,1)S(1)}, u32[]{:S(2)}, u32[]{:S(2)}) collective-permute-start(bf16[16,512]{1,0:T(8,128)(2,1)} %get-tuple-element.94), channel_id=1, source_target_pairs={{0,16},{4,20},{8,24},{12,28},{16,0},{20,4},{24,8},{28,12},{1,17},{... | collective-permute-start | bytes 49160 | tf_op jit(solution)/shard_map/ppermute | solution.py:565
  67.2 2.6 %collective-permute-start.18 = (bf16[16,512]{1,0:T(8,128)(2,1)}, bf16[16,512]{1,0:T(8,128)(2,1)S(1)}, u32[]{:S(2)}, u32[]{:S(2)}) collective-permute-start(bf16[16,512]{1,0:T(8,128)(2,1)} %get-tuple-element.96), channel_id=1, source_target_pairs={{0,24},{4,28},{8,16},{12,20},{16,8},{20,12},{24,0},{28,4},{1,25},{... | collective-permute-start | bytes 49160 | tf_op jit(solution)/shard_map/ppermute | solution.py:565
  69.8 5.6 %collective-permute-done.14.rest_1_ = bf16[16,512]{1,0:T(8,128)(2,1)S(1)} collective-permute-done((bf16[16,512]{1,0:T(8,128)(2,1)}, bf16[16,512]{1,0:T(8,128)(2,1)S(1)}, u32[]{:S(2)}, u32[]{:S(2)}) %collective-permute-start.14) | collective-permute-done | bytes 16416 | tf_op jit(solution)/shard_map/ppermute | solution.py:565
  76.7 3.0 %collective-permute-done.19.rest_6_ = bf16[16,512]{1,0:T(8,128)(2,1)S(1)} collective-permute-done((bf16[16,512]{1,0:T(8,128)(2,1)}, bf16[16,512]{1,0:T(8,128)(2,1)S(1)}, u32[]{:S(2)}, u32[]{:S(2)}) %collective-permute-start.19) | collective-permute-done | bytes 16416 | tf_op jit(solution)/shard_map/ppermute | solution.py:565
  80.3 4.8 %arrive.1 = (bf16[13,512]{1,0:T(8,128)(2,1)}, bf16[3,13,512]{2,1,0:T(8,128)(2,1)}, bf16[3,13,512]{2,1,0:T(8,128)(2,1)}, bf16[13,8,64,256]{3,2,1,0:T(8,128)(2,1)}, bf16[104,32,512]{2,1,0:T(8,128)(2,1)}) custom-call(s32[1]{0:T(128)} %bitcast.col_ref, s32[42]{0:T(128)} %get-tuple-element.54.plan, ...), custom_call_target="tpu_custom_call", output_to_operand_aliasing={{3}: (6, {}), {4}: (7, {})} | custom-call | flops 1000000 | bytes 8388608 | tf_op jit(solution)/shard_map/arrive/pallas_call | solution.py:699
  (64 shorter events, 4.1 us)
Async XLA Ops:
  6.4 4.9 %collective-permute-start = (bf16[16,3328]{1,0:T(8,128)(2,1)}, bf16[16,3328]{1,0:T(8,128)(2,1)S(1)}, u32[]{:S(2)}, u32[]{:S(2)}) collective-permute-start(bf16[16,3328]{1,0:T(8,128)(2,1)} %get-tuple-element.57), channel_id=1, source_target_pairs={{0,4},{4,0},{8,12},{12,8},{16,20},{20,16},{24,28},{28,24},{1,5},{5... | collective-permute-start | bytes 319496 | tf_op jit(solution)/shard_map/ppermute | solution.py:565
  6.9 7.0 %collective-permute-start.1 = (bf16[16,3328]{1,0:T(8,128)(2,1)}, bf16[16,3328]{1,0:T(8,128)(2,1)S(1)}, u32[]{:S(2)}, u32[]{:S(2)}) collective-permute-start(bf16[16,3328]{1,0:T(8,128)(2,1)} %get-tuple-element.58), channel_id=1, source_target_pairs={{0,8},{4,12},{8,0},{12,4},{16,24},{20,28},{24,16},{28,20},{1,9},{5... | collective-permute-start | bytes 319496 | tf_op jit(solution)/shard_map/ppermute | solution.py:565
  9.6 5.8 %collective-permute-start.2 = (bf16[16,3328]{1,0:T(8,128)(2,1)}, bf16[16,3328]{1,0:T(8,128)(2,1)S(1)}, u32[]{:S(2)}, u32[]{:S(2)}) collective-permute-start(bf16[16,3328]{1,0:T(8,128)(2,1)} %get-tuple-element.59), channel_id=1, source_target_pairs={{0,12},{4,8},{8,4},{12,0},{16,28},{20,24},{24,20},{28,16},{1,13},{... | collective-permute-start | bytes 319496 | tf_op jit(solution)/shard_map/ppermute | solution.py:565
  9.6 5.9 %collective-permute-start.3 = (bf16[16,3328]{1,0:T(8,128)(2,1)}, bf16[16,3328]{1,0:T(8,128)(2,1)S(1)}, u32[]{:S(2)}, u32[]{:S(2)}) collective-permute-start(bf16[16,3328]{1,0:T(8,128)(2,1)} %get-tuple-element.60), channel_id=1, source_target_pairs={{0,16},{4,20},{8,24},{12,28},{16,0},{20,4},{24,8},{28,12},{1,17},{... | collective-permute-start | bytes 319496 | tf_op jit(solution)/shard_map/ppermute | solution.py:565
  11.4 9.9 %collective-permute-start.4 = (bf16[16,3328]{1,0:T(8,128)(2,1)}, bf16[16,3328]{1,0:T(8,128)(2,1)S(1)}, u32[]{:S(2)}, u32[]{:S(2)}) collective-permute-start(bf16[16,3328]{1,0:T(8,128)(2,1)} %get-tuple-element.61), channel_id=1, source_target_pairs={{0,20},{4,16},{8,28},{12,24},{16,4},{20,0},{24,12},{28,8},{1,21},{... | collective-permute-start | bytes 319496 | tf_op jit(solution)/shard_map/ppermute | solution.py:565
  11.4 9.9 %copy-start = (bf16[16,3328]{1,0:T(8,128)(2,1)}, bf16[16,3328]{1,0:T(8,128)(2,1)S(1)}, u32[]{:S(2)}) copy-start(bf16[16,3328]{1,0:T(8,128)(2,1)S(1)} %collective-permute-done.rest_1_) | copy-start | bytes 319492
  11.4 9.9 %collective-permute-start.5 = (bf16[16,3328]{1,0:T(8,128)(2,1)}, bf16[16,3328]{1,0:T(8,128)(2,1)S(1)}, u32[]{:S(2)}, u32[]{:S(2)}) collective-permute-start(bf16[16,3328]{1,0:T(8,128)(2,1)} %get-tuple-element.62), channel_id=1, source_target_pairs={{0,24},{4,28},{8,16},{12,20},{16,8},{20,12},{24,0},{28,4},{1,25},{... | collective-permute-start | bytes 319496 | tf_op jit(solution)/shard_map/ppermute | solution.py:565
  14.0 7.3 %copy-start.1 = (bf16[16,3328]{1,0:T(8,128)(2,1)}, bf16[16,3328]{1,0:T(8,128)(2,1)S(1)}, u32[]{:S(2)}) copy-start(bf16[16,3328]{1,0:T(8,128)(2,1)S(1)} %collective-permute-done.1.rest_2_) | copy-start | bytes 319492
  14.0 7.3 %collective-permute-start.6 = (bf16[16,3328]{1,0:T(8,128)(2,1)}, bf16[16,3328]{1,0:T(8,128)(2,1)S(1)}, u32[]{:S(2)}, u32[]{:S(2)}) collective-permute-start(bf16[16,3328]{1,0:T(8,128)(2,1)} %get-tuple-element.63), channel_id=1, source_target_pairs={{0,28},{4,24},{8,20},{12,16},{16,12},{20,8},{24,4},{28,0},{1,29},{... | collective-permute-start | bytes 319496 | tf_op jit(solution)/shard_map/ppermute | solution.py:565
  22.0 57.7 %all-to-all-start = ((bf16[8,16,32,512]{3,2,1,0:T(8,128)(2,1)}), bf16[8,16,32,512]{3,2,1,0:T(8,128)(2,1)}, u32[]{:S(2)}, u32[]{:S(2)}) async-start(bf16[8,16,32,512]{3,2,1,0:T(8,128)(2,1)} %get-tuple-element.90), calls=%async_computation | async-start | bytes 8388608 | tf_op jit(solution)/shard_map/all_to_all | solution.py:559
  34.9 11.8 %collective-permute-start.7 = (f32[16,384]{1,0:T(8,128)}, f32[16,384]{1,0:T(8,128)S(1)}, u32[]{:S(2)}, u32[]{:S(2)}) collective-permute-start(f32[16,384]{1,0:T(8,128)} %get-tuple-element.80), channel_id=1, source_target_pairs={{0,1},{1,0},{2,3},{3,2},{4,5},{5,4},{6,7},{7,6},{8,9},{9,8},{10,11... | collective-permute-start | bytes 73736 | tf_op jit(solution)/shard_map/ppermute | solution.py:565
  36.9 9.9 %collective-permute-start.8 = (f32[16,384]{1,0:T(8,128)}, f32[16,384]{1,0:T(8,128)S(1)}, u32[]{:S(2)}, u32[]{:S(2)}) collective-permute-start(f32[16,384]{1,0:T(8,128)} %get-tuple-element.81), channel_id=1, source_target_pairs={{0,2},{1,3},{2,0},{3,1},{4,6},{5,7},{6,4},{7,5},{8,10},{9,11},{10,... | collective-permute-start | bytes 73736 | tf_op jit(solution)/shard_map/ppermute | solution.py:565
  39.4 7.3 %collective-permute-start.9 = (f32[16,384]{1,0:T(8,128)}, f32[16,384]{1,0:T(8,128)S(1)}, u32[]{:S(2)}, u32[]{:S(2)}) collective-permute-start(f32[16,384]{1,0:T(8,128)} %get-tuple-element.82), channel_id=1, source_target_pairs={{0,3},{1,2},{2,1},{3,0},{4,7},{5,6},{6,5},{7,4},{8,11},{9,10},{10,... | collective-permute-start | bytes 73736 | tf_op jit(solution)/shard_map/ppermute | solution.py:565
  50.5 4.4 %collective-permute-start.10 = (f32[16,512]{1,0:T(8,128)}, f32[16,512]{1,0:T(8,128)S(1)}, u32[]{:S(2)}, u32[]{:S(2)}) collective-permute-start(f32[16,512]{1,0:T(8,128)} %get-tuple-element.84), channel_id=1, source_target_pairs={{0,1},{1,0},{2,3},{3,2},{4,5},{5,4},{6,7},{7,6},{8,9},{9,8},{10,11... | collective-permute-start | bytes 98312 | tf_op jit(solution)/shard_map/ppermute | solution.py:565
  51.4 6.0 %collective-permute-start.11 = (f32[16,512]{1,0:T(8,128)}, f32[16,512]{1,0:T(8,128)S(1)}, u32[]{:S(2)}, u32[]{:S(2)}) collective-permute-start(f32[16,512]{1,0:T(8,128)} %get-tuple-element.85), channel_id=1, source_target_pairs={{0,2},{1,3},{2,0},{3,1},{4,6},{5,7},{6,4},{7,5},{8,10},{9,11},{10,... | collective-permute-start | bytes 98312 | tf_op jit(solution)/shard_map/ppermute | solution.py:565
  54.9 5.9 %collective-permute-start.12 = (f32[16,512]{1,0:T(8,128)}, f32[16,512]{1,0:T(8,128)S(1)}, u32[]{:S(2)}, u32[]{:S(2)}) collective-permute-start(f32[16,512]{1,0:T(8,128)} %get-tuple-element.86), channel_id=1, source_target_pairs={{0,3},{1,2},{2,1},{3,0},{4,7},{5,6},{6,5},{7,4},{8,11},{9,10},{10,... | collective-permute-start | bytes 98312 | tf_op jit(solution)/shard_map/ppermute | solution.py:565
  63.4 3.8 %collective-permute-start.13 = (bf16[16,512]{1,0:T(8,128)(2,1)}, bf16[16,512]{1,0:T(8,128)(2,1)S(1)}, u32[]{:S(2)}, u32[]{:S(2)}) collective-permute-start(bf16[16,512]{1,0:T(8,128)(2,1)} %get-tuple-element.91), channel_id=1, source_target_pairs={{0,4},{4,0},{8,12},{12,8},{16,20},{20,16},{24,28},{28,24},{1,5},{5... | collective-permute-start | bytes 49160 | tf_op jit(solution)/shard_map/ppermute | solution.py:565
  63.5 12.0 %collective-permute-start.14 = (bf16[16,512]{1,0:T(8,128)(2,1)}, bf16[16,512]{1,0:T(8,128)(2,1)S(1)}, u32[]{:S(2)}, u32[]{:S(2)}) collective-permute-start(bf16[16,512]{1,0:T(8,128)(2,1)} %get-tuple-element.92), channel_id=1, source_target_pairs={{0,8},{4,12},{8,0},{12,4},{16,24},{20,28},{24,16},{28,20},{1,9},{5... | collective-permute-start | bytes 49160 | tf_op jit(solution)/shard_map/ppermute | solution.py:565
  65.4 10.5 %collective-permute-start.15 = (bf16[16,512]{1,0:T(8,128)(2,1)}, bf16[16,512]{1,0:T(8,128)(2,1)S(1)}, u32[]{:S(2)}, u32[]{:S(2)}) collective-permute-start(bf16[16,512]{1,0:T(8,128)(2,1)} %get-tuple-element.93), channel_id=1, source_target_pairs={{0,12},{4,8},{8,4},{12,0},{16,28},{20,24},{24,20},{28,16},{1,13},{... | collective-permute-start | bytes 49160 | tf_op jit(solution)/shard_map/ppermute | solution.py:565
  65.4 10.7 %collective-permute-start.16 = (bf16[16,512]{1,0:T(8,128)(2,1)}, bf16[16,512]{1,0:T(8,128)(2,1)S(1)}, u32[]{:S(2)}, u32[]{:S(2)}) collective-permute-start(bf16[16,512]{1,0:T(8,128)(2,1)} %get-tuple-element.94), channel_id=1, source_target_pairs={{0,16},{4,20},{8,24},{12,28},{16,0},{20,4},{24,8},{28,12},{1,17},{... | collective-permute-start | bytes 49160 | tf_op jit(solution)/shard_map/ppermute | solution.py:565
  67.2 9.3 %collective-permute-start.17 = (bf16[16,512]{1,0:T(8,128)(2,1)}, bf16[16,512]{1,0:T(8,128)(2,1)S(1)}, u32[]{:S(2)}, u32[]{:S(2)}) collective-permute-start(bf16[16,512]{1,0:T(8,128)(2,1)} %get-tuple-element.95), channel_id=1, source_target_pairs={{0,20},{4,16},{8,28},{12,24},{16,4},{20,0},{24,12},{28,8},{1,21},{... | collective-permute-start | bytes 49160 | tf_op jit(solution)/shard_map/ppermute | solution.py:565
  67.2 12.5 %copy-start.13 = (bf16[16,512]{1,0:T(8,128)(2,1)}, bf16[16,512]{1,0:T(8,128)(2,1)S(1)}, u32[]{:S(2)}) copy-start(bf16[16,512]{1,0:T(8,128)(2,1)S(1)} %collective-permute-done.13.rest_0_) | copy-start | bytes 49156
  67.2 9.5 %collective-permute-start.18 = (bf16[16,512]{1,0:T(8,128)(2,1)}, bf16[16,512]{1,0:T(8,128)(2,1)S(1)}, u32[]{:S(2)}, u32[]{:S(2)}) collective-permute-start(bf16[16,512]{1,0:T(8,128)(2,1)} %get-tuple-element.96), channel_id=1, source_target_pairs={{0,24},{4,28},{8,16},{12,20},{16,8},{20,12},{24,0},{28,4},{1,25},{... | collective-permute-start | bytes 49160 | tf_op jit(solution)/shard_map/ppermute | solution.py:565
  75.4 4.3 %collective-permute-start.19 = (bf16[16,512]{1,0:T(8,128)(2,1)}, bf16[16,512]{1,0:T(8,128)(2,1)S(1)}, u32[]{:S(2)}, u32[]{:S(2)}) collective-permute-start(bf16[16,512]{1,0:T(8,128)(2,1)} %get-tuple-element.97), channel_id=1, source_target_pairs={{0,28},{4,24},{8,20},{12,16},{16,12},{20,8},{24,4},{28,0},{1,29},{... | collective-permute-start | bytes 49160 | tf_op jit(solution)/shard_map/ppermute | solution.py:565
  (17 other events, 44.2 us)
